TPU v7x, 32 devices: a whole 2x2x4 slice. The times are simulated.
32 devices in a mesh: dp: 8 (over y, x, core), head: 4 (over z).
Axes of the slice: x: 2, y: 2, z: 4, core: 2. Of those that a mesh axis runs over, the one named last changes fastest.
Arguments:
- tokens: bfloat16 [8, 4, 512, 768], P('dp'), may hold values from -6 to 6
- doc_ids: int32 [8, 4, 512], P('dp'), may hold values from 0 to 7, never falling along the last dimension, each value on 1 to 192 neighbouring positions
- reset: int32 [8, 4], P('dp'), may hold values 0 or 1
- mem_init: bfloat16 [10, 768], replicated, may hold values from -6 to 6
- w_query: bfloat16 [768, 768], P(None, 'head'), may hold values from -0.21875 to 0.21875
- w_key: bfloat16 [768, 768], P(None, 'head'), may hold values from -0.21875 to 0.21875
- w_value: bfloat16 [768, 768], P(None, 'head'), may hold values from -0.21875 to 0.21875
- b_query: bfloat16 [12, 64], P('head'), may hold values from -2 to 2
- b_value: bfloat16 [12, 64], P('head'), may hold values from -2 to 2
- w_out: bfloat16 [768, 768], P('head'), may hold values from -1.25 to 1.25
- b_out: bfloat16 [768], replicated, may hold values from -2 to 2
- gain_attn: bfloat16 [768], replicated, may hold values from 0.5 to 1.5
- shift_attn: bfloat16 [768], replicated, may hold values from -2 to 2
- w_in: bfloat16 [768, 3072], P(None, ('dp', 'head')), may hold values from -0.21875 to 0.21875
- b_in: bfloat16 [3072], P(('dp', 'head')), may hold values from -3 to 3
- w_down: bfloat16 [3072, 768], P(('dp', 'head')), may hold values from -0.109375 to 0.109375
- b_down: bfloat16 [768], replicated, may hold values from -2 to 2
- gain_ffn: bfloat16 [768], replicated, may hold values from 0.5 to 1.5
- shift_ffn: bfloat16 [768], replicated, may hold values from -2 to 2
- cotangent: bfloat16 [8, 4, 512, 768], P('dp', None, 'head'), may hold values from -6 to 6
Outputs:
- output: bfloat16 [8, 4, 512, 768], P('dp', None, 'head')
- memory_norm: float32 [8, 4], P('dp')
- grad_tokens: float32 [8, 4, 512, 768], P('dp', None, 'head')
- grad_w_query: float32 [768, 768], P('dp', 'head')
- grad_w_key: float32 [768, 768], P('dp', 'head')
- grad_w_value: float32 [768, 768], P('dp', 'head')
- grad_b_query: float32 [12, 64], P('head', 'dp')
- grad_b_value: float32 [12, 64], P('head', 'dp')
- grad_w_out: float32 [768, 768], P('head', 'dp')
- grad_b_out: float32 [768], P(('dp', 'head'))
- grad_gain_attn: float32 [768], P(('dp', 'head'))
- grad_shift_attn: float32 [768], P(('dp', 'head'))
- grad_w_in: float32 [768, 3072], P(None, ('dp', 'head'))
- grad_b_in: float32 [3072], P(('dp', 'head'))
- grad_w_down: float32 [3072, 768], P(('dp', 'head'))
- grad_b_down: float32 [768], P(('dp', 'head'))
- grad_gain_ffn: float32 [768], P(('dp', 'head'))
- grad_shift_ffn: float32 [768], P(('dp', 'head'))
- grad_mem_init: float32 [10, 768], P(None, ('dp', 'head'))
Inputs may be any that keep to these rules, and one draw needn't show every extreme that they name: `doc_ids`: within a segment the document numbers never fall, and each document has at most 192 tokens.
All inputs are finite; a program needn't handle non-finite values. No bound on the sum of `reset` on one device may be relied on, other than what follows from the above.
Results may differ from a plain program's by a relative error of at most 0.017.
Values may be sent and summed in bfloat16 or wider, within the bound.
No kernel may reach another device: no remote copies, remote signals or barrier semaphores. Data moves between devices by JAX's collectives and lax.ppermute only.
A program may use at most 192 MiB of HBM per device.

v0:
```python
import functools

import jax
import jax.numpy as jnp
from jax import lax
from jax.experimental import pallas as pl
from jax.experimental.pallas import tpu as pltpu
from jax.sharding import PartitionSpec as P

EPSILON = 1e-06
SCALE = 0.125
NEGATIVE = -1e30
ROOT_HALF = 0.7071067811865476
DENSITY = 0.3989422804014327
LOW = jnp.bfloat16
FULL = jnp.float32
PAD = 16
VECTORS = ("b_query", "b_value", "b_out", "gain_attn", "shift_attn", "b_down", "gain_ffn", "shift_ffn")
VMEM_LIMIT = 60 * 1024 * 1024


def nn(left, right):
    return lax.dot_general(left, right, (((1,), (0,)), ((), ())), preferred_element_type=FULL)


def nt(left, right):
    return lax.dot_general(left, right, (((1,), (1,)), ((), ())), preferred_element_type=FULL)


def tn(left, right):
    return lax.dot_general(left, right, (((0,), (0,)), ((), ())), preferred_element_type=FULL)


def norm_parts(rows):
    centred = rows - jnp.mean(rows, -1, keepdims=True)
    inverse = lax.rsqrt(jnp.mean(centred * centred, -1, keepdims=True) + EPSILON)
    return centred * inverse, inverse


def norm_pull(normed, inverse, grad):
    along = jnp.mean(grad * normed, -1, keepdims=True)
    return inverse * (grad - jnp.mean(grad, -1, keepdims=True) - normed * along)


def gelu(v):
    return 0.5 * v * (1.0 + lax.erf(v * ROOT_HALF))


def gelu_slope(v):
    return 0.5 * (1.0 + lax.erf(v * ROOT_HALF)) + v * (DENSITY * jnp.exp(-0.5 * v * v))


def swap(array, axis, bit):
    return lax.ppermute(array, axis, [(i, i ^ bit) for i in range(lax.axis_size(axis))])


def bits_of(count):
    return [1 << i for i in range(count.bit_length() - 1)]


def gather(array, stages):
    for axis, bit in stages:
        array = jnp.concatenate([array, swap(array, axis, bit)], 0)
    return array


def summed(terms, kind=LOW, first=0):
    size = terms[-1].shape[0] - first
    total = terms[0][first : first + size].astype(FULL)
    for term in terms[1:]:
        total = total + term[first : first + size].astype(FULL)
    return total.astype(kind)


def add_up(count, together, *refs):
    out_refs = list(refs[sum(count) :])
    pair_ref = None
    if together:
        pair_ref = out_refs[0]
        out_refs = [None, None] + out_refs[1:]
    at = 0
    for number_of, (number, out_ref) in enumerate(zip(count, out_refs)):
        total = refs[at][...].astype(FULL)
        for ref in refs[at + 1 : at + number]:
            total = total + ref[...].astype(FULL)
        total = total.astype(refs[at].dtype)
        at += number
        if pair_ref is not None and number_of < 2:
            pair_ref[:, number_of] = total
        else:
            out_ref[...] = total


def parcels(groups, together=False):
    halves = [terms[-1].shape[0] // 2 for terms in groups]
    steps = min(min(halves), 4)
    in_specs, operands, out_specs, shapes = [], [], [], []

    def spec(half, rest, first):
        index = lambda i: (first + i,) + (0,) * len(rest)
        return pl.BlockSpec((half // steps, *rest), index)

    for half, terms in zip(halves, groups):
        rest = terms[0].shape[1:]
        in_specs += [spec(half, rest, steps)] * len(terms)
        operands += terms
        if together and len(operands) < len(groups[0]) + len(groups[1]) + 1:
            if len(shapes):
                continue
            rest = (2, *rest)
        out_specs.append(spec(half, rest, 0))
        shapes.append(jax.ShapeDtypeStruct((half, *rest), terms[0].dtype))
    return pl.pallas_call(
        functools.partial(add_up, [len(terms) for terms in groups], together),
        grid=(steps,),
        out_shape=shapes,
        in_specs=in_specs,
        out_specs=out_specs,
        compiler_params=pltpu.CompilerParams(vmem_limit_bytes=VMEM_LIMIT),
        cost_estimate=pl.CostEstimate(flops=1000, bytes_accessed=1000, transcendentals=0),
    )(*operands)


def posted(groups, sends, stages):
    return [
        terms + [swap(send, *stage)] for terms, send, stage in zip(groups, sends, stages)
    ]


def reduce_step(terms, stage):
    half = terms[-1].shape[0] // 2
    return terms + [swap(summed(terms, terms[0].dtype, half), *stage)]


def partner(index, stages, axis):
    place = 0
    for k, (name, bit) in enumerate(stages):
        if name == axis:
            place = place + ((index >> k) & 1) * bit
    return place


def position(partner_bits, order):
    place = 0
    for k, bit in enumerate(order):
        place = place + ((partner_bits // bit) % 2) * (1 << k)
    return place


def order_in(order, index_order):
    return [1 << index_order.index(bit) for bit in order]


def head_mask(rows, width, heads):
    group = lax.broadcasted_iota(jnp.int32, (rows, width), 0) // PAD
    column = lax.broadcasted_iota(jnp.int32, (rows, width), 1) // (width // heads)
    return group == column


def by_head(rows, mask, heads):
    return jnp.where(mask, jnp.concatenate([rows] * heads, 0), jnp.zeros((), rows.dtype))


def own_head(rows, mask, heads):
    kept = jnp.where(mask, rows, 0.0)
    total = kept[:PAD]
    for i in range(1, heads):
        total = total + kept[i * PAD : (i + 1) * PAD]
    return total


def vector(vec_ref, name):
    i = VECTORS.index(name)
    return vec_ref[i : i + 1, :]


class Units:
    def __init__(self, dps, heads, rows, width):
        self.dps, self.heads, self.rows, self.width = dps, heads, rows, width
        self.blocks = dps * heads
        self.chunks = max(2 * self.blocks * rows // width, 4)
        self.size = 2 * self.blocks * rows // self.chunks
        self.whole = rows % 16 != 0

    def at(self, index):
        return (index % self.heads) * self.dps + index // self.heads

    def pieces(self):
        if self.whole:
            return [(0, self.chunks)]
        part = self.blocks // 4
        return [(half * self.blocks + p * part, part) for half in range(2) for p in range(4)]

    def copies(self):
        for number, (first, count) in enumerate(self.pieces()):
            for entry in range(count):
                if self.whole:
                    yield number, entry, entry, 0, self.size
                    continue
                half, index = divmod(first + entry, self.blocks)
                row = (half * self.blocks + self.at(index)) * self.rows
                yield number, entry, row // self.size, row % self.size, self.rows

    def scratch(self):
        buffer = pltpu.VMEM((self.chunks, self.size, self.width), LOW)
        count = sum(2 for _ in self.copies())
        return (buffer, buffer, pltpu.SemaphoreType.DMA((count,)))

    def loads(self, pieces, up_ref, down_ref, arrived):
        made = []
        for number, entry, chunk, row, rows in self.copies():
            for side, to_ref in enumerate((up_ref, down_ref)):
                made.append(
                    pltpu.make_async_copy(
                        pieces[number].at[entry, side],
                        to_ref.at[chunk, pl.ds(row, rows)],
                        arrived.at[len(made)],
                    )
                )
        return made

    def assembled(self, halves):
        rows = []
        for array in halves:
            array = array.reshape(self.dps, self.heads, 2, self.rows, self.width)
            rows.append(array.transpose(1, 0, 3, 2, 4).reshape(-1, 2, self.width))
        rows = jnp.concatenate(rows, 0).reshape(self.chunks, self.size, 2, self.width)
        return [rows.transpose(0, 2, 1, 3)]

    def taken_apart(self, piece):
        rows = piece.transpose(0, 2, 1, 3).reshape(2, self.heads, self.dps, self.rows, 2, -1)
        rows = rows.transpose(0, 2, 1, 4, 3, 5)
        return [half.reshape(self.blocks, 2, self.rows, self.width) for half in rows]


def head_groups(ref, flip):
    value = ref[...]
    half = value.shape[1] // 2
    low, high = value[:, :half], value[:, half:]
    if flip & 2:
        low, high = high, low
    if flip & 1:
        low, high = pltpu.roll(low, half // 2, 1), pltpu.roll(high, half // 2, 1)
    return jnp.concatenate([low, high], 1)


def memory_queries(read, attn_ref, vec_ref):
    low = read.astype(LOW)
    queries = (nt(low, attn_ref[0]) + vector(vec_ref, "b_query")).astype(LOW)
    keys = nt(low, attn_ref[1]).astype(LOW)
    values = (nt(low, attn_ref[2]) + vector(vec_ref, "b_value")).astype(LOW)
    return queries, keys, values


def memory_attention(heads, memory_rows, queries, keys, values, key_low, value_low):
    rows, width = heads * PAD, queries.shape[1]
    mask = head_mask(rows, width, heads)
    real_key = lax.broadcasted_iota(jnp.int32, (rows, PAD), 1) < memory_rows
    spread = by_head(queries, mask, heads)
    scores = nt(spread, key_low) * SCALE
    scores_mem = jnp.where(real_key, nt(spread, keys) * SCALE, NEGATIVE)
    top = jnp.maximum(jnp.max(scores, -1, keepdims=True), jnp.max(scores_mem, -1, keepdims=True))
    raised = jnp.exp(scores - top)
    raised_mem = jnp.exp(scores_mem - top)
    total = jnp.sum(raised, -1, keepdims=True) + 2.0 * jnp.sum(raised_mem, -1, keepdims=True)
    soft = raised / total
    soft_mem = raised_mem / total
    mixed = nn(soft.astype(LOW), value_low) + 2.0 * nn(soft_mem.astype(LOW), values)
    return own_head(mixed, mask, heads).astype(LOW), soft, soft_mem


def memory_norm(result, memory_rows):
    real_row = lax.broadcasted_iota(jnp.int32, result.shape, 0) < memory_rows
    square = jnp.sum(jnp.where(real_row, result * result, 0.0), axis=(0, 1), keepdims=True)
    return jnp.sqrt(square / (memory_rows * result.shape[1]))


def chain_forward(
    layout,
    heads,
    memory_rows,
    reset_ref,
    init_ref,
    bias_ref,
    vec_ref,
    attn_from,
    key_from,
    value_from,
    *refs,
):
    count = len(layout.pieces())
    pieces, refs = refs[:count], refs[count:]
    (
        read_ref,
        qkv_ref,
        soft_ref,
        soft_mem_ref,
        attended_ref,
        z_attn_ref,
        hidden_ref,
        pre_ref,
        z_ffn_ref,
        norm_ref,
        attn_ref,
        key_ref,
        value_ref,
        attn_arrived,
        key_arrived,
        value_arrived,
        up_ref,
        down_ref,
        arrived,
    ) = refs
    last = key_ref.shape[0]
    attn_loads = [
        pltpu.make_async_copy(attn_from.at[i], attn_ref.at[i], attn_arrived.at[i])
        for i in range(4)
    ]

    def token_loads(s):
        return [
            pltpu.make_async_copy(key_from.at[s], key_ref.at[s], key_arrived.at[s]),
            pltpu.make_async_copy(value_from.at[s], value_ref.at[s], value_arrived.at[s]),
        ]

    loads = layout.loads(pieces, up_ref, down_ref, arrived)
    for load in attn_loads[:3] + token_loads(0) + attn_loads[3:] + loads:
        load.start()
    for s in range(1, last):
        for load in token_loads(s):
            load.start()
    chunks, size, _ = up_ref.shape
    norm_ref[...] = jnp.zeros_like(norm_ref)
    for load in attn_loads[:3]:
        load.wait()

    def enter(s, carried):
        fresh = (reset_ref[0, s] > 0) | (s == 0)
        read = jnp.where(fresh, init_ref[...], carried)
        read_ref[s] = read
        queries, keys, values = memory_queries(read, attn_ref, vec_ref)
        qkv_ref[s, 0] = queries
        qkv_ref[s, 1] = keys
        qkv_ref[s, 2] = values
        return read, queries, keys, values

    def step(s, carried):
        read, queries, keys, values = enter(s, carried)
        for load in token_loads(s):
            load.wait()
        attended, soft, soft_mem = memory_attention(
            heads, memory_rows, queries, keys, values, key_ref[s], value_ref[s]
        )
        soft_ref[s] = soft
        soft_mem_ref[s] = soft_mem
        attended_ref[s] = attended

        @pl.when(s == 0)
        def _():
            attn_loads[3].wait()

        z_attn = read + nn(attended, attn_ref[3]) + vector(vec_ref, "b_out")
        z_attn_ref[s] = z_attn
        normed, _ = norm_parts(z_attn)
        hidden = normed * vector(vec_ref, "gain_attn") + vector(vec_ref, "shift_attn")
        hidden_low = hidden.astype(LOW)
        hidden_ref[s] = hidden_low
        z_ffn = hidden + vector(vec_ref, "b_down")

        @pl.when(s == 0)
        def _():
            for load in loads:
                load.wait()

        for i in range(chunks):
            pre = nt(hidden_low, up_ref[i]) + bias_ref[i]
            pre_ref[s, :, i * size : (i + 1) * size] = pre
            z_ffn = z_ffn + nn(gelu(pre).astype(LOW), down_ref[i])
        z_ffn_ref[s] = z_ffn
        normed, _ = norm_parts(z_ffn)
        result = normed * vector(vec_ref, "gain_ffn") + vector(vec_ref, "shift_ffn")
        lane = lax.broadcasted_iota(jnp.int32, norm_ref.shape, 1)
        norm_ref[...] = jnp.where(lane == s, memory_norm(result, memory_rows), norm_ref[...])
        return result

    carried = lax.fori_loop(0, last, step, init_ref[...])
    enter(last, carried)


def last_norm(heads, memory_rows, bias_ref, vec_ref, read, qkv, key, value, weights):
    out_w, up_ref, down_ref = weights
    attended, _, _ = memory_attention(heads, memory_rows, *qkv, key, value)
    z_attn = read + nn(attended, out_w) + vector(vec_ref, "b_out")
    normed, _ = norm_parts(z_attn)
    hidden = normed * vector(vec_ref, "gain_attn") + vector(vec_ref, "shift_attn")
    hidden_low = hidden.astype(LOW)
    z_ffn = hidden + vector(vec_ref, "b_down")
    for i in range(up_ref.shape[0]):
        pre = nt(hidden_low, up_ref[i]) + bias_ref[i]
        z_ffn = z_ffn + nn(gelu(pre).astype(LOW), down_ref[i])
    normed, _ = norm_parts(z_ffn)
    result = normed * vector(vec_ref, "gain_ffn") + vector(vec_ref, "shift_ffn")
    return memory_norm(result, memory_rows)


def chain_backward(
    layout,
    head_order,
    heads,
    memory_rows,
    reset_ref,
    place_ref,
    bias_ref,
    read_ref,
    norms_ref,
    vec_ref,
    qkv_ref,
    soft_ref,
    soft_mem_ref,
    z_attn_ref,
    pre_ref,
    z_ffn_ref,
    hidden_ref,
    *refs,
):
    segments, _, _, width = qkv_ref.shape
    part_ref, *refs = refs
    attn_from, key_from, value_from, *refs = refs
    count = len(layout.pieces())
    pieces, refs = refs[:count], refs[count:]
    (
        score_ref,
        attended_ref,
        mixed_ref,
        small_ref,
        factor_ref,
        bias_grad_ref,
        vec_grad_ref,
        init_grad_ref,
        norm_ref,
        ffn_ref,
        pre_grad_ref,
        token_part_ref,
        attn_ref,
        key_ref,
        value_ref,
        attn_arrived,
        key_arrived,
        value_arrived,
        up_ref,
        down_ref,
        arrived,
    ) = refs
    attn_loads = [
        pltpu.make_async_copy(attn_from.at[i], attn_ref.at[i], attn_arrived.at[i])
        for i in range(4)
    ]

    def token_loads(s):
        return [
            pltpu.make_async_copy(key_from.at[s], key_ref.at[s], key_arrived.at[s]),
            pltpu.make_async_copy(value_from.at[s], value_ref.at[s], value_arrived.at[s]),
        ]

    loads = layout.loads(pieces, up_ref, down_ref, arrived)
    for load in attn_loads[1:3] + loads + attn_loads[3:] + attn_loads[:1]:
        load.start()
    for s in range(segments - 1, -1, -1):
        for load in token_loads(s):
            load.start()
    for j in range(segments):
        token_part_ref[j] = head_groups(part_ref.at[position(j, head_order)], j)
    me = place_ref[1]
    rows = heads * PAD
    mask = head_mask(rows, width, heads)
    chunks, size, _ = up_ref.shape
    half = chunks * size // 2
    vec_grad_ref[...] = jnp.zeros_like(vec_grad_ref)
    bias_grad_ref[...] = jnp.zeros_like(bias_grad_ref)

    def add_vector(name, grad):
        i = VECTORS.index(name)
        vec_grad_ref[i : i + 1, :] += jnp.sum(grad, 0, keepdims=True)

    last = segments - 1
    for load in attn_loads[1:3]:
        load.wait()
    grad_key = token_part_ref[last ^ me, :PAD].astype(LOW)
    grad_value = token_part_ref[last ^ me, PAD:].astype(LOW)
    small_ref[last, 0] = jnp.zeros((PAD, width), LOW)
    small_ref[last, 1] = grad_key
    small_ref[last, 2] = grad_value
    add_vector("b_value", 2.0 * grad_value.astype(FULL))
    grad_read = 2.0 * (nn(grad_key, attn_ref[1]) + nn(grad_value, attn_ref[2]))
    stop = reset_ref[0, last] > 0
    init_grad_ref[...] = jnp.where(stop, grad_read, 0.0)
    grad_write = jnp.where(stop, 0.0, grad_read)

    for load in [attn_loads[0], attn_loads[3], *loads, *token_loads(last)]:
        load.wait()
    norm = last_norm(
        heads,
        memory_rows,
        bias_ref,
        vec_ref,
        read_ref[last],
        [qkv_ref[last, i] for i in range(3)],
        key_ref[last],
        value_ref[last],
        (attn_ref[3], up_ref, down_ref),
    )
    lane = lax.broadcasted_iota(jnp.int32, norm_ref.shape, 1)
    norm_ref[...] = jnp.where(lane == last, norm, norms_ref[...])

    def step(back, grad_write):
        s = segments - 2 - back
        normed, inverse = norm_parts(z_ffn_ref[s])
        add_vector("gain_ffn", grad_write * normed)
        add_vector("shift_ffn", grad_write)
        grad_sum = norm_pull(normed, inverse, grad_write * vector(vec_ref, "gain_ffn"))
        grad_low = grad_sum.astype(LOW)
        ffn_ref[s] = grad_low
        add_vector("b_down", grad_low.astype(FULL))
        grad_hidden = grad_sum

        for i in range(chunks):
            part = slice(i * size, (i + 1) * size)
            grad_act = nt(grad_low, down_ref[i])
            grad_pre = (grad_act * gelu_slope(pre_ref[s, :, part])).astype(LOW)
            pre_grad_ref[s, :, part] = grad_pre
            bias_grad_ref[i] += jnp.sum(grad_pre.astype(FULL), 0, keepdims=True)
            grad_hidden = grad_hidden + nn(grad_pre, up_ref[i])
        normed, inverse = norm_parts(z_attn_ref[s])
        add_vector("gain_attn", grad_hidden * normed)
        add_vector("shift_attn", grad_hidden)
        grad_attn = norm_pull(normed, inverse, grad_hidden * vector(vec_ref, "gain_attn"))
        add_vector("b_out", grad_attn)
        grad_mixed = grad_attn.astype(LOW)
        mixed_ref[s] = grad_mixed

        for load in token_loads(s):
            load.wait()
        grad_attended = nt(grad_mixed, attn_ref[3]).astype(LOW)
        attended_ref[s] = grad_attended
        queries, keys, values = qkv_ref[s, 0], qkv_ref[s, 1], qkv_ref[s, 2]
        spread = by_head(grad_attended, mask, heads)
        soft, soft_mem = soft_ref[s], soft_mem_ref[s]
        pull = nt(spread, value_ref[s])
        pull_mem = nt(spread, values)
        inner = jnp.sum(soft * pull, -1, keepdims=True) + 2.0 * jnp.sum(
            soft_mem * pull_mem, -1, keepdims=True
        )
        grad_score = (soft * (pull - inner)).astype(LOW)
        grad_score_mem = (soft_mem * (pull_mem - inner)).astype(LOW)
        score_ref[s] = grad_score
        grad_query = nn(grad_score, key_ref[s]) + 2.0 * nn(grad_score_mem, keys)
        grad_query = (SCALE * own_head(grad_query, mask, heads)).astype(LOW)
        grad_key = SCALE * tn(grad_score_mem, by_head(queries, mask, heads))
        grad_key = (token_part_ref[s ^ me, :PAD] + grad_key).astype(LOW)
        grad_value = tn(soft_mem.astype(LOW), spread)
        grad_value = (token_part_ref[s ^ me, PAD:] + grad_value).astype(LOW)
        small_ref[s, 0] = grad_query
        small_ref[s, 1] = grad_key
        small_ref[s, 2] = grad_value
        add_vector("b_query", grad_query.astype(FULL))
        add_vector("b_value", 2.0 * grad_value.astype(FULL))
        grad_read = 2.0 * (nn(grad_key, attn_ref[1]) + nn(grad_value, attn_ref[2]))
        grad_read = grad_read + nn(grad_query, attn_ref[0]) + grad_attn
        stop = (reset_ref[0, s] > 0) | (s == 0)
        init_grad_ref[...] += jnp.where(stop, grad_read, 0.0)
        return jnp.where(stop, 0.0, grad_read)

    lax.fori_loop(0, segments - 1, step, grad_write)

    packed, wide = factor_ref.shape[1], (segments - 1) * PAD
    row = lax.broadcasted_iota(jnp.int32, (packed, wide), 0)
    source = lax.broadcasted_iota(jnp.int32, (packed, wide), 1)
    take = (source // PAD == row // memory_rows) & (source % PAD == row % memory_rows)
    take = jnp.where(take, 1.0, 0.0).astype(LOW)
    mine = width // 2

    def own_units(ref):
        first = ref[: segments - 1, :, :mine].reshape(wide, mine)
        second = ref[: segments - 1, :, half : half + mine].reshape(wide, mine)
        return jnp.concatenate([first, second], 1)

    acts = gelu(own_units(pre_ref)).astype(LOW)
    factor_ref[0] = nn(take, hidden_ref[: segments - 1].reshape(wide, width)).astype(LOW)
    factor_ref[1] = nn(take, ffn_ref[...].reshape(wide, width)).astype(LOW)
    factor_ref[2] = nn(take, acts).astype(LOW)
    factor_ref[3] = nn(take, own_units(pre_grad_ref)).astype(LOW)


def whole_call(body, scalars, operands, outside, shapes, flops, scratch=(), outside_shapes=()):
    in_vmem = pl.BlockSpec(memory_space=pltpu.VMEM)
    in_smem = pl.BlockSpec(memory_space=pltpu.SMEM)
    anywhere = pl.BlockSpec(memory_space=pl.ANY)
    size = sum(a.size * a.dtype.itemsize for a in (*operands, *outside, *shapes))
    return pl.pallas_call(
        body,
        out_shape=(*shapes, *outside_shapes),
        in_specs=[in_smem] * len(scalars) + [in_vmem] * len(operands) + [anywhere] * len(outside),
        out_specs=[in_vmem] * len(shapes) + [anywhere] * len(outside_shapes),
        scratch_shapes=scratch,
        compiler_params=pltpu.CompilerParams(vmem_limit_bytes=VMEM_LIMIT),
        cost_estimate=pl.CostEstimate(flops=flops // 1000, bytes_accessed=size // 1000, transcendentals=0),
    )(*scalars, *operands, *outside)


def unit_owner(column, order, stages, head_order, layout, index):
    head = position(partner(index, stages, "head"), head_order)
    at = head * layout.dps + position(partner(index, stages, "dp"), order)
    return column // layout.rows == at


def project(
    layout,
    stages,
    order_a,
    order_b,
    head_order,
    place_ref,
    token_ref,
    attn_ref,
    bias_ref,
    other_ref,
    key_ref,
    value_ref,
    x_ref,
    q_ref,
    k_ref,
    v_ref,
    vec_ref,
    bias_in_ref,
):
    devices, entries = bias_ref.shape
    width, rows = layout.width, layout.rows
    here = width // layout.heads
    packets = bias_ref[...].astype(FULL)

    def laid_out(first, count, period, owner):
        entry = lax.broadcasted_iota(jnp.int32, (entries, count), 0)
        column = lax.broadcasted_iota(jnp.int32, (entries, count), 1)
        pick = jnp.where(entry == first + column % period, 1.0, 0.0).astype(LOW)
        index = lax.broadcasted_iota(jnp.int32, (devices, count), 0)
        column = lax.broadcasted_iota(jnp.int32, (devices, count), 1)
        chosen = jnp.where(owner(column, index), nn(packets.astype(LOW), pick), 0.0)
        return jnp.sum(chosen, 0, keepdims=True)

    def of_head(column, index):
        head = partner(index, stages, "head")
        return (partner(index, stages, "dp") == 0) & (head == column // here)

    vec_ref[0:1, :] = laid_out(0, width, here, of_head)
    vec_ref[1:2, :] = laid_out(here, width, here, of_head)
    vec_ref[2:, :] = other_ref[...].astype(FULL)
    for half, order in enumerate((order_a, order_b)):
        owner = functools.partial(
            unit_owner, order=order, stages=stages, head_order=head_order, layout=layout
        )
        row = laid_out(
            2 * here + half * rows,
            layout.blocks * rows,
            rows,
            lambda column, index: owner(column, index=index),
        )
        per = layout.chunks // 2
        for i in range(per):
            bias_in_ref[half * per + i] = row[:, i * layout.size : (i + 1) * layout.size]

    for s in range(token_ref.shape[0]):
        x = token_ref[s]
        key_ref[s] = nt(x, attn_ref[1]).astype(LOW)
        value_ref[s] = (nt(x, attn_ref[2]) + vector(vec_ref, "b_value")).astype(LOW)
    own = place_ref[1]
    x = token_ref[own]
    x_ref[...] = x
    q_ref[...] = (nt(x, attn_ref[0]) + vector(vec_ref, "b_query")).astype(LOW)
    k_ref[...] = key_ref[own]
    v_ref[...] = value_ref[own]


SUMS = ("b_out", "gain_attn", "shift_attn", "b_down", "gain_ffn", "shift_ffn")


def token_layer(layout, x_ref, attended_ref, cot_ref, bias_ref, vec_ref, attn_ref, *refs):
    count = len(layout.pieces())
    pieces, refs = refs[:count], refs[count:]
    (
        result_ref,
        skip_ref,
        mixed_ref,
        grad_attended_ref,
        bias_sum_ref,
        sum_ref,
        *grad_refs,
        out_w_ref,
        out_arrived,
        up_ref,
        down_ref,
        arrived,
        z_attn_ref,
        hidden_ref,
        low_ref,
        total_ref,
        pre_ref,
        act_ref,
        stage_ref,
        sent,
    ) = refs
    out_load = pltpu.make_async_copy(attn_ref.at[3], out_w_ref, out_arrived)
    out_load.start()
    loads = layout.loads(pieces, up_ref, down_ref, arrived)
    for load in loads:
        load.start()
    chunks = layout.chunks
    out_load.wait()
    sum_ref[...] = jnp.zeros_like(sum_ref)

    def add_vector(name, grad):
        i = SUMS.index(name)
        sum_ref[i : i + 1, :] += jnp.sum(grad, 0, keepdims=True)

    z_attn = x_ref[...].astype(FULL) + nn(attended_ref[...], out_w_ref[...])
    z_attn = z_attn + vector(vec_ref, "b_out")
    z_attn_ref[...] = z_attn
    normed, _ = norm_parts(z_attn)
    hidden = normed * vector(vec_ref, "gain_attn") + vector(vec_ref, "shift_attn")
    hidden_ref[...] = hidden.astype(LOW)
    total_ref[...] = hidden + vector(vec_ref, "b_down")
    for load in loads:
        load.wait()

    def forward(i, nothing):
        pre = nt(hidden_ref[...], up_ref[i]) + bias_ref[i]
        pre_ref[i] = pre
        act = gelu(pre).astype(LOW)
        act_ref[i] = act
        total_ref[...] += nn(act, down_ref[i])
        return nothing

    lax.fori_loop(0, chunks, forward, 0)
    normed, inverse = norm_parts(total_ref[...])
    result = normed * vector(vec_ref, "gain_ffn") + vector(vec_ref, "shift_ffn")
    result_ref[...] = result.astype(LOW)
    grad = cot_ref[...].astype(FULL)
    add_vector("gain_ffn", grad * normed)
    add_vector("shift_ffn", grad)
    grad = norm_pull(normed, inverse, grad * vector(vec_ref, "gain_ffn"))
    total_ref[...] = grad
    low_ref[...] = grad.astype(LOW)
    add_vector("b_down", low_ref[...].astype(FULL))

    copies = list(layout.copies())
    spans = [first for first, _ in layout.pieces()]
    stores = []
    for i in range(chunks):
        grad_pre = (nt(low_ref[...], down_ref[i]) * gelu_slope(pre_ref[i])).astype(LOW)
        bias_sum_ref[i] = jnp.sum(grad_pre.astype(FULL), 0, keepdims=True)
        total_ref[...] += nn(grad_pre, up_ref[i])
        slot = i % 2
        if i > 1:
            for store in stores[i - 2]:
                store.wait()
        stage_ref[slot, 0] = tn(grad_pre, hidden_ref[...]).astype(LOW)
        stage_ref[slot, 1] = tn(act_ref[i], low_ref[...]).astype(LOW)
        stores.append([])
        for number, entry, chunk, row, rows in copies:
            if chunk != i:
                continue
            for side in range(2):
                to_ref = grad_refs[number // (len(spans) // len(grad_refs))]
                entry_at = spans[number] - spans[number - number % (len(spans) // len(grad_refs))]
                store = pltpu.make_async_copy(
                    stage_ref.at[slot, side, pl.ds(row, rows)],
                    to_ref.at[entry_at + entry, side],
                    sent.at[i, len(stores[i])],
                )
                store.start()
                stores[i].append(store)

    grad_hidden = total_ref[...]
    normed, inverse = norm_parts(z_attn_ref[...])
    add_vector("gain_attn", grad_hidden * normed)
    add_vector("shift_attn", grad_hidden)
    grad = norm_pull(normed, inverse, grad_hidden * vector(vec_ref, "gain_attn"))
    add_vector("b_out", grad)
    skip_ref[...] = grad
    mixed_ref[...] = grad.astype(LOW)
    grad_attended_ref[...] = nt(mixed_ref[...], out_w_ref[...]).astype(LOW)
    for i in range(max(chunks - 2, 0), chunks):
        for store in stores[i]:
            store.wait()


def part_rows(keep_ref, send_ref, first, columns, grad, place_ref, order, count):
    rows = grad.shape[0] // count
    for c in range(count):
        block = grad[c * rows : (c + 1) * rows].astype(keep_ref.dtype)
        at = position(place_ref[0] ^ c, order)

        @pl.when(at < count // 2)
        def _():
            keep_ref[at, first : first + rows, columns] = block

        @pl.when(at >= count // 2)
        def _():
            send_ref[at - count // 2, first : first + rows, columns] = block


SUM_ROWS = 32


def pack_sums(
    layout, order_a, order_b, head_order, heads_here, memory_rows, place_ref, groups, rows, halves
):
    count, width = rows.shape
    dps = layout.dps
    devices = dps * groups
    here, part = width // layout.heads, width // (dps * layout.heads)
    head_dim = here // heads_here
    head_part = head_dim // dps

    def partners(index):
        head = index % groups
        dp = 0
        for k, bit in enumerate(order_a):
            dp = dp + ((index // groups >> k) & 1) * bit
        return dp, head

    shape = (devices, count, width)
    index, row, column = (lax.broadcasted_iota(jnp.int32, shape, i) for i in range(3))
    dp_flip, head_flip = partners(index)
    dp, head = place_ref[0] ^ dp_flip, place_ref[1] ^ head_flip
    plain = len(SUMS) + memory_rows
    of_device = column // part == dp * layout.heads + head
    of_head = (column // here == head_flip) & (column % head_dim // head_part == dp)
    chosen = ((row < plain) & of_device) | ((row >= plain) & of_head)
    chosen = jnp.where(chosen, jnp.broadcast_to(rows[None], shape), 0.0)
    chosen = chosen.reshape(devices * count, width).astype(LOW)
    source = lax.broadcasted_iota(jnp.int32, (width, part), 0)
    target = lax.broadcasted_iota(jnp.int32, (width, part), 1)
    plain_fold = jnp.where(source % part == target, 1.0, 0.0).astype(LOW)
    head_column = source // head_dim % heads_here * head_part + source % head_part
    head_fold = jnp.where(head_column == target, 1.0, 0.0).astype(LOW)
    row = lax.broadcasted_iota(jnp.int32, (devices, count, part), 1)
    folded = jnp.where(
        row < plain,
        nn(chosen, plain_fold).reshape(devices, count, part),
        nn(chosen, head_fold).reshape(devices, count, part),
    )
    unit_rows = []
    span = halves[0].shape[1]
    index, column = (lax.broadcasted_iota(jnp.int32, (devices, span), i) for i in range(2))
    source = lax.broadcasted_iota(jnp.int32, (span, layout.rows), 0)
    target = lax.broadcasted_iota(jnp.int32, (span, layout.rows), 1)
    fold = jnp.where(source % layout.rows == target, 1.0, 0.0).astype(LOW)
    for order, half in zip((order_a, order_b), halves):
        dp_flip, head_flip = partners(index)
        at = position(head_flip, head_order) * dps + position(dp_flip, order)
        chosen = jnp.where(column // layout.rows == at, half, 0.0)
        unit_rows.append(nn(chosen.astype(LOW), fold))
    return folded, unit_rows


def put_sums(ref, entry, first_row, first_column, packed, index, memory_rows):
    folded, unit_rows = packed
    plain = len(SUMS) + memory_rows
    part, block = folded.shape[2], unit_rows[0].shape[1]
    columns = slice(first_column, first_column + part)
    ref[entry, first_row : first_row + plain + 2, columns] = folded[index, : plain + 2].astype(LOW)
    columns = slice(first_column, first_column + block)
    for half, rows in enumerate(unit_rows):
        row = first_row + plain + 2 + half
        ref[entry, row : row + 1, columns] = rows[index : index + 1].astype(LOW)


def half_rows(ref, layout):
    per = layout.chunks // 2
    return [
        jnp.concatenate([ref[half * per + i] for i in range(per)], 1) for half in range(2)
    ]


def value_grads(
    order,
    count,
    place_ref,
    x_ref,
    mixed_ref,
    attended_ref,
    dv0_ref,
    dv1_ref,
    skip_ref,
    attn_from,
    keep_ref,
    send_ref,
    grad_x_ref,
    sum_ref,
    attn_ref,
    arrived,
):
    load = pltpu.make_async_copy(attn_from.at[2], attn_ref, arrived)
    load.start()
    x, low, high = x_ref[...], dv0_ref[...], dv1_ref[...]
    half = low.shape[1]
    share = x.shape[1] // count
    every = slice(None)
    both = jnp.concatenate([tn(x, low), tn(x, high)], 1)
    part_rows(keep_ref, send_ref, 0, every, both, place_ref, order, count)
    both = tn(mixed_ref[...], attended_ref[...])
    part_rows(keep_ref, send_ref, share, every, both, place_ref, order, count)
    sum_ref[:, :half] = jnp.sum(low.astype(FULL), 0, keepdims=True)
    sum_ref[:, half:] = jnp.sum(high.astype(FULL), 0, keepdims=True)
    load.wait()
    grad_x_ref[...] = skip_ref[...] + nn(low, attn_ref[:half]) + nn(high, attn_ref[half:])


def query_key_grads(
    layout,
    order_a,
    order_b,
    head_order,
    heads_here,
    memory_rows,
    place_ref,
    x_ref,
    dq0_ref,
    dq1_ref,
    dk0_ref,
    dk1_ref,
    part_ref,
    value_sum_ref,
    layer_sum_ref,
    bias_sum_ref,
    attn_from,
    keep_ref,
    send_ref,
    grad_x_ref,
    rows_ref,
    attn_ref,
    arrived,
):
    loads = [
        pltpu.make_async_copy(attn_from.at[i], attn_ref.at[i], arrived.at[i]) for i in range(2)
    ]
    for load in loads:
        load.start()
    count = layout.dps
    x = x_ref[...]
    half = dq0_ref.shape[1]
    share = x.shape[1] // count
    pairs = [(dq0_ref[...], dq1_ref[...]), (dk0_ref[...], dk1_ref[...])]
    for m, (low, high) in enumerate(pairs):
        both = jnp.concatenate([tn(x, low), tn(x, high)], 1)
        part_rows(keep_ref, send_ref, m * share, slice(None), both, place_ref, order_a, count)
    plain = len(SUMS) + memory_rows
    rows_ref[...] = jnp.zeros_like(rows_ref)
    rows_ref[: len(SUMS), :] = layer_sum_ref[: len(SUMS), :]
    for at, array in zip((0, half), pairs[0]):
        rows_ref[plain : plain + 1, at : at + half] = jnp.sum(array.astype(FULL), 0, keepdims=True)
    rows_ref[plain + 1 : plain + 2, :] = value_sum_ref[...]
    packed = pack_sums(
        layout,
        order_a,
        order_b,
        head_order,
        heads_here,
        memory_rows,
        place_ref,
        layout.heads,
        rows_ref[...],
        half_rows(bias_sum_ref, layout),
    )
    here = x.shape[1] // layout.heads
    for at in range(count):
        ref = keep_ref if at < count // 2 else send_ref
        entry = at % (count // 2)
        ref[entry, 2 * share :, :] = jnp.zeros((SUM_ROWS, x.shape[1]), LOW)
        for g in range(layout.heads):
            index = at * layout.heads + g
            put_sums(ref, entry, 2 * share, g * here, packed, index, memory_rows)
    total = part_ref[...]
    for m, (low, high) in enumerate(pairs):
        loads[m].wait()
        total = total + nn(low, attn_ref[m, :half]) + nn(high, attn_ref[m, half:])
    grad_x_ref[...] = total.astype(LOW)


def own_grads(
    layout,
    order_a,
    order_b,
    head_order,
    heads,
    heads_here,
    memory_rows,
    place_ref,
    score_ref,
    soft_ref,
    qkv_ref,
    attended_grad_ref,
    mixed_ref,
    attended_ref,
    small_ref,
    read_ref,
    token_ref,
    bias_grad_ref,
    vec_grad_ref,
    init_grad_ref,
    keep_ref,
    send_ref,
    rows_ref,
):
    count = layout.dps
    writes, rows, _ = score_ref.shape
    width = qkv_ref.shape[-1]
    here = width // heads * heads_here
    mine = heads_here * PAD
    mask = head_mask(rows, width, heads)[:mine]
    total = jnp.zeros((1, here), FULL)
    grads = [jnp.zeros((width, here), FULL) for _ in range(4)]
    for s in range(writes + 1):
        low = read_ref[s].astype(LOW)
        grads[1] = grads[1] + 2.0 * tn(low, small_ref[s, 1, :, :here])
        grads[2] = grads[2] + 2.0 * tn(low, small_ref[s, 2, :, :here])
        if s == writes:
            break
        grads[0] = grads[0] + tn(low, small_ref[s, 0, :, :here])
        grads[3] = grads[3] + tn(mixed_ref[s], attended_ref[s, :, :here])
        spread = by_head(qkv_ref[s, 0], mask, heads_here)[:, :here]
        pulled = by_head(attended_grad_ref[s], mask, heads_here)[:, :here]
        dk = (SCALE * tn(score_ref[s, :mine], spread)).astype(LOW)
        dv = tn(soft_ref[s, :mine].astype(LOW), pulled).astype(LOW)
        grads[1] = grads[1] + tn(token_ref[s], dk)
        grads[2] = grads[2] + tn(token_ref[s], dv)
        total = total + jnp.sum(dv.astype(FULL), 0, keepdims=True)
    both = jnp.concatenate(grads, 1)
    part_rows(keep_ref, send_ref, 0, slice(None), both, place_ref, order_a, count)
    rows_ref[...] = jnp.zeros_like(rows_ref)
    for i, name in enumerate(SUMS):
        at = VECTORS.index(name)
        rows_ref[i : i + 1, :] = vec_grad_ref[at : at + 1, :]
    for i in range(memory_rows):
        at = len(SUMS) + i
        rows_ref[at : at + 1, :] = init_grad_ref[i : i + 1, :]
    at = len(SUMS) + memory_rows
    rows_ref[at : at + 2, :] = vec_grad_ref[0:2, :]
    rows_ref[at + 1 : at + 2, :here] += total
    packed = pack_sums(
        layout,
        order_a,
        order_b,
        head_order,
        heads_here,
        memory_rows,
        place_ref,
        1,
        rows_ref[...],
        half_rows(bias_grad_ref, layout),
    )
    share = width // count
    for at in range(count):
        ref = keep_ref if at < count // 2 else send_ref
        entry = at % (count // 2)
        ref[entry, share:, :] = jnp.zeros((SUM_ROWS, width), LOW)
        put_sums(ref, entry, share, 0, packed, at, memory_rows)


def write_rows(
    heads,
    quarter,
    place_ref,
    score_ref,
    soft_ref,
    qkv_ref,
    attended_grad_ref,
    moved_ref,
    attn_from,
    grad_token_ref,
    attn_ref,
    arrived,
):
    writes, rows, _ = score_ref.shape
    loads = [
        pltpu.make_async_copy(attn_from.at[i + 1], attn_ref.at[i], arrived.at[i])
        for i in range(2)
    ]
    for load in loads:
        load.start()
    mask = head_mask(rows, qkv_ref.shape[-1], heads)
    at = pl.multiple_of(place_ref[1] * quarter, quarter)
    for load in loads:
        load.wait()
    for s in range(writes):
        spread = by_head(qkv_ref[s, 0], mask, heads)
        pulled = by_head(attended_grad_ref[s], mask, heads)
        score_here = score_ref[s, :, pl.ds(at, quarter)]
        soft_here = soft_ref[s, :, pl.ds(at, quarter)].astype(LOW)
        dk = (SCALE * tn(score_here, spread)).astype(LOW)
        dv = tn(soft_here, pulled).astype(LOW)
        extra = nn(dk, attn_ref[0]) + nn(dv, attn_ref[1])
        grad_token_ref[s] = moved_ref[s].astype(FULL) + extra
    grad_token_ref[writes] = moved_ref[writes].astype(FULL)


def finish(
    order_a,
    order_b,
    memory_rows,
    numbers,
    *refs,
):
    groups = []
    for number in numbers:
        groups.append(refs[:number])
        refs = refs[number:]
    factor_refs, *groups = groups

    def total_of(group, *at):
        total = group[0][(0, *at)].astype(FULL)
        for ref in group[1:]:
            total = total + ref[(0, *at)].astype(FULL)
        return total

    ffn_a, ffn_b, attn_terms, own_terms = groups
    (
    query_ref,
    key_ref,
    value_ref,
    b_query_ref,
    b_value_ref,
    out_ref,
    b_out_ref,
    gain_attn_ref,
    shift_attn_ref,
    up_ref,
    b_in_ref,
    down_ref,
    b_down_ref,
    gain_ffn_ref,
    shift_ffn_ref,
    init_ref,
    ) = refs
    factor = jnp.concatenate([ref[...] for ref in factor_refs], 0)
    count, _, rows, width = factor.shape
    block = width // 2 // count
    column = lax.broadcasted_iota(jnp.int32, (rows, width), 1)

    def own(j, i):
        first, second = position(j, order_a), position(j, order_b) + count
        keep = (column // block == first) | (column // block == second)
        return jnp.where(keep, factor[j, i], jnp.zeros((), LOW))

    units = []
    for side, left, right in ((0, 3, 0), (1, 2, 1)):
        chosen = jnp.concatenate([own(j, left) for j in range(count)], 0)
        others = jnp.concatenate([factor[j, right] for j in range(count)], 0)
        product = tn(chosen, others)
        halves = []
        for i in range(2):
            total = total_of((ffn_a, ffn_b)[i], side)
            for j in range(count):
                at = (i * count + j) * block
                total = total + product[at : at + block]
            halves.append(total)
        units.append(jnp.concatenate(halves, 0))
    up_ref[...] = units[0]
    down_ref[...] = units[1]
    attn, own_total = total_of(attn_terms), total_of(own_terms)
    here = attn.shape[-1] // 2
    share = own_total.shape[0] - SUM_ROWS
    totals = []
    for m in range(4):
        row, column = m % 2 * share, m // 2 * here
        from_tokens = attn[row : row + share, column : column + here]
        totals.append(from_tokens + own_total[:share, m * here : (m + 1) * here])
    query_ref[...] = totals[0]
    key_ref[...] = totals[1]
    value_ref[...] = totals[2]
    out_ref[...] = totals[3].T
    pack = attn[2 * share : 2 * share + SUM_ROWS, :here] + own_total[share:, :here]
    refs = {
        "b_out": b_out_ref,
        "gain_attn": gain_attn_ref,
        "shift_attn": shift_attn_ref,
        "b_down": b_down_ref,
        "gain_ffn": gain_ffn_ref,
        "shift_ffn": shift_ffn_ref,
    }
    part = init_ref.shape[1]
    for i, name in enumerate(SUMS):
        refs[name][...] = pack[i : i + 1, :part]
    at = len(SUMS) + memory_rows
    init_ref[...] = pack[len(SUMS) : at, :part]
    heads_here, head_part = b_query_ref.shape
    for i in range(heads_here):
        columns = slice(i * head_part, (i + 1) * head_part)
        b_query_ref[i : i + 1, :] = pack[at : at + 1, columns]
        b_value_ref[i : i + 1, :] = pack[at + 1 : at + 2, columns]
    b_in_ref[:, :block] = pack[at + 2 : at + 3, :block]
    b_in_ref[:, block:] = pack[at + 3 : at + 4, :block]


def columns_of(head, head_dim, array, factor=None):
    lane = lax.broadcasted_iota(jnp.int32, array.shape, 1) // head_dim
    if factor is not None:
        array = array * jnp.asarray(factor, array.dtype)
    return jnp.where(lane == head, array, jnp.zeros((), array.dtype))


def memory_scores(memory_rows, km, mine):
    scores = nt(km, mine)
    real_key = lax.broadcasted_iota(jnp.int32, scores.shape, 0) < memory_rows
    return jnp.where(real_key, scores, NEGATIVE)


def token_attention(head_dim, place_ref, row_ref, column_ref, q_ref, k_ref, v_ref, sum_ref, stat_ref):
    q, k, v = q_ref[...], k_ref[...], v_ref[...]
    allowed = column_ref[...] == row_ref[...]
    stat_ref[...] = jnp.zeros_like(stat_ref)
    for head in range(q.shape[1] // head_dim):
        scores = nt(k, columns_of(head, head_dim, q, SCALE))
        scores = jnp.where(allowed, scores, NEGATIVE)
        top = jnp.max(scores, 0, keepdims=True)
        raised = jnp.exp(scores - top)
        stat_ref[0, 2 * head : 2 * head + 1] = top
        stat_ref[0, 2 * head + 1 : 2 * head + 2] = jnp.sum(raised, 0, keepdims=True)
        rows = slice(head * head_dim, (head + 1) * head_dim)
        sum_ref[0, rows] = tn(v, raised.astype(LOW))[rows]


def with_memory(
    memory_rows, head_dim, place_ref, q_ref, qkv_ref, sum_ref, stat_ref, out_ref, log_ref
):
    q, km, vm = q_ref[...], qkv_ref[place_ref[1], 1], qkv_ref[place_ref[1], 2]
    log_ref[...] = jnp.zeros_like(log_ref)
    mixed = []
    for head in range(q.shape[1] // head_dim):
        scores = memory_scores(memory_rows, km, columns_of(head, head_dim, q, SCALE))
        top_before = stat_ref[0, 2 * head : 2 * head + 1]
        top = jnp.maximum(jnp.max(scores, 0, keepdims=True), top_before)
        raised = jnp.exp(scores - top)
        shrink = jnp.exp(top_before - top)
        total = stat_ref[0, 2 * head + 1 : 2 * head + 2] * shrink
        total = total + 2.0 * jnp.sum(raised, 0, keepdims=True)
        rows = slice(head * head_dim, (head + 1) * head_dim)
        both = sum_ref[0, rows] * shrink + 2.0 * tn(vm, raised.astype(LOW))[rows]
        mixed.append(both * (1.0 / total))
        log_ref[0, head : head + 1] = top + jnp.log(total)
    out_ref[...] = jnp.concatenate(mixed, 0).T.astype(LOW)


def token_attention_back(
    memory_rows,
    head_dim,
    place_ref,
    row_ref,
    column_ref,
    q_ref,
    k_ref,
    v_ref,
    qkv_ref,
    log_ref,
    grad_ref,
    dq_ref,
    dk_ref,
    dv_ref,
    dmem_ref,
):
    q, k, v, grad = (ref[...] for ref in (q_ref, k_ref, v_ref, grad_ref))
    km, vm = qkv_ref[place_ref[1], 1], qkv_ref[place_ref[1], 2]
    allowed = column_ref[...] == row_ref[...]
    lane = lax.broadcasted_iota(jnp.int32, q.shape, 1) // head_dim
    dq, dk, dv = (jnp.zeros(q.shape, FULL) for _ in range(3))
    dkm, dvm = (jnp.zeros(km.shape, FULL) for _ in range(2))
    for head in range(q.shape[1] // head_dim):
        mine = columns_of(head, head_dim, q, SCALE)
        mine_grad = columns_of(head, head_dim, grad)
        log_total = log_ref[0, head : head + 1]
        scores = jnp.where(allowed, nt(k, mine), NEGATIVE)
        soft = jnp.exp(scores - log_total)
        soft_mem = jnp.exp(memory_scores(memory_rows, km, mine) - log_total)
        pull, pull_mem = nt(v, mine_grad), nt(vm, mine_grad)
        inner = jnp.sum(soft * pull, 0, keepdims=True) + 2.0 * jnp.sum(
            soft_mem * pull_mem, 0, keepdims=True
        )
        score = (soft * (pull - inner)).astype(LOW)
        score_mem = (soft_mem * (pull_mem - inner)).astype(LOW)
        dq = jnp.where(lane == head, tn(score, k) + 2.0 * tn(score_mem, km), dq)
        dk = dk + nn(score, mine)
        dv = dv + nn(soft.astype(LOW), mine_grad)
        dkm = dkm + nn(score_mem, mine)
        dvm = dvm + nn(soft_mem.astype(LOW), mine_grad)
    dq_ref[...] = (SCALE * dq).astype(LOW)
    dk_ref[...] = dk.astype(LOW)
    dv_ref[...] = dv.astype(LOW)
    dmem_ref[:PAD] = dkm
    dmem_ref[PAD:] = dvm


def head_pairs(body, place, doc, operands, shapes, width, flops, steps, first=0):
    seg_len = operands[0].shape[0]

    def spec(array, first):
        if len(array.shape) == 4:
            return pl.BlockSpec((*array.shape[:3], width), lambda i: (0, 0, 0, i + first))
        if len(array.shape) == 3:
            return pl.BlockSpec((1, *array.shape[1:]), lambda i: (i + first, 0, 0))
        return pl.BlockSpec((array.shape[0], width), lambda i: (0, i + first))

    return pl.pallas_call(
        body,
        grid=(steps,),
        out_shape=shapes,
        in_specs=[pl.BlockSpec(memory_space=pltpu.SMEM)]
        + [pl.BlockSpec(a.shape, lambda i: (0, 0)) for a in doc]
        + [spec(a, first) for a in operands],
        out_specs=[spec(s, 0) for s in shapes],
        compiler_params=pltpu.CompilerParams(vmem_limit_bytes=VMEM_LIMIT),
        cost_estimate=pl.CostEstimate(
            flops=flops // 1000, bytes_accessed=seg_len, transcendentals=0
        ),
    )(place, *doc, *operands)


def on_device(
    tokens,
    doc_ids,
    reset,
    mem_init,
    w_query,
    w_key,
    w_value,
    b_query,
    b_value,
    w_out,
    b_out,
    gain_attn,
    shift_attn,
    w_in,
    b_in,
    w_down,
    b_down,
    gain_ffn,
    shift_ffn,
    cotangent,
):
    chains, segments, seg_len, width = tokens.shape
    dps, groups = lax.axis_size("dp"), lax.axis_size("head")
    assert chains == 1 and segments == groups
    memory_rows = mem_init.shape[0]
    heads_here, head_dim = b_query.shape
    heads = heads_here * groups
    here = heads_here * head_dim
    units = w_in.shape[1]
    half_units = units // 2
    quarter = seg_len // groups
    dp, head = lax.axis_index("dp"), lax.axis_index("head")
    place = jnp.stack([dp, head])
    bits = bits_of(dps)
    levels = len(bits)
    order_a = bits[1:] + bits[:1]
    order_b = bits[1:][::-1] + bits[:1]
    head_order = bits_of(groups)[::-1]
    head_stages = [("head", bit) for bit in head_order]
    stages_a = head_stages + [("dp", bit) for bit in order_a]
    stages_b = head_stages + [("dp", bit) for bit in order_b]
    layout = Units(dps, groups, half_units, width)
    landing = layout.scratch()
    shape = jax.ShapeDtypeStruct
    dp_stages = [("dp", bit) for bit in bits]
    bias_groups = (head_stages[:1], dp_stages[1:], head_stages[1:] + dp_stages[:1])
    bias_stages = [stage for group in bias_groups for stage in group]
    tokens, doc_ids, cotangent = tokens[0], doc_ids[0], cotangent[0]

    shard = jnp.concatenate([w_query.T, w_key.T, w_value.T, w_out], 0)
    share = shard.shape[0] // dps
    chunk = lax.dynamic_slice_in_dim(shard, dp * share, share, 0)[None]
    biases = jnp.concatenate([b_query.reshape(-1), b_value.reshape(-1), b_in])[None]
    up = w_in.T.reshape(2, half_units, width)
    down = w_down.reshape(2, half_units, width)
    halves = [jnp.stack([up[i], down[i]])[None] for i in range(2)]
    for i, stage in enumerate(head_stages):
        chunk = gather(chunk, [stage])
        if i:
            halves = [gather(half, [head_stages[i - 1]]) for half in halves]
        biases = gather(biases, bias_groups[i])
        chunk, biases, halves = lax.optimization_barrier((chunk, biases, halves))
    halves = [gather(half, head_stages[-1:]) for half in halves]
    biases = gather(biases, bias_groups[2])
    chunk = jnp.stack([chunk[position(j, head_order)] for j in range(1, groups)])
    parts = []

    def joined(part, have, bit):
        at = sum(1 for b in have if b > bit)
        mine = (dp // bit) % 2
        other = swap(part, "dp", bit)
        return jnp.where(mine == 1, jnp.stack([other, part], at), jnp.stack([part, other], at))

    for rows, order in ((slice(0, share // 2), order_a), (slice(share // 2, share), order_b)):
        part = chunk[:, rows]
        for i, bit in enumerate(order[:-1]):
            part = joined(part, order[:i], bit)
        parts.append(part)
    doc = lax.dynamic_index_in_dim(doc_ids, head, 0, False)
    doc_row, doc_column = doc[None, :], doc[:, None]
    init = jnp.pad(mem_init.astype(FULL), ((0, PAD - memory_rows), (0, 0)))
    vectors = jnp.concatenate([b_out, gain_attn, shift_attn, b_down, gain_ffn, shift_ffn])
    vectors = vectors.reshape(-1, width)
    halves, parts, biases, cotangent, doc_row, doc_column, init, vectors = (
        lax.optimization_barrier(
            (halves, parts, biases, cotangent, doc_row, doc_column, init, vectors)
        )
    )
    parts = [
        joined(part, order[:-1], order[-1]).reshape(dps, groups - 1, share // 2, width)
        for part, order in zip(parts, (order_a, order_b))
    ]
    others = jnp.concatenate(parts, 2).transpose(1, 0, 2, 3).reshape(groups - 1, 4, here, width)
    cotangent = lax.all_to_all(cotangent, "head", 0, 0, tiled=True).reshape(seg_len, width)
    w_attn = jnp.concatenate([shard.reshape(4, 1, here, width), others.transpose(1, 0, 2, 3)], 1)
    w_attn = w_attn.reshape(4, groups * here, width)
    halves = [
        gather(half, stages[len(head_stages) : -2])
        for half, stages in zip(halves, (stages_a, stages_b))
    ]
    keys, values, x, q, k, v, vectors, bias_in = whole_call(
        functools.partial(project, layout, bias_stages, order_a, order_b, head_order),
        (place,),
        (tokens, w_attn, biases, vectors),
        (),
        (shape(tokens.shape, LOW),) * 2
        + (shape((seg_len, width), LOW),) * 4
        + (shape((len(VECTORS), width), FULL), shape((layout.chunks, 1, layout.size), FULL)),
        6_000_000_000,
    )

    pair = 2 * head_dim
    partial = head_pairs(
        functools.partial(token_attention, head_dim),
        place,
        (doc_row, doc_column),
        (q, k, v),
        (shape((width // pair, pair, seg_len), FULL), shape((width // pair, 8, seg_len), FULL)),
        pair,
        8_000_000_000,
        width // pair,
    )
    halves = lax.optimization_barrier(halves)
    other_halves = [
        swap(half, *stages[-2]) for half, stages in zip(halves, (stages_a, stages_b))
    ]
    other_halves, partial, keys, cotangent = lax.optimization_barrier(
        (other_halves, partial, keys, cotangent)
    )
    pieces = []
    for half, other, stages in zip(halves, other_halves, (stages_a, stages_b)):
        pieces += [half, other, swap(half, *stages[-1]), swap(other, *stages[-1])]
    if layout.whole:
        pieces = layout.assembled([jnp.concatenate(pieces[i : i + 4], 0) for i in (0, 4)])

    ff = layout.chunks * layout.size
    writes = segments - 1
    rows_shape = lambda kind: shape((writes, PAD, width), kind)
    tokens_scratch = lambda count: (
        pltpu.VMEM((4, width, width), LOW),
        pltpu.VMEM((count, seg_len, width), LOW),
        pltpu.VMEM((count, seg_len, width), LOW),
        pltpu.SemaphoreType.DMA((4,)),
        pltpu.SemaphoreType.DMA((count,)),
        pltpu.SemaphoreType.DMA((count,)),
    )
    read, qkv, soft, soft_mem, attended_w, z_attn_w, hidden_w, pre_w, z_ffn_w, norms = whole_call(
        functools.partial(chain_forward, layout, heads, memory_rows),
        (reset,),
        (init, bias_in, vectors),
        (w_attn, keys, values, *pieces),
        (
            shape((segments, PAD, width), FULL),
            shape((segments, 3, PAD, width), LOW),
            shape((writes, heads * PAD, seg_len), FULL),
            shape((writes, heads * PAD, PAD), FULL),
            rows_shape(LOW),
            rows_shape(FULL),
            rows_shape(LOW),
            shape((writes, PAD, ff), FULL),
            rows_shape(FULL),
            shape((1, 128), FULL),
        ),
        20_000_000_000,
        tokens_scratch(writes) + landing,
    )

    attended, log_total = head_pairs(
        functools.partial(with_memory, memory_rows, head_dim),
        place,
        (),
        (q, qkv, *partial),
        (shape((seg_len, width), LOW), shape((width // pair, 8, seg_len), FULL)),
        pair,
        8_000_000_000,
        width // pair,
    )
    if layout.whole:
        grad_shapes = (shape((layout.chunks, 2, layout.size, width), LOW),)
    else:
        grad_shapes = (shape((layout.blocks // 2, 2, half_units, width), LOW),) * 4
    sides = 2 * max(layout.size // (layout.size if layout.whole else half_units), 1)
    result, grad_attn, grad_mixed, grad_attended, bias_sum, layer_sums, *ffn_grads = whole_call(
        functools.partial(token_layer, layout),
        (),
        (x, attended, cotangent, bias_in, vectors),
        (w_attn, *pieces),
        (
            shape((seg_len, width), LOW),
            shape((seg_len, width), FULL),
            shape((seg_len, width), LOW),
            shape((seg_len, width), LOW),
            shape((layout.chunks, 1, layout.size), FULL),
            shape((8, width), FULL),
        ),
        25_000_000_000,
        (pltpu.VMEM((width, width), LOW), pltpu.SemaphoreType.DMA(()))
        + landing
        + (
            pltpu.VMEM((seg_len, width), FULL),
            pltpu.VMEM((seg_len, width), LOW),
            pltpu.VMEM((seg_len, width), LOW),
            pltpu.VMEM((seg_len, width), FULL),
            pltpu.VMEM((layout.chunks, seg_len, layout.size), FULL),
            pltpu.VMEM((layout.chunks, seg_len, layout.size), LOW),
            pltpu.VMEM((2, 2, layout.size, width), LOW),
            pltpu.SemaphoreType.DMA((layout.chunks, sides)),
        ),
        grad_shapes,
    )
    if layout.whole:
        half_blocks = layout.blocks // 2
        ffn_grads = [
            part
            for half in layout.taken_apart(ffn_grads[0])
            for part in (half[:half_blocks], half[half_blocks:])
        ]

    back_a, back_b = stages_a[::-1], stages_b[::-1]

    def stages_of(level):
        return back_a[level], back_b[level]

    def attention_back(block, count):
        cut = width // 2
        return head_pairs(
            functools.partial(token_attention_back, memory_rows, head_dim),
            place,
            (doc_row, doc_column),
            (q, k, v, qkv, log_total, grad_attended),
            (shape((seg_len, cut), LOW),) * 3 + (shape((2 * PAD, cut), FULL),),
            pair,
            10_000_000_000,
            count,
            block * count,
        )

    blocks = width // pair // 2
    moving = [
        [keep, swap(send, *back[0])]
        for keep, send, back in zip(ffn_grads[::2], ffn_grads[1::2], (back_a, back_b))
    ]
    back_low = attention_back(0, blocks)
    back_low, moving, grad_attended, result = lax.optimization_barrier(
        (back_low, moving, grad_attended, result)
    )
    sends = parcels(moving)
    sends, grad_attended, result = lax.optimization_barrier((sends, grad_attended, result))
    moving = posted(moving, sends, stages_of(1))
    output = lax.all_to_all(result.reshape(groups, quarter, width), "head", 0, 0, tiled=True)
    back_high = attention_back(1, blocks)
    token_part = jnp.concatenate([back_low[3], back_high[3]], 1)
    token_part, back_high = lax.optimization_barrier((token_part, back_high))
    token_parts = gather(token_part[None], head_stages[:1])
    share = width // dps
    rows_a, rows_b, rows_own = 2 * share + SUM_ROWS, 2 * share, share + SUM_ROWS
    keep_b, send_b, grad_x, value_sum = whole_call(
        functools.partial(value_grads, order_b, dps),
        (place,),
        (x, grad_mixed, attended, back_low[2], back_high[2], grad_attn),
        (w_attn,),
        (
            *(shape((dps // 2, rows_b, width), LOW),) * 2,
            shape((seg_len, width), FULL),
            shape((1, width), FULL),
        ),
        5_000_000_000,
        (pltpu.VMEM((width, width), LOW), pltpu.SemaphoreType.DMA(())),
    )
    down_a, down_b = ([("dp", bit) for bit in order[::-1]] for order in (order_a, order_b))
    grad_x, send_b, moving, output, token_parts = lax.optimization_barrier(
        (grad_x, send_b, moving, output, token_parts)
    )
    token_parts = gather(token_parts, head_stages[1:])
    other_b = swap(send_b, *down_b[0])
    sends = parcels(moving)
    sends, grad_x = lax.optimization_barrier((sends, grad_x))
    moving = posted(moving, sends, stages_of(2))
    for level in range(3, levels):
        moving = posted(moving, parcels(moving), stages_of(level))
    sum_scratch = (pltpu.VMEM((SUM_ROWS, width), FULL),)
    keep_a, send_a, grad_x = whole_call(
        functools.partial(
            query_key_grads, layout, order_a, order_b, head_order, heads_here, memory_rows
        ),
        (place,),
        (
            x,
            back_low[0],
            back_high[0],
            back_low[1],
            back_high[1],
            grad_x,
            value_sum,
            layer_sums,
            bias_sum,
        ),
        (w_attn,),
        (
            *(shape((dps // 2, rows_a, width), LOW),) * 2,
            shape((seg_len, width), LOW),
        ),
        10_000_000_000,
        sum_scratch + (pltpu.VMEM((2, width, width), LOW), pltpu.SemaphoreType.DMA((2,))),
    )

    def advance_both(parts, level):
        return [reduce_step(p, down[level]) for p, down in zip(parts, (down_a, down_b))]

    token_parts, send_a, other_b, grad_x, moving = lax.optimization_barrier(
        (token_parts, send_a, other_b, grad_x, moving)
    )
    attn_moving = [[keep_a, swap(send_a, *down_a[0])], [keep_b, other_b]]
    sends = parcels(moving, True)
    attn_moving, sends = lax.optimization_barrier((attn_moving, sends))
    others = swap(sends[0], *back_a[levels])
    sends = parcels(attn_moving)
    sends, grad_x, token_parts = lax.optimization_barrier((sends, grad_x, token_parts))
    attn_moving = posted(attn_moving, sends, (down_a[1], down_b[1]))
    moved = lax.all_to_all(grad_x.reshape(groups, quarter, width), "head", 0, 0, tiled=True)

    packed_rows = writes * memory_rows + (-writes * memory_rows) % PAD
    score_w, grad_attended_w, grad_mixed_w, small_w, factors, bias_w, vec_w, init_w, norms = whole_call(
        functools.partial(chain_backward, layout, head_order, heads, memory_rows),
        (reset, place),
        (
            bias_in,
            read,
            norms,
            vectors,
            qkv,
            soft,
            soft_mem,
            z_attn_w,
            pre_w,
            z_ffn_w,
            hidden_w,
            token_parts,
        ),
        (w_attn, keys, values, *pieces),
        (
            shape((writes, heads * PAD, seg_len), LOW),
            shape((writes, PAD, width), LOW),
            shape((writes, PAD, width), LOW),
            shape((segments, 3, PAD, width), LOW),
            shape((4, packed_rows, width), LOW),
            shape((layout.chunks, 1, layout.size), FULL),
            shape((len(VECTORS), width), FULL),
            shape((PAD, width), FULL),
            shape((1, 128), FULL),
        ),
        20_000_000_000,
        (
            pltpu.VMEM((writes, PAD, width), LOW),
            pltpu.VMEM((writes, PAD, ff), LOW),
            pltpu.VMEM((segments, 2 * PAD, width), FULL),
        )
        + tokens_scratch(segments)
        + landing,
    )
    score_w, factors, moving, others, attn_moving, moved = lax.optimization_barrier(
        (score_w, factors, moving, others, attn_moving, moved)
    )

    moving = [terms + [others[:, i]] for i, terms in enumerate(moving)]
    sends = parcels(moving + attn_moving, True)
    sends, score_w = lax.optimization_barrier((sends, score_w))
    others = swap(sends[0], *back_a[levels + 1])
    moving = [terms + [others[:, i]] for i, terms in enumerate(moving)]
    attn_moving = posted(attn_moving, sends[1:], (down_a[2], down_b[2]))
    for level in range(3, levels):
        attn_moving = advance_both(attn_moving, level)
    factors = gather(factors[None], [("dp", order_a[0])])
    keep_own, send_own = whole_call(
        functools.partial(
            own_grads, layout, order_a, order_b, head_order, heads, heads_here, memory_rows
        ),
        (place,),
        (
            score_w,
            soft,
            qkv,
            grad_attended_w,
            grad_mixed_w,
            attended_w,
            small_w,
            read,
            tokens,
            bias_w,
            vec_w,
            init_w,
        ),
        (),
        (shape((dps // 2, rows_own, width), LOW),) * 2,
        5_000_000_000,
        sum_scratch,
    )
    keep_own, send_own, attn_moving, factors, score_w, moving = lax.optimization_barrier(
        (keep_own, send_own, attn_moving, factors, score_w, moving)
    )
    own = [keep_own, swap(send_own, *down_a[0])]
    left, right = (summed(terms)[0] for terms in attn_moving)
    right = jnp.pad(right, ((0, SUM_ROWS), (0, 0)))
    both = [
        jnp.concatenate([part[:, g * here : (g + 1) * here] for part in (left, right)], 1)
        for g in range(groups)
    ]
    attn_moving = [jnp.stack([both[partner(i, head_stages, "head")] for i in range(groups)])]
    attn_send = summed(attn_moving, LOW, groups // 2)
    own_send = summed(own, LOW, own[-1].shape[0] // 2)
    attn_send, own_send, score_w = lax.optimization_barrier((attn_send, own_send, score_w))
    attn_moving = attn_moving + [swap(attn_send, "head", head_order[-1])]
    own = own + [swap(own_send, *down_a[1])]
    factors = gather(factors, [("dp", order_a[1])])
    (grad_tokens,) = whole_call(
        functools.partial(write_rows, heads, quarter),
        (place,),
        (score_w, soft, qkv, grad_attended_w, moved),
        (w_attn,),
        (shape((segments, quarter, width), FULL),),
        5_000_000_000,
        (pltpu.VMEM((2, width, width), LOW), pltpu.SemaphoreType.DMA((2,))),
    )
    grad_tokens, own, factors, attn_moving = lax.optimization_barrier(
        (grad_tokens, own, factors, attn_moving)
    )
    for bit in head_order[:-1][::-1]:
        attn_moving = reduce_step(attn_moving, ("head", bit))
    factors = gather(factors, stages_a[len(head_stages) + 2 : -1])
    factors = [factors, swap(factors, *stages_a[-1])]
    for level in range(2, levels):
        own = reduce_step(own, down_a[level])
    own, factors, attn_moving, moving = lax.optimization_barrier(
        (own, factors, attn_moving, moving)
    )
    part = width // dps // groups
    row = shape((1, part), FULL)
    groups_in = [factors, *moving, attn_moving, own]
    first_entry = lambda array: pl.BlockSpec(
        (1, *array.shape[1:]), lambda i: (0,) * len(array.shape)
    )
    whole = lambda array: pl.BlockSpec(array.shape, lambda i: (0,) * len(array.shape))
    shapes = (
        *(shape((share, here), FULL),) * 3,
        *(shape((heads_here, head_dim // dps), FULL),) * 2,
        shape((here, share), FULL),
        *(row,) * 3,
        shape((units, width), FULL),
        shape((1, units), FULL),
        shape((units, width), FULL),
        *(row,) * 3,
        shape((memory_rows, part), FULL),
    )
    outs = pl.pallas_call(
        functools.partial(
            finish,
            order_in(order_a, order_a),
            order_in(order_b, order_a),
            memory_rows,
            [len(group) for group in groups_in],
        ),
        grid=(1,),
        out_shape=shapes,
        in_specs=[whole(a) for a in factors]
        + [first_entry(a) for group in groups_in[1:] for a in group],
        out_specs=[whole(a) for a in shapes],
        compiler_params=pltpu.CompilerParams(vmem_limit_bytes=VMEM_LIMIT),
        cost_estimate=pl.CostEstimate(flops=1000, bytes_accessed=1000, transcendentals=0),
    )(*(a for group in groups_in for a in group))
    flat = (6, 7, 8, 10, 12, 13, 14)
    outs = [out.reshape(-1) if i in flat else out for i, out in enumerate(outs)]
    outs[9] = outs[9].T
    return (output[None], norms[:, :segments], grad_tokens[None], *outs)


def solution(mesh):
    in_specs = (
        P("dp", None, None, None),
        P("dp", None, None),
        P("dp", None),
        P(),
        P(None, "head"),
        P(None, "head"),
        P(None, "head"),
        P("head", None),
        P("head", None),
        P("head", None),
        P(),
        P(),
        P(),
        P(None, ("dp", "head")),
        P(("dp", "head")),
        P(("dp", "head"), None),
        P(),
        P(),
        P(),
        P("dp", None, "head", None),
    )
    out_specs = (
        P("dp", None, "head", None),
        P("dp", None),
        P("dp", None, "head", None),
        P("dp", "head"),
        P("dp", "head"),
        P("dp", "head"),
        P("head", "dp"),
        P("head", "dp"),
        P("head", "dp"),
        P(("dp", "head")),
        P(("dp", "head")),
        P(("dp", "head")),
        P(None, ("dp", "head")),
        P(("dp", "head")),
        P(("dp", "head"), None),
        P(("dp", "head")),
        P(("dp", "head")),
        P(("dp", "head")),
        P(None, ("dp", "head")),
    )
    return jax.shard_map(
        on_device, mesh=mesh, in_specs=in_specs, out_specs=out_specs, check_vma=False
    )
```

profile of v0, /device:TPU:0, one launch (start us, length us, event | category | flops | bytes accessed | tf_op | source)
XLA Modules:
  0.0 358.0 jit_solution(834613741602797546)
XLA Ops:
  0.7 1.4 pad_maximum_fusion.1
  3.1 4.1 %collective-permute-start = (bf16[1,96,768]{2,1,0:T(8,128)(2,1)S(1)}, bf16[1,96,768]{2,1,0:T(8,128)(2,1)S(1)}, u32[]{:S(2)}, u32[]{:S(2)}) collective-permute-start(bf16[1,96,768]{2,1,0:T(8,128)(2,1)S(1)} %dynamic-slice_bitcast_fusion), channel_id=1, source_target_pairs={{0,2},{1,3},{2,0},{3,1},{4,6},{5,7},{6,4},{7,5},{8,10},{9,11},{10,... | collective-permute-start | bytes 442376 | tf_op jit(solution)/shard_map/ppermute | solution.py:54
  7.6 6.7 %collective-permute-done.1 = bf16[1,480]{1,0:T(2,128)(2,1)S(1)} collective-permute-done((bf16[1,480]{1,0:T(2,128)(2,1)S(1)}, bf16[1,480]{1,0:T(2,128)(2,1)S(1)}, u32[]{:S(2)}, u32[]{:S(2)}) %collective-permute-start.1) | collective-permute-done | bytes 992 | tf_op jit(solution)/shard_map/ppermute | solution.py:54
  14.4 1.6 collective-permute-start.3
  16.0 2.0 collective-permute-done.3
  18.1 1.6 collective-permute-start.4
  20.3 2.0 collective-permute-start.2
  22.3 2.1 collective-permute-start.6
  25.1 6.0 %collective-permute-done.6 = bf16[1,2,48,768]{3,2,1,0:T(8,128)(2,1)S(1)} collective-permute-done((bf16[1,2,48,768]{3,2,1,0:T(8,128)(2,1)S(1)}, bf16[1,2,48,768]{3,2,1,0:T(8,128)(2,1)S(1)}, u32[]{:S(2)}, u32[]{:S(2)}) %collective-permute-start.6) | collective-permute-done | bytes 147488 | tf_op jit(solution)/shard_map/ppermute | solution.py:54
  31.1 2.2 collective-permute-done.2
  33.8 1.5 collective-permute-start.9
  35.3 1.9 collective-permute-done.13
  37.2 1.3 dynamic-slice_bitcast_fusion.1
  40.4 1.9 collective-permute-start.8
  43.6 1.6 collective-permute-start.10
  45.1 5.5 %collective-permute-done.11 = bf16[3,48,768]{2,1,0:T(8,128)(2,1)S(1)} collective-permute-done((bf16[3,48,768]{2,1,0:T(8,128)(2,1)S(1)}, bf16[3,48,768]{2,1,0:T(8,128)(2,1)S(1)}, u32[]{:S(2)}, u32[]{:S(2)}) %collective-permute-start.11) | collective-permute-done | bytes 221216 | tf_op jit(solution)/shard_map/ppermute | solution.py:54
  51.5 4.5 %collective-permute-done.8 = bf16[2,2,48,768]{3,2,1,0:T(8,128)(2,1)S(1)} collective-permute-done((bf16[2,2,48,768]{3,2,1,0:T(8,128)(2,1)S(1)}, bf16[2,2,48,768]{3,2,1,0:T(8,128)(2,1)S(1)}, u32[]{:S(2)}, u32[]{:S(2)}) %collective-permute-start.8) | collective-permute-done | bytes 294944 | tf_op jit(solution)/shard_map/ppermute | solution.py:54
  56.1 3.0 collective-permute-done.10
  63.5 4.8 %all-to-all-start = ((bf16[4,128,768]{2,1,0:T(8,128)(2,1)}), bf16[4,128,768]{2,1,0:T(8,128)(2,1)}, u32[]{:S(2)}, u32[]{:S(2)}) async-start(bf16[4,128,768]{2,1,0:T(8,128)(2,1)} %bitcast.25), calls=%async_computation | async-start | bytes 1572864 | tf_op jit(solution)/shard_map/all_to_all | solution.py:1421
  68.3 7.2 %collective-permute-done.17 = bf16[4,2,48,768]{3,2,1,0:T(8,128)(2,1)S(1)} collective-permute-done((bf16[4,2,48,768]{3,2,1,0:T(8,128)(2,1)S(1)}, bf16[4,2,48,768]{3,2,1,0:T(8,128)(2,1)S(1)}, u32[]{:S(2)}, u32[]{:S(2)}) %collective-permute-start.17) | collective-permute-done | bytes 589856 | tf_op jit(solution)/shard_map/ppermute | solution.py:54
  76.5 1.5 collective-permute-start.20
  79.9 2.3 maximum_select_fusion.1
  82.4 2.3 maximum_select_fusion
  86.8 2.5 copy.44
  89.3 12.6 %shard_map.339 = (bf16[4,512,768]{2,1,0:T(8,128)(2,1)}, bf16[4,512,768]{2,1,0:T(8,128)(2,1)}, bf16[512,768]{1,0:T(8,128)(2,1)}, bf16[512,768]{1,0:T(8,128)(2,1)}...) custom-call(s32[2]{0:T(128)} %pad_add_fusion.place_ref, ...), custom_call_target="tpu_custom_call" | custom-call | flops 6000000 | bytes 17378 | tf_op jit(solution)/shard_map/pallas_call | solution.py:599
  101.9 9.5 %shard_map.340 = (f32[6,128,512]{2,1,0:T(8,128)}, f32[6,8,512]{2,1,0:T(8,128)}) custom-call(s32[2]{0:T(128)} %pad_add_fusion.place_ref, s32[1,512]{1,0:T(1,128)} %get-tuple-element.278.row_ref, s32[512,1]{1,0:T(8,128)} %copy.45.column_ref, bf16[512,768]{1,0:T(8,128)(2,1)} %get-tuple-element.270.q_ref, bf16[512,768]{1,0:T(8,128)(2,1)} %get-tuple-element.280.k_ref, ...), custom_call_target="tpu_custom_call" | custom-call | flops 8000000 | bytes 512 | tf_op jit(solution)/shard_map/pallas_call | solution.py:1312
  112.0 3.2 collective-permute-done.22.refs_3_.refs_7_
  117.3 26.7 %shard_map.341 = (f32[4,16,768]{2,1,0:T(8,128)}, bf16[4,3,16,768]{3,2,1,0:T(8,128)(2,1)}, f32[3,192,512]{2,1,0:T(8,128)}, f32[3,192,16]{2,1,0:T(8,128)}, bf16[3,...) custom-call(s32[1,4]{1,0:T(1,128)} %reset_ref.3, ...), custom_call_target="tpu_custom_call" | custom-call | flops 20000000 | bytes 23273 | tf_op jit(solution)/shard_map/pallas_call | solution.py:599
  144.0 6.5 %shard_map.342 = (bf16[512,768]{1,0:T(8,128)(2,1)}, f32[6,8,512]{2,1,0:T(8,128)}) custom-call(s32[2]{0:T(128)} %pad_add_fusion.place_ref, bf16[512,768]{1,0:T(8,128)(2,1)} %get-tuple-element.270.q_ref, bf16[4,3,16,768]{3,2,1,0:T(8,128)(2,1)} %get-tuple-element.290.qkv_ref, f32[6,128,512]{2,1,0:T(8,128)} %get-tuple-element.291.sum_ref, ...), custom_call_target="tpu_custom_call" | custom-call | flops 8000000 | bytes 512 | tf_op jit(solution)/shard_map/pallas_call | solution.py:1312
  150.5 33.2 %shard_map.343 = (bf16[512,768]{1,0:T(8,128)(2,1)}, f32[512,768]{1,0:T(8,128)}, bf16[512,768]{1,0:T(8,128)(2,1)}, bf16[512,768]{1,0:T(8,128)(2,1)}, f32[4,1,768]...) custom-call(bf16[512,768]{1,0:T(8,128)(2,1)} %get-tuple-element.269., ...), custom_call_target="tpu_custom_call" | custom-call | flops 25000000 | bytes 20520 | tf_op jit(solution)/shard_map/pallas_call | solution.py:599
  184.3 9.3 %shard_map.344 = (bf16[512,384]{1,0:T(8,128)(2,1)}, bf16[512,384]{1,0:T(8,128)(2,1)}, bf16[512,384]{1,0:T(8,128)(2,1)}, f32[32,384]{1,0:T(8,128)}) custom-call(s32[2]{0:T(128)} %pad_add_fusion.place_ref, s32[1,512]{1,0:T(1,128)} %get-tuple-element.278.row_ref, s32[512,1]{1,0:T(8,128)} %copy.45.column_ref, bf16[512,768]{1,0:T(8,128)(2,1)} %get-tuple-element.270.q_ref, ...), custom_call_target="tpu_custom_call" | custom-call | flops 10000000 | bytes 512 | tf_op jit(solution)/shard_map/pallas_call | solution.py:1312
  193.6 1.5 copy-done
  195.1 4.3 %shard_map.345 = (bf16[8,2,48,768]{3,2,1,0:T(8,128)(2,1)}, bf16[8,2,48,768]{3,2,1,0:T(8,128)(2,1)}) custom-call(bf16[16,2,48,768]{3,2,1,0:T(8,128)(2,1)} %get-tuple-element.460.refs_0_.refs_2_, bf16[16,2,48,768]{3,2,1,0:T(8,128)(2,1)} %copy-done, bf16[16,2,48,768]{3,2,1,0:T(8,128)(2,1)} %get-tuple-element.466.refs_2_.refs_3_.refs_4_.refs_5_.refs_8_, ...), custom_call_target="tpu_custom_call" | custom-call | flops 1000 | bytes 1000 | tf_op jit(solution)/shard_map/pallas_call | solution.py:113
  199.4 1.5 collective-permute-start.27
  201.4 3.5 all-to-all-start.1
  205.0 9.3 %shard_map.346 = (bf16[512,384]{1,0:T(8,128)(2,1)}, bf16[512,384]{1,0:T(8,128)(2,1)}, bf16[512,384]{1,0:T(8,128)(2,1)}, f32[32,384]{1,0:T(8,128)}) custom-call(s32[2]{0:T(128)} %pad_add_fusion.place_ref, s32[1,512]{1,0:T(1,128)} %get-tuple-element.278.row_ref, s32[512,1]{1,0:T(8,128)} %copy.45.column_ref, bf16[512,768]{1,0:T(8,128)(2,1)} %get-tuple-element.270.q_ref, ...), custom_call_target="tpu_custom_call" | custom-call | flops 10000000 | bytes 512 | tf_op jit(solution)/shard_map/pallas_call | solution.py:1312
  215.1 2.9 collective-permute-start.29
  218.0 7.6 %shard_map.347 = (bf16[4,192,768]{2,1,0:T(8,128)(2,1)}, bf16[4,192,768]{2,1,0:T(8,128)(2,1)}, f32[512,768]{1,0:T(8,128)}, f32[1,768]{1,0:T(1,128)}) custom-call(s32[2]{0:T(128)} %pad_add_fusion.place_ref, bf16[512,768]{1,0:T(8,128)(2,1)} %get-tuple-element.269.x_ref, bf16[512,768]{1,0:T(8,128)(2,1)} %get-tuple-element.295.mixed_ref, ...), custom_call_target="tpu_custom_call" | custom-call | flops 5000000 | bytes 13372 | tf_op jit(solution)/shard_map/pallas_call | solution.py:599
  225.7 3.6 %collective-permute-done.29 = f32[1,32,768]{2,1,0:T(8,128)S(1)} collective-permute-done((f32[1,32,768]{2,1,0:T(8,128)S(1)}, f32[1,32,768]{2,1,0:T(8,128)S(1)}, u32[]{:S(2)}, u32[]{:S(2)}) %collective-permute-start.29) | collective-permute-done | bytes 98336 | tf_op jit(solution)/shard_map/ppermute | solution.py:54
  231.5 4.0 %shard_map.348 = (bf16[4,2,48,768]{3,2,1,0:T(8,128)(2,1)}, bf16[4,2,48,768]{3,2,1,0:T(8,128)(2,1)}) custom-call(bf16[16,2,48,768]{3,2,1,0:T(8,128)(2,1)} %get-tuple-element.460.refs_0_.refs_2_, bf16[16,2,48,768]{3,2,1,0:T(8,128)(2,1)} %copy-done, bf16[8,2,48,768]{3,2,1,0:T(8,128)(2,1)} %copy-done.1, ...), custom_call_target="tpu_custom_call" | custom-call | flops 1000 | bytes 1000 | tf_op jit(solution)/shard_map/pallas_call | solution.py:113
  235.5 1.5 collective-permute-start.32
  237.0 1.4 collective-permute-start.33
  238.4 10.4 %shard_map.349 = (bf16[4,224,768]{2,1,0:T(8,128)(2,1)}, bf16[4,224,768]{2,1,0:T(8,128)(2,1)}, bf16[512,768]{1,0:T(8,128)(2,1)}) custom-call(s32[2]{0:T(128)} %pad_add_fusion.place_ref, bf16[512,768]{1,0:T(8,128)(2,1)} %get-tuple-element.269.x_ref, bf16[512,384]{1,0:T(8,128)(2,1)} %get-tuple-element.339.dq0_ref, bf16[512,384]{1,0:T(8,128)(2,1)} %get-tuple-element.340.dq1_ref, ...), custom_call_target="tpu_custom_call" | custom-call | flops 10000000 | bytes 12229 | tf_op jit(solution)/shard_map/pallas_call | solution.py:599
  249.6 1.2 collective-permute-done.32.refs_3_.refs_5_
  250.8 1.2 collective-permute-done.33.refs_7_.refs_8_.refs_11_
  252.9 2.6 shard_map.350
  257.3 2.6 shard_map.351
  259.8 3.6 %all-to-all-start.2 = ((bf16[4,128,768]{2,1,0:T(8,128)(2,1)}), bf16[4,128,768]{2,1,0:T(8,128)(2,1)S(1)}, u32[]{:S(2)}, u32[]{:S(2)}) async-start(bf16[4,128,768]{2,1,0:T(8,128)(2,1)} %bitcast.42), calls=%async_computation.2 | async-start | bytes 1572864 | tf_op jit(solution)/shard_map/all_to_all | solution.py:1647
  263.5 1.4 collective-permute-start.36
  265.0 2.0 collective-permute-start.35
  267.5 29.3 %shard_map.352 = (bf16[3,192,512]{2,1,0:T(8,128)(2,1)}, bf16[3,16,768]{2,1,0:T(8,128)(2,1)}, bf16[3,16,768]{2,1,0:T(8,128)(2,1)}, bf16[4,3,16,768]{3,2,1,0:T(8,1...) custom-call(s32[1,4]{1,0:T(1,128)} %reset_ref.3, ...), custom_call_target="tpu_custom_call" | custom-call | flops 20000000 | bytes 24859 | tf_op jit(solution)/shard_map/pallas_call | solution.py:599
  296.8 1.5 collective-permute-start.40
  299.2 3.1 shard_map.353
  302.4 2.4 collective-permute-start.41
  306.0 9.1 %shard_map.354 = (bf16[4,128,768]{2,1,0:T(8,128)(2,1)}, bf16[4,128,768]{2,1,0:T(8,128)(2,1)}) custom-call(s32[2]{0:T(128)} %pad_add_fusion.place_ref, bf16[3,192,512]{2,1,0:T(8,128)(2,1)} %get-tuple-element.434.score_ref, f32[3,192,512]{2,1,0:T(8,128)} %get-tuple-element.333.soft_ref, bf16[4,3,16,768]{3,2,1,0:T(8,128)(2,1)} %get-tuple-element.290.qkv_ref, ...), custom_call_target="tpu_custom_call" | custom-call | flops 5000000 | bytes 7581 | tf_op jit(solution)/shard_map/pallas_call | solution.py:599
  315.2 2.1 collective-permute-done.41
  318.9 1.3 fusion
  320.1 1.2 fusion.1
  323.5 1.4 collective-permute-start.43
  325.3 4.8 %collective-permute-done.44 = bf16[2,4,32,768]{3,2,1,0:T(8,128)(2,1)S(1)} collective-permute-done((bf16[2,4,32,768]{3,2,1,0:T(8,128)(2,1)S(1)}, bf16[2,4,32,768]{3,2,1,0:T(8,128)(2,1)S(1)}, u32[]{:S(2)}, u32[]{:S(2)}) %collective-permute-start.44) | collective-permute-done | bytes 393248 | tf_op jit(solution)/shard_map/ppermute | solution.py:54
  330.2 6.6 %shard_map.355 = f32[4,128,768]{2,1,0:T(8,128)} custom-call(s32[2]{0:T(128)} %pad_add_fusion.place_ref, bf16[3,192,512]{2,1,0:T(8,128)(2,1)} %get-tuple-element.434.score_ref, f32[3,192,512]{2,1,0:T(8,128)} %get-tuple-element.333.soft_ref, bf16[4,3,16,768]{3,2,1,0:T(8,128)(2,1)} %get-tuple-element.290.qkv_ref, ...), custom_call_target="tpu_custom_call" | custom-call | flops 5000000 | bytes 9216 | tf_op jit(solution)/shard_map/pallas_call | solution.py:599
  336.8 1.3 collective-permute-done.43.refs_19_
  341.1 11.0 %collective-permute-done.48.refs_16_ = bf16[1,224,384]{2,1,0:T(8,128)(2,1)S(1)} collective-permute-done((bf16[1,224,384]{2,1,0:T(8,128)(2,1)S(1)}, bf16[1,224,384]{2,1,0:T(8,128)(2,1)S(1)}, u32[]{:S(2)}, u32[]{:S(2)}) %collective-permute-start.48) | collective-permute-done | bytes 172064 | tf_op jit(solution)/shard_map/ppermute | solution.py:54
  352.8 3.8 %shard_map.356 = (f32[96,192]{1,0:T(8,128)}, f32[96,192]{1,0:T(8,128)}, f32[96,192]{1,0:T(8,128)}, f32[3,8]{1,0:T(4,128)}, f32[3,8]{1,0:T(4,128)}, /*index=5*/f3...) custom-call(bf16[4,4,32,768]{3,2,1,0:T(8,128)(2,1)} %copy-done.15, ...), custom_call_target="tpu_custom_call" | custom-call | flops 1000 | bytes 1000 | tf_op jit(solution)/shard_map/pallas_call | solution.py:1781
  (216 shorter events, 38.4 us)
Async XLA Ops:
  0.7 6.7 %copy-start.40 = (bf16[96]{0:T(256)(128)(2,1)S(1)}, bf16[96]{0:T(256)(128)(2,1)}, u32[]{:S(2)}) copy-start(bf16[96]{0:T(256)(128)(2,1)} %param.34) | copy-start | bytes 580
  0.7 6.8 %copy-start.30 = (bf16[96,768]{1,0:T(8,128)(2,1)S(1)}, bf16[96,768]{1,0:T(8,128)(2,1)}, u32[]{:S(2)}) copy-start(bf16[96,768]{1,0:T(8,128)(2,1)} %param.35) | copy-start | bytes 442372
  0.7 6.8 %copy-start.31 = (bf16[768,96]{0,1:T(8,128)(2,1)S(1)}, bf16[768,96]{0,1:T(8,128)(2,1)}, u32[]{:S(2)}) copy-start(bf16[768,96]{0,1:T(8,128)(2,1)} %param.33) | copy-start | bytes 442372
  0.7 19.0 %copy-start.33 = (bf16[10,768]{1,0:T(8,128)(2,1)S(1)}, bf16[10,768]{1,0:T(8,128)(2,1)}, u32[]{:S(2)}) copy-start(bf16[10,768]{1,0:T(8,128)(2,1)} %param.23) | copy-start | bytes 46084
  3.1 11.2 %collective-permute-start = (bf16[1,96,768]{2,1,0:T(8,128)(2,1)S(1)}, bf16[1,96,768]{2,1,0:T(8,128)(2,1)S(1)}, u32[]{:S(2)}, u32[]{:S(2)}) collective-permute-start(bf16[1,96,768]{2,1,0:T(8,128)(2,1)S(1)} %dynamic-slice_bitcast_fusion), channel_id=1, source_target_pairs={{0,2},{1,3},{2,0},{3,1},{4,6},{5,7},{6,4},{7,5},{8,10},{9,11},{10,... | collective-permute-start | bytes 442376 | tf_op jit(solution)/shard_map/ppermute | solution.py:54
  7.5 6.8 %collective-permute-start.1 = (bf16[1,480]{1,0:T(2,128)(2,1)S(1)}, bf16[1,480]{1,0:T(2,128)(2,1)S(1)}, u32[]{:S(2)}, u32[]{:S(2)}) collective-permute-start(bf16[1,480]{1,0:T(2,128)(2,1)S(1)} %broadcast_in_dim.29), channel_id=1, source_target_pairs={{0,2},{1,3},{2,0},{3,1},{4,6},{5,7},{6,4},{7,5},{8,10},{9,11},{10,... | collective-permute-start | bytes 2888 | tf_op jit(solution)/shard_map/ppermute | solution.py:54
  14.4 3.7 %collective-permute-start.3 = (bf16[2,480]{1,0:T(2,128)(2,1)S(1)}, bf16[2,480]{1,0:T(2,128)(2,1)S(1)}, u32[]{:S(2)}, u32[]{:S(2)}) collective-permute-start(bf16[2,480]{1,0:T(2,128)(2,1)S(1)} %pad_maximum_fusion.22), channel_id=1, source_target_pairs={{0,8},{4,12},{8,0},{12,4},{16,24},{20,28},{24,16},{28,20},{1,9},{5... | collective-permute-start | bytes 5768 | tf_op jit(solution)/shard_map/ppermute | solution.py:54
  16.0 9.0 %collective-permute-start.5 = (bf16[1,2,48,768]{3,2,1,0:T(8,128)(2,1)S(1)}, bf16[1,2,48,768]{3,2,1,0:T(8,128)(2,1)S(1)}, u32[]{:S(2)}, u32[]{:S(2)}) collective-permute-start(bf16[1,2,48,768]{3,2,1,0:T(8,128)(2,1)S(1)} %get-tuple-element.259), channel_id=1, source_target_pairs={{0,2},{1,3},{2,0},{3,1},{4,6},{5,7},{6,4},{7,5},{8,10},{9,11},{10,... | collective-permute-start | bytes 442376 | tf_op jit(solution)/shard_map/ppermute | solution.py:54
  18.1 6.3 %collective-permute-start.4 = (bf16[4,480]{1,0:T(4,128)(2,1)S(1)}, bf16[4,480]{1,0:T(4,128)(2,1)S(1)}, u32[]{:S(2)}, u32[]{:S(2)}) collective-permute-start(bf16[4,480]{1,0:T(4,128)(2,1)S(1)} %pad_maximum_fusion.21), channel_id=1, source_target_pairs={{0,16},{4,20},{8,24},{12,28},{16,0},{20,4},{24,8},{28,12},{1,17},{... | collective-permute-start | bytes 11528 | tf_op jit(solution)/shard_map/ppermute | solution.py:54
  20.3 12.9 %collective-permute-start.2 = (bf16[2,96,768]{2,1,0:T(8,128)(2,1)S(1)}, bf16[2,96,768]{2,1,0:T(8,128)(2,1)S(1)}, u32[]{:S(2)}, u32[]{:S(2)}) collective-permute-start(bf16[2,96,768]{2,1,0:T(8,128)(2,1)S(1)} %pad_maximum_fusion.13), channel_id=1, source_target_pairs={{0,1},{1,0},{2,3},{3,2},{4,5},{5,4},{6,7},{7,6},{8,9},{9,8},{10,11... | collective-permute-start | bytes 884744 | tf_op jit(solution)/shard_map/ppermute | solution.py:54
  22.3 8.8 %collective-permute-start.6 = (bf16[1,2,48,768]{3,2,1,0:T(8,128)(2,1)S(1)}, bf16[1,2,48,768]{3,2,1,0:T(8,128)(2,1)S(1)}, u32[]{:S(2)}, u32[]{:S(2)}) collective-permute-start(bf16[1,2,48,768]{3,2,1,0:T(8,128)(2,1)S(1)} %get-tuple-element.260), channel_id=1, source_target_pairs={{0,2},{1,3},{2,0},{3,1},{4,6},{5,7},{6,4},{7,5},{8,10},{9,11},{10,... | collective-permute-start | bytes 442376 | tf_op jit(solution)/shard_map/ppermute | solution.py:54
  33.4 3.7 %collective-permute-start.13 = (bf16[8,480]{1,0:T(8,128)(2,1)S(1)}, bf16[8,480]{1,0:T(8,128)(2,1)S(1)}, u32[]{:S(2)}, u32[]{:S(2)}) collective-permute-start(bf16[8,480]{1,0:T(8,128)(2,1)S(1)} %pad_maximum_fusion.20), channel_id=1, source_target_pairs={{0,1},{1,0},{2,3},{3,2},{4,5},{5,4},{6,7},{7,6},{8,9},{9,8},{10,11... | collective-permute-start | bytes 23048 | tf_op jit(solution)/shard_map/ppermute | solution.py:54
  33.8 9.7 %collective-permute-start.9 = (bf16[3,48,768]{2,1,0:T(8,128)(2,1)S(1)}, bf16[3,48,768]{2,1,0:T(8,128)(2,1)S(1)}, u32[]{:S(2)}, u32[]{:S(2)}) collective-permute-start(bf16[3,48,768]{2,1,0:T(8,128)(2,1)S(1)} %get-tuple-element.505), channel_id=1, source_target_pairs={{0,8},{4,12},{8,0},{12,4},{16,24},{20,28},{24,16},{28,20},{1,9},{5... | collective-permute-start | bytes 663560 | tf_op jit(solution)/shard_map/ppermute | solution.py:54
  37.2 5.7 %collective-permute-start.14 = (bf16[16,480]{1,0:T(8,128)(2,1)S(1)}, bf16[16,480]{1,0:T(8,128)(2,1)S(1)}, u32[]{:S(2)}, u32[]{:S(2)}) collective-permute-start(bf16[16,480]{1,0:T(8,128)(2,1)S(1)} %pad_maximum_fusion.19), channel_id=1, source_target_pairs={{0,4},{4,0},{8,12},{12,8},{16,20},{20,16},{24,28},{28,24},{1,5},{5... | collective-permute-start | bytes 46088 | tf_op jit(solution)/shard_map/ppermute | solution.py:54
  40.3 11.1 %collective-permute-start.7 = (bf16[2,2,48,768]{3,2,1,0:T(8,128)(2,1)S(1)}, bf16[2,2,48,768]{3,2,1,0:T(8,128)(2,1)S(1)}, u32[]{:S(2)}, u32[]{:S(2)}) collective-permute-start(bf16[2,2,48,768]{3,2,1,0:T(8,128)(2,1)S(1)} %pad_maximum_fusion.14), channel_id=1, source_target_pairs={{0,1},{1,0},{2,3},{3,2},{4,5},{5,4},{6,7},{7,6},{8,9},{9,8},{10,11... | collective-permute-start | bytes 884744 | tf_op jit(solution)/shard_map/ppermute | solution.py:54
  40.4 15.6 %collective-permute-start.8 = (bf16[2,2,48,768]{3,2,1,0:T(8,128)(2,1)S(1)}, bf16[2,2,48,768]{3,2,1,0:T(8,128)(2,1)S(1)}, u32[]{:S(2)}, u32[]{:S(2)}) collective-permute-start(bf16[2,2,48,768]{3,2,1,0:T(8,128)(2,1)S(1)} %pad_maximum_fusion.15), channel_id=1, source_target_pairs={{0,1},{1,0},{2,3},{3,2},{4,5},{5,4},{6,7},{7,6},{8,9},{9,8},{10,11... | collective-permute-start | bytes 884744 | tf_op jit(solution)/shard_map/ppermute | solution.py:54
  42.4 8.3 %collective-permute-start.11 = (bf16[3,48,768]{2,1,0:T(8,128)(2,1)S(1)}, bf16[3,48,768]{2,1,0:T(8,128)(2,1)S(1)}, u32[]{:S(2)}, u32[]{:S(2)}) collective-permute-start(bf16[3,48,768]{2,1,0:T(8,128)(2,1)S(1)} %get-tuple-element.504), channel_id=1, source_target_pairs={{0,16},{4,20},{8,24},{12,28},{16,0},{20,4},{24,8},{28,12},{1,17},{... | collective-permute-start | bytes 663560 | tf_op jit(solution)/shard_map/ppermute | solution.py:54
  43.6 15.5 %collective-permute-start.10 = (bf16[2,3,48,768]{3,2,1,0:T(8,128)(2,1)S(1)}, bf16[2,3,48,768]{3,2,1,0:T(8,128)(2,1)S(1)}, u32[]{:S(2)}, u32[]{:S(2)}) collective-permute-start(bf16[2,3,48,768]{3,2,1,0:T(8,128)(2,1)S(1)} %maximum_select_fusion.4), channel_id=1, source_target_pairs={{0,16},{4,20},{8,24},{12,28},{16,0},{20,4},{24,8},{28,12},{1,17},{... | collective-permute-start | bytes 1327112 | tf_op jit(solution)/shard_map/ppermute | solution.py:54
  50.7 10.2 %collective-permute-start.12 = (bf16[2,3,48,768]{3,2,1,0:T(8,128)(2,1)S(1)}, bf16[2,3,48,768]{3,2,1,0:T(8,128)(2,1)S(1)}, u32[]{:S(2)}, u32[]{:S(2)}) collective-permute-start(bf16[2,3,48,768]{3,2,1,0:T(8,128)(2,1)S(1)} %maximum_select_fusion.6), channel_id=1, source_target_pairs={{0,8},{4,12},{8,0},{12,4},{16,24},{20,28},{24,16},{28,20},{1,9},{5... | collective-permute-start | bytes 1327112 | tf_op jit(solution)/shard_map/ppermute | solution.py:54
  61.9 13.6 %collective-permute-start.17 = (bf16[4,2,48,768]{3,2,1,0:T(8,128)(2,1)S(1)}, bf16[4,2,48,768]{3,2,1,0:T(8,128)(2,1)S(1)}, u32[]{:S(2)}, u32[]{:S(2)}) collective-permute-start(bf16[4,2,48,768]{3,2,1,0:T(8,128)(2,1)S(1)} %pad_maximum_fusion.7), channel_id=1, source_target_pairs={{0,8},{4,12},{8,0},{12,4},{16,24},{20,28},{24,16},{28,20},{1,9},{5... | collective-permute-start | bytes 1769480 | tf_op jit(solution)/shard_map/ppermute | solution.py:54
  62.5 13.3 %collective-permute-start.18 = (bf16[4,2,48,768]{3,2,1,0:T(8,128)(2,1)S(1)}, bf16[4,2,48,768]{3,2,1,0:T(8,128)(2,1)S(1)}, u32[]{:S(2)}, u32[]{:S(2)}) collective-permute-start(bf16[4,2,48,768]{3,2,1,0:T(8,128)(2,1)S(1)} %pad_maximum_fusion.8), channel_id=1, source_target_pairs={{0,16},{4,20},{8,24},{12,28},{16,0},{20,4},{24,8},{28,12},{1,17},{... | collective-permute-start | bytes 1769480 | tf_op jit(solution)/shard_map/ppermute | solution.py:54
  63.0 16.4 %collective-permute-start.16 = (bf16[2,2,3,48,768]{4,3,2,1,0:T(8,128)(2,1)}, bf16[2,2,3,48,768]{4,3,2,1,0:T(8,128)(2,1)}, u32[]{:S(2)}, u32[]{:S(2)}) collective-permute-start(bf16[2,2,3,48,768]{4,3,2,1,0:T(8,128)(2,1)} %maximum_select_fusion.3), channel_id=1, source_target_pairs={{0,4},{4,0},{8,12},{12,8},{16,20},{20,16},{24,28},{28,24},{1,5},{5... | collective-permute-start | bytes 2654216 | tf_op jit(solution)/shard_map/ppermute | solution.py:54
  63.0 19.4 %collective-permute-start.15 = (bf16[2,2,3,48,768]{4,3,2,1,0:T(8,128)(2,1)}, bf16[2,2,3,48,768]{4,3,2,1,0:T(8,128)(2,1)}, u32[]{:S(2)}, u32[]{:S(2)}) collective-permute-start(bf16[2,2,3,48,768]{4,3,2,1,0:T(8,128)(2,1)} %maximum_select_fusion.2), channel_id=1, source_target_pairs={{0,4},{4,0},{8,12},{12,8},{16,20},{20,16},{24,28},{28,24},{1,5},{5... | collective-permute-start | bytes 2654216 | tf_op jit(solution)/shard_map/ppermute | solution.py:54
  63.5 47.9 %all-to-all-start = ((bf16[4,128,768]{2,1,0:T(8,128)(2,1)}), bf16[4,128,768]{2,1,0:T(8,128)(2,1)}, u32[]{:S(2)}, u32[]{:S(2)}) async-start(bf16[4,128,768]{2,1,0:T(8,128)(2,1)} %bitcast.25), calls=%async_computation | async-start | bytes 1572864 | tf_op jit(solution)/shard_map/all_to_all | solution.py:1421
  75.9 35.5 %collective-permute-start.19 = (bf16[8,2,48,768]{3,2,1,0:T(8,128)(2,1)S(1)}, bf16[8,2,48,768]{3,2,1,0:T(8,128)(2,1)S(1)}, u32[]{:S(2)}, u32[]{:S(2)}) collective-permute-start(bf16[8,2,48,768]{3,2,1,0:T(8,128)(2,1)S(1)} %pad_maximum_fusion.2.refs_0_.refs_4_), channel_id=1, source_target_pairs={{0,16},{4,20},{8,24},{12,28},{16,0},{20,4},{24,8},{28,12},{1,17},{... | collective-permute-start | bytes 3538952 | tf_op jit(solution)/shard_map/ppermute | solution.py:54
  76.5 34.9 %collective-permute-start.20 = (bf16[8,2,48,768]{3,2,1,0:T(8,128)(2,1)S(1)}, bf16[8,2,48,768]{3,2,1,0:T(8,128)(2,1)}, u32[]{:S(2)}, u32[]{:S(2)}) collective-permute-start(bf16[8,2,48,768]{3,2,1,0:T(8,128)(2,1)S(1)} %pad_maximum_fusion.3.refs_4_.refs_8_), channel_id=1, source_target_pairs={{0,8},{4,12},{8,0},{12,4},{16,24},{20,28},{24,16},{28,20},{1,9},{5... | collective-permute-start | bytes 3538952 | tf_op jit(solution)/shard_map/ppermute | solution.py:54
  79.4 32.6 %collective-permute-start.21 = (bf16[8,2,48,768]{3,2,1,0:T(8,128)(2,1)S(1)}, bf16[8,2,48,768]{3,2,1,0:T(8,128)(2,1)}, u32[]{:S(2)}, u32[]{:S(2)}) collective-permute-start(bf16[8,2,48,768]{3,2,1,0:T(8,128)(2,1)S(1)} %pad_maximum_fusion.2.refs_0_.refs_4_), channel_id=1, source_target_pairs={{0,4},{4,0},{8,12},{12,8},{16,20},{20,16},{24,28},{28,24},{1,5},{5... | collective-permute-start | bytes 3538952 | tf_op jit(solution)/shard_map/ppermute | solution.py:54
  79.4 32.6 %collective-permute-start.23 = (bf16[8,2,48,768]{3,2,1,0:T(8,128)(2,1)S(1)}, bf16[8,2,48,768]{3,2,1,0:T(8,128)(2,1)}, u32[]{:S(2)}, u32[]{:S(2)}) collective-permute-start(bf16[8,2,48,768]{3,2,1,0:T(8,128)(2,1)S(1)} %pad_maximum_fusion.3.refs_4_.refs_8_), channel_id=1, source_target_pairs={{0,4},{4,0},{8,12},{12,8},{16,20},{20,16},{24,28},{28,24},{1,5},{5... | collective-permute-start | bytes 3538952 | tf_op jit(solution)/shard_map/ppermute | solution.py:54
  111.4 3.8 %collective-permute-start.22 = (bf16[8,2,48,768]{3,2,1,0:T(8,128)(2,1)S(1)}, bf16[8,2,48,768]{3,2,1,0:T(8,128)(2,1)S(1)}, u32[]{:S(2)}, u32[]{:S(2)}) collective-permute-start(bf16[8,2,48,768]{3,2,1,0:T(8,128)(2,1)S(1)} %collective-permute-done.19.refs_1_.refs_5_), channel_id=1, source_target_pairs={{0,4},{4,0},{8,12},{12,8},{16,20},{20,16},{24,28},{28,24},{1,5},{5... | collective-permute-start | bytes 3538952 | tf_op jit(solution)/shard_map/ppermute | solution.py:54
  111.5 4.8 %collective-permute-start.24 = (bf16[8,2,48,768]{3,2,1,0:T(8,128)(2,1)}, bf16[8,2,48,768]{3,2,1,0:T(8,128)(2,1)S(1)}, u32[]{:S(2)}, u32[]{:S(2)}) collective-permute-start(bf16[8,2,48,768]{3,2,1,0:T(8,128)(2,1)} %collective-permute-done.20.refs_5_.refs_9_), channel_id=1, source_target_pairs={{0,4},{4,0},{8,12},{12,8},{16,20},{20,16},{24,28},{28,24},{1,5},{5... | collective-permute-start | bytes 3538952 | tf_op jit(solution)/shard_map/ppermute | solution.py:54
  183.7 9.9 %collective-permute-start.25 = (bf16[16,2,48,768]{3,2,1,0:T(8,128)(2,1)}, bf16[16,2,48,768]{3,2,1,0:T(8,128)(2,1)S(1)}, u32[]{:S(2)}, u32[]{:S(2)}) collective-permute-start(bf16[16,2,48,768]{3,2,1,0:T(8,128)(2,1)} %get-tuple-element.303), channel_id=1, source_target_pairs={{0,4},{4,0},{8,12},{12,8},{16,20},{20,16},{24,28},{28,24},{1,5},{5... | collective-permute-start | bytes 7077896 | tf_op jit(solution)/shard_map/ppermute | solution.py:54
  183.9 9.7 %collective-permute-start.26 = (bf16[16,2,48,768]{3,2,1,0:T(8,128)(2,1)}, bf16[16,2,48,768]{3,2,1,0:T(8,128)(2,1)}, u32[]{:S(2)}, u32[]{:S(2)}) collective-permute-start(bf16[16,2,48,768]{3,2,1,0:T(8,128)(2,1)} %get-tuple-element.305), channel_id=1, source_target_pairs={{0,4},{4,0},{8,12},{12,8},{16,20},{20,16},{24,28},{28,24},{1,5},{5... | collective-permute-start | bytes 7077896 | tf_op jit(solution)/shard_map/ppermute | solution.py:54
  199.4 30.5 %collective-permute-start.27 = (bf16[8,2,48,768]{3,2,1,0:T(8,128)(2,1)}, bf16[8,2,48,768]{3,2,1,0:T(8,128)(2,1)S(1)}, u32[]{:S(2)}, u32[]{:S(2)}) collective-permute-start(bf16[8,2,48,768]{3,2,1,0:T(8,128)(2,1)} %get-tuple-element.326), channel_id=1, source_target_pairs={{0,16},{4,20},{8,24},{12,28},{16,0},{20,4},{24,8},{28,12},{1,17},{... | collective-permute-start | bytes 3538952 | tf_op jit(solution)/shard_map/ppermute | solution.py:54
  200.9 29.0 %collective-permute-start.28 = (bf16[8,2,48,768]{3,2,1,0:T(8,128)(2,1)}, bf16[8,2,48,768]{3,2,1,0:T(8,128)(2,1)S(1)}, u32[]{:S(2)}, u32[]{:S(2)}) collective-permute-start(bf16[8,2,48,768]{3,2,1,0:T(8,128)(2,1)} %get-tuple-element.327), channel_id=1, source_target_pairs={{0,8},{4,12},{8,0},{12,4},{16,24},{20,28},{24,16},{28,20},{1,9},{5... | collective-permute-start | bytes 3538952 | tf_op jit(solution)/shard_map/ppermute | solution.py:54
  201.4 28.5 %all-to-all-start.1 = ((bf16[4,128,768]{2,1,0:T(8,128)(2,1)}), bf16[4,128,768]{2,1,0:T(8,128)(2,1)S(1)}, u32[]{:S(2)}, u32[]{:S(2)}) async-start(bf16[4,128,768]{2,1,0:T(8,128)(2,1)} %bitcast.108), calls=%async_computation.1 | async-start | bytes 1572864 | tf_op jit(solution)/shard_map/all_to_all | solution.py:1577
  205.0 9.3 %copy-start.32 = (f32[32,384]{1,0:T(8,128)S(1)}, f32[32,384]{1,0:T(8,128)}, u32[]{:S(2)}) copy-start(f32[32,384]{1,0:T(8,128)} %get-tuple-element.308) | copy-start | bytes 147460
  215.1 14.1 %collective-permute-start.29 = (f32[1,32,768]{2,1,0:T(8,128)S(1)}, f32[1,32,768]{2,1,0:T(8,128)S(1)}, u32[]{:S(2)}, u32[]{:S(2)}) collective-permute-start(f32[1,32,768]{2,1,0:T(8,128)S(1)} %bitcast.111), channel_id=1, source_target_pairs={{0,2},{1,3},{2,0},{3,1},{4,6},{5,7},{6,4},{7,5},{8,10},{9,11},{10,... | collective-permute-start | bytes 294920 | tf_op jit(solution)/shard_map/ppermute | solution.py:54
  230.9 21.2 %collective-permute-start.31 = (bf16[4,192,768]{2,1,0:T(8,128)(2,1)}, bf16[4,192,768]{2,1,0:T(8,128)(2,1)S(1)}, u32[]{:S(2)}, u32[]{:S(2)}) collective-permute-start(bf16[4,192,768]{2,1,0:T(8,128)(2,1)} %get-tuple-element.359), channel_id=1, source_target_pairs={{0,4},{4,0},{8,12},{12,8},{16,20},{20,16},{24,28},{28,24},{1,5},{5... | collective-permute-start | bytes 3538952 | tf_op jit(solution)/shard_map/ppermute | solution.py:54
  235.5 15.3 %collective-permute-start.32 = (bf16[4,2,48,768]{3,2,1,0:T(8,128)(2,1)}, bf16[4,2,48,768]{3,2,1,0:T(8,128)(2,1)S(1)}, u32[]{:S(2)}, u32[]{:S(2)}) collective-permute-start(bf16[4,2,48,768]{3,2,1,0:T(8,128)(2,1)} %get-tuple-element.361), channel_id=1, source_target_pairs={{0,8},{4,12},{8,0},{12,4},{16,24},{20,28},{24,16},{28,20},{1,9},{5... | collective-permute-start | bytes 1769480 | tf_op jit(solution)/shard_map/ppermute | solution.py:54
  237.0 15.0 %collective-permute-start.33 = (bf16[4,2,48,768]{3,2,1,0:T(8,128)(2,1)}, bf16[4,2,48,768]{3,2,1,0:T(8,128)(2,1)S(1)}, u32[]{:S(2)}, u32[]{:S(2)}) collective-permute-start(bf16[4,2,48,768]{3,2,1,0:T(8,128)(2,1)} %get-tuple-element.362), channel_id=1, source_target_pairs={{0,16},{4,20},{8,24},{12,28},{16,0},{20,4},{24,8},{28,12},{1,17},{... | collective-permute-start | bytes 1769480 | tf_op jit(solution)/shard_map/ppermute | solution.py:54
  238.4 10.4 %collective-permute-start.30 = (f32[2,32,768]{2,1,0:T(8,128)}, f32[2,32,768]{2,1,0:T(8,128)S(1)}, u32[]{:S(2)}, u32[]{:S(2)}) collective-permute-start(f32[2,32,768]{2,1,0:T(8,128)} %pad_maximum_fusion.16), channel_id=1, source_target_pairs={{0,1},{1,0},{2,3},{3,2},{4,5},{5,4},{6,7},{7,6},{8,9},{9,8},{10,11... | collective-permute-start | bytes 589832 | tf_op jit(solution)/shard_map/ppermute | solution.py:54
  238.4 10.4 %copy-start.26 = (f32[2,32,768]{2,1,0:T(8,128)S(1)}, f32[2,32,768]{2,1,0:T(8,128)}, u32[]{:S(2)}) copy-start(f32[2,32,768]{2,1,0:T(8,128)} %pad_maximum_fusion.16) | copy-start | bytes 589828
  252.9 3.3 collective-permute-start.34
  259.8 37.0 %all-to-all-start.2 = ((bf16[4,128,768]{2,1,0:T(8,128)(2,1)}), bf16[4,128,768]{2,1,0:T(8,128)(2,1)S(1)}, u32[]{:S(2)}, u32[]{:S(2)}) async-start(bf16[4,128,768]{2,1,0:T(8,128)(2,1)} %bitcast.42), calls=%async_computation.2 | async-start | bytes 1572864 | tf_op jit(solution)/shard_map/all_to_all | solution.py:1647
  263.5 33.3 %collective-permute-start.36 = (bf16[2,224,768]{2,1,0:T(8,128)(2,1)}, bf16[2,224,768]{2,1,0:T(8,128)(2,1)S(1)}, u32[]{:S(2)}, u32[]{:S(2)}) collective-permute-start(bf16[2,224,768]{2,1,0:T(8,128)(2,1)} %get-tuple-element.387), channel_id=1, source_target_pairs={{0,16},{4,20},{8,24},{12,28},{16,0},{20,4},{24,8},{28,12},{1,17},{... | collective-permute-start | bytes 2064392 | tf_op jit(solution)/shard_map/ppermute | solution.py:54
  265.0 31.8 %collective-permute-start.35 = (bf16[2,2,2,48,768]{4,3,2,0,1:T(8,128)(2,1)S(1)}, bf16[2,2,2,48,768]{4,3,2,0,1:T(8,128)(2,1)S(1)}, u32[]{:S(2)}, u32[]{:S(2)}) collective-permute-start(bf16[2,2,2,48,768]{4,3,2,0,1:T(8,128)(2,1)S(1)} %copy.48), channel_id=1, source_target_pairs={{0,1},{1,0},{2,3},{3,2},{4,5},{5,4},{6,7},{7,6},{8,9},{9,8},{10,11... | collective-permute-start | bytes 1769480 | tf_op jit(solution)/shard_map/ppermute | solution.py:54
  266.9 29.8 %collective-permute-start.37 = (bf16[2,192,768]{2,1,0:T(8,128)(2,1)}, bf16[2,192,768]{2,1,0:T(8,128)(2,1)S(1)}, u32[]{:S(2)}, u32[]{:S(2)}) collective-permute-start(bf16[2,192,768]{2,1,0:T(8,128)(2,1)} %get-tuple-element.388), channel_id=1, source_target_pairs={{0,8},{4,12},{8,0},{12,4},{16,24},{20,28},{24,16},{28,20},{1,9},{5... | collective-permute-start | bytes 1769480 | tf_op jit(solution)/shard_map/ppermute | solution.py:54
  296.8 18.4 %collective-permute-start.40 = (bf16[1,4,32,768]{3,2,1,0:T(8,128)(2,1)}, bf16[1,4,32,768]{3,2,1,0:T(8,128)(2,1)S(1)}, u32[]{:S(2)}, u32[]{:S(2)}) collective-permute-start(bf16[1,4,32,768]{3,2,1,0:T(8,128)(2,1)} %bitcast.116), channel_id=1, source_target_pairs={{0,8},{4,12},{8,0},{12,4},{16,24},{20,28},{24,16},{28,20},{1,9},{5... | collective-permute-start | bytes 589832 | tf_op jit(solution)/shard_map/ppermute | solution.py:54
  302.4 15.0 %collective-permute-start.41 = (bf16[1,2,2,48,768]{4,3,2,1,0:T(8,128)(2,1)}, bf16[1,2,2,48,768]{4,3,2,1,0:T(8,128)(2,1)S(1)}, u32[]{:S(2)}, u32[]{:S(2)}) collective-permute-start(bf16[1,2,2,48,768]{4,3,2,1,0:T(8,128)(2,1)} %get-tuple-element.422), channel_id=1, source_target_pairs={{0,2},{1,3},{2,0},{3,1},{4,6},{5,7},{6,4},{7,5},{8,10},{9,11},{10,... | collective-permute-start | bytes 884744 | tf_op jit(solution)/shard_map/ppermute | solution.py:54
  304.8 13.3 %collective-permute-start.38 = (bf16[1,224,768]{2,1,0:T(8,128)(2,1)}, bf16[1,224,768]{2,1,0:T(8,128)(2,1)S(1)}, u32[]{:S(2)}, u32[]{:S(2)}) collective-permute-start(bf16[1,224,768]{2,1,0:T(8,128)(2,1)} %get-tuple-element.419), channel_id=1, source_target_pairs={{0,8},{4,12},{8,0},{12,4},{16,24},{20,28},{24,16},{28,20},{1,9},{5... | collective-permute-start | bytes 1032200 | tf_op jit(solution)/shard_map/ppermute | solution.py:54
  305.4 12.7 %collective-permute-start.39 = (bf16[1,192,768]{2,1,0:T(8,128)(2,1)}, bf16[1,192,768]{2,1,0:T(8,128)(2,1)S(1)}, u32[]{:S(2)}, u32[]{:S(2)}) collective-permute-start(bf16[1,192,768]{2,1,0:T(8,128)(2,1)} %get-tuple-element.420), channel_id=1, source_target_pairs={{0,16},{4,20},{8,24},{12,28},{16,0},{20,4},{24,8},{28,12},{1,17},{... | collective-permute-start | bytes 884744 | tf_op jit(solution)/shard_map/ppermute | solution.py:54
  306.0 9.2 %copy-start.28 = (bf16[4,32,768]{2,1,0:T(8,128)(2,1)S(1)}, bf16[4,32,768]{2,1,0:T(8,128)(2,1)}, u32[]{:S(2)}) copy-start(bf16[4,32,768]{2,1,0:T(8,128)(2,1)} %get-tuple-element.421) | copy-start | bytes 589828
  306.0 12.8 %copy-start.23 = (bf16[2,224,768]{2,1,0:T(8,128)(2,1)S(1)}, bf16[2,224,768]{2,1,0:T(8,128)(2,1)}, u32[]{:S(2)}) copy-start(bf16[2,224,768]{2,1,0:T(8,128)(2,1)} %copy-done.22) | copy-start | bytes 2064388
  318.1 4.5 %collective-permute-start.42 = (bf16[4,128,768]{2,1,0:T(8,128)(2,1)}, bf16[4,128,768]{2,1,0:T(8,128)(2,1)S(1)}, u32[]{:S(2)}, u32[]{:S(2)}) collective-permute-start(bf16[4,128,768]{2,1,0:T(8,128)(2,1)} %get-tuple-element.432), channel_id=1, source_target_pairs={{0,4},{4,0},{8,12},{12,8},{16,20},{20,16},{24,28},{28,24},{1,5},{5... | collective-permute-start | bytes 2359304 | tf_op jit(solution)/shard_map/ppermute | solution.py:54
  318.1 12.0 %collective-permute-start.44 = (bf16[2,4,32,768]{3,2,1,0:T(8,128)(2,1)S(1)}, bf16[2,4,32,768]{3,2,1,0:T(8,128)(2,1)S(1)}, u32[]{:S(2)}, u32[]{:S(2)}) collective-permute-start(bf16[2,4,32,768]{3,2,1,0:T(8,128)(2,1)S(1)} %pad_maximum_fusion.11), channel_id=1, source_target_pairs={{0,16},{4,20},{8,24},{12,28},{16,0},{20,4},{24,8},{28,12},{1,17},{... | collective-permute-start | bytes 1179656 | tf_op jit(solution)/shard_map/ppermute | solution.py:54
  322.6 15.6 %copy-start.20 = (bf16[4,128,768]{2,1,0:T(8,128)(2,1)}, bf16[4,128,768]{2,1,0:T(8,128)(2,1)S(1)}, u32[]{:S(2)}) copy-start(bf16[4,128,768]{2,1,0:T(8,128)(2,1)S(1)} %collective-permute-done.42.refs_18_) | copy-start | bytes 2359300
  323.5 14.6 %collective-permute-start.43 = (bf16[2,128,768]{2,1,0:T(8,128)(2,1)}, bf16[2,128,768]{2,1,0:T(8,128)(2,1)}, u32[]{:S(2)}, u32[]{:S(2)}) collective-permute-start(bf16[2,128,768]{2,1,0:T(8,128)(2,1)} %add_convert_fusion), channel_id=1, source_target_pairs={{0,16},{4,20},{8,24},{12,28},{16,0},{20,4},{24,8},{28,12},{1,17},{... | collective-permute-start | bytes 1179656 | tf_op jit(solution)/shard_map/ppermute | solution.py:54
  325.0 11.8 %collective-permute-start.45 = (bf16[2,224,384]{2,1,0:T(8,128)(2,1)}, bf16[2,224,384]{2,1,0:T(8,128)(2,1)}, u32[]{:S(2)}, u32[]{:S(2)}) collective-permute-start(bf16[2,224,384]{2,1,0:T(8,128)(2,1)} %pad_maximum_fusion.12), channel_id=1, source_target_pairs={{0,1},{1,0},{2,3},{3,2},{4,5},{5,4},{6,7},{7,6},{8,9},{9,8},{10,11... | collective-permute-start | bytes 1032200 | tf_op jit(solution)/shard_map/ppermute | solution.py:54
  325.3 14.7 %copy-start.14 = (bf16[4,224,384]{2,1,0:T(8,128)(2,1)}, bf16[4,224,384]{2,1,0:T(8,128)(2,1)S(1)}, u32[]{:S(2)}) copy-start(bf16[4,224,384]{2,1,0:T(8,128)(2,1)S(1)} %pad_maximum_fusion.5.refs_14_) | copy-start | bytes 2064388
  330.2 8.0 %copy-start.15 = (bf16[4,4,32,768]{3,2,1,0:T(8,128)(2,1)}, bf16[4,4,32,768]{3,2,1,0:T(8,128)(2,1)S(1)}, u32[]{:S(2)}) copy-start(bf16[4,4,32,768]{3,2,1,0:T(8,128)(2,1)S(1)} %pad_maximum_fusion.4.refs_0_) | copy-start | bytes 2359300
  338.2 13.9 %collective-permute-start.47 = (bf16[4,4,32,768]{3,2,1,0:T(8,128)(2,1)S(1)}, bf16[4,4,32,768]{3,2,1,0:T(8,128)(2,1)}, u32[]{:S(2)}, u32[]{:S(2)}) collective-permute-start(bf16[4,4,32,768]{3,2,1,0:T(8,128)(2,1)S(1)} %pad_maximum_fusion.4.refs_0_), channel_id=1, source_target_pairs={{0,4},{4,0},{8,12},{12,8},{16,20},{20,16},{24,28},{28,24},{1,5},{5... | collective-permute-start | bytes 2359304 | tf_op jit(solution)/shard_map/ppermute | solution.py:54
  339.2 12.9 %collective-permute-start.46 = (bf16[1,128,768]{2,1,0:T(8,128)(2,1)S(1)}, bf16[1,128,768]{2,1,0:T(8,128)(2,1)S(1)}, u32[]{:S(2)}, u32[]{:S(2)}) collective-permute-start(bf16[1,128,768]{2,1,0:T(8,128)(2,1)S(1)} %add_convert_fusion.3), channel_id=1, source_target_pairs={{0,8},{4,12},{8,0},{12,4},{16,24},{20,28},{24,16},{28,20},{1,9},{5... | collective-permute-start | bytes 589832 | tf_op jit(solution)/shard_map/ppermute | solution.py:54
  341.0 11.1 %collective-permute-start.48 = (bf16[1,224,384]{2,1,0:T(8,128)(2,1)S(1)}, bf16[1,224,384]{2,1,0:T(8,128)(2,1)S(1)}, u32[]{:S(2)}, u32[]{:S(2)}) collective-permute-start(bf16[1,224,384]{2,1,0:T(8,128)(2,1)S(1)} %add_convert_fusion.4), channel_id=1, source_target_pairs={{0,2},{1,3},{2,0},{3,1},{4,6},{5,7},{6,4},{7,5},{8,10},{9,11},{10,... | collective-permute-start | bytes 516104 | tf_op jit(solution)/shard_map/ppermute | solution.py:54
  341.1 15.6 %copy-start.17 = (bf16[4,128,768]{2,1,0:T(8,128)(2,1)S(1)}, bf16[4,128,768]{2,1,0:T(8,128)(2,1)}, u32[]{:S(2)}) copy-start(bf16[4,128,768]{2,1,0:T(8,128)(2,1)} %copy-done.16) | copy-start | bytes 2359300
  (31 other events, 105.8 us)
where the time goes:
time: 363 us; the launch traced here: 358 us
  Pallas kernels  191 us (53%)
  waiting for transfers between devices  69.8 us (19%)
  starting transfers between devices  55.2 us (15%)
  other arithmetic  20.6 us (6%)
  local copies, waits for them, and re-layouts  19.9 us (5%)
    pallas_call x8, Pallas kernels, whole_call(): pl.pallas_call(body, out_shape=(*shapes, *outside_shapes), in_specs=[in_s...  135 us
    ppermute x49, waiting for transfers between devices, swap(): lax.ppermute(array, axis, [(i, i ^ bit) for i in range(lax.axis_size(axis...  69.8 us
    ppermute x49, starting transfers between devices, swap(): lax.ppermute(array, axis, [(i, i ^ bit) for i in range(lax.axis_size(axis...  43.2 us
    pallas_call x4, Pallas kernels, head_pairs(): pl.pallas_call(body, grid=(steps,), out_shape=shapes, in_specs=[pl.BlockS...  34.6 us
    pallas_call x5, Pallas kernels, parcels(): pl.pallas_call(functools.partial(add_up, [len(terms) for terms in groups]...  16.6 us
    unnamed x92, local copies, waits for them, and re-layouts  11.8 us
  transfers between devices with their start and end apart: 52, of which 21 were waited for; matrix products, arithmetic and copies ran while one was open for 8% of the time, Pallas kernels for 32%

commit v1 on v0

--- a/solution.py
+++ b/solution.py
@@ -591,7 +591,17 @@
     factor_ref[3] = nn(take, own_units(pre_grad_ref)).astype(LOW)
 
 
-def whole_call(body, scalars, operands, outside, shapes, flops, scratch=(), outside_shapes=()):
+def whole_call(
+    body,
+    scalars,
+    operands,
+    outside,
+    shapes,
+    flops,
+    scratch=(),
+    outside_shapes=(),
+    limit=VMEM_LIMIT,
+):
     in_vmem = pl.BlockSpec(memory_space=pltpu.VMEM)
     in_smem = pl.BlockSpec(memory_space=pltpu.SMEM)
     anywhere = pl.BlockSpec(memory_space=pl.ANY)
@@ -602,7 +612,7 @@
         in_specs=[in_smem] * len(scalars) + [in_vmem] * len(operands) + [anywhere] * len(outside),
         out_specs=[in_vmem] * len(shapes) + [anywhere] * len(outside_shapes),
         scratch_shapes=scratch,
-        compiler_params=pltpu.CompilerParams(vmem_limit_bytes=VMEM_LIMIT),
+        compiler_params=pltpu.CompilerParams(vmem_limit_bytes=limit),
         cost_estimate=pl.CostEstimate(flops=flops // 1000, bytes_accessed=size // 1000, transcendentals=0),
     )(*scalars, *operands, *outside)
 
@@ -611,6 +621,34 @@
     head = position(partner(index, stages, "head"), head_order)
     at = head * layout.dps + position(partner(index, stages, "dp"), order)
     return column // layout.rows == at
+
+
+def attention_loads(layout, place_ref, order_a, order_b, pieces, attn_ref, arrived):
+    loads = []
+
+    def copy(source, target):
+        loads.append(pltpu.make_async_copy(source, target, arrived.at[len(loads)]))
+
+    if layout.whole:
+        copy(pieces[0], attn_ref)
+        return loads
+    here = layout.width // layout.heads
+    for m in range(4):
+        copy(pieces[0].at[m], attn_ref.at[m, pl.ds(0, here)])
+    per = layout.dps // 4
+    rows = here // per // 2
+    for side, order in enumerate((order_a, order_b)):
+        for index in range(layout.dps):
+            flip = sum(((index >> k) & 1) * bit for k, bit in enumerate(order))
+            owner = place_ref[0] ^ flip
+            piece = pieces[1 + 4 * side + index // (layout.dps // 4)]
+            for group in range(1, layout.heads):
+                row = group * here + (owner % per) * 2 * rows + side * rows
+                copy(
+                    piece.at[index % (layout.dps // 4), group - 1],
+                    attn_ref.at[owner // per, pl.ds(pl.multiple_of(row, 16), rows)],
+                )
+    return loads
 
 
 def project(
@@ -621,18 +659,29 @@
     head_order,
     place_ref,
     token_ref,
-    attn_ref,
     bias_ref,
     other_ref,
-    key_ref,
-    value_ref,
-    x_ref,
-    q_ref,
-    k_ref,
-    v_ref,
-    vec_ref,
-    bias_in_ref,
+    *refs,
 ):
+    count = 1 if layout.whole else 9
+    pieces, refs = refs[:count], refs[count:]
+    (
+        key_ref,
+        value_ref,
+        x_ref,
+        q_ref,
+        k_ref,
+        v_ref,
+        vec_ref,
+        bias_in_ref,
+        attn_to,
+        attn_ref,
+        arrived,
+        stored,
+    ) = refs
+    loads = attention_loads(layout, place_ref, order_a, order_b, pieces, attn_ref, arrived)
+    for load in loads:
+        load.start()
     devices, entries = bias_ref.shape
     width, rows = layout.width, layout.rows
     here = width // layout.heads
@@ -668,6 +717,10 @@
         for i in range(per):
             bias_in_ref[half * per + i] = row[:, i * layout.size : (i + 1) * layout.size]
 
+    for load in loads:
+        load.wait()
+    store = pltpu.make_async_copy(attn_ref, attn_to, stored)
+    store.start()
     for s in range(token_ref.shape[0]):
         x = token_ref[s]
         key_ref[s] = nt(x, attn_ref[1]).astype(LOW)
@@ -678,15 +731,33 @@
     q_ref[...] = (nt(x, attn_ref[0]) + vector(vec_ref, "b_query")).astype(LOW)
     k_ref[...] = key_ref[own]
     v_ref[...] = value_ref[own]
+    store.wait()
 
 
 SUMS = ("b_out", "gain_attn", "shift_attn", "b_down", "gain_ffn", "shift_ffn")
 
 
-def token_layer(layout, x_ref, attended_ref, cot_ref, bias_ref, vec_ref, attn_ref, *refs):
+def token_layer(
+    layout,
+    memory_rows,
+    head_dim,
+    place_ref,
+    x_ref,
+    q_ref,
+    qkv_ref,
+    part_ref,
+    stat_ref,
+    cot_ref,
+    bias_ref,
+    vec_ref,
+    attn_ref,
+    *refs,
+):
     count = len(layout.pieces())
     pieces, refs = refs[:count], refs[count:]
     (
+        attended_ref,
+        log_ref,
         result_ref,
         skip_ref,
         mixed_ref,
@@ -714,6 +785,22 @@
     for load in loads:
         load.start()
     chunks = layout.chunks
+    pair = part_ref.shape[1]
+    log_ref[...] = jnp.zeros_like(log_ref)
+    for i in range(part_ref.shape[0]):
+        columns = slice(i * pair, (i + 1) * pair)
+        mixed, logs = with_memory(
+            memory_rows,
+            head_dim,
+            q_ref[:, columns],
+            qkv_ref[place_ref[1], 1, :, columns],
+            qkv_ref[place_ref[1], 2, :, columns],
+            part_ref[i],
+            stat_ref[i],
+        )
+        attended_ref[:, columns] = mixed
+        for head, log in enumerate(logs):
+            log_ref[i, head : head + 1] = log
     out_load.wait()
     sum_ref[...] = jnp.zeros_like(sum_ref)
 
@@ -731,15 +818,12 @@
     for load in loads:
         load.wait()
 
-    def forward(i, nothing):
+    for i in range(chunks):
         pre = nt(hidden_ref[...], up_ref[i]) + bias_ref[i]
         pre_ref[i] = pre
         act = gelu(pre).astype(LOW)
         act_ref[i] = act
         total_ref[...] += nn(act, down_ref[i])
-        return nothing
-
-    lax.fori_loop(0, chunks, forward, 0)
     normed, inverse = norm_parts(total_ref[...])
     result = normed * vector(vec_ref, "gain_ffn") + vector(vec_ref, "shift_ffn")
     result_ref[...] = result.astype(LOW)
@@ -1230,25 +1314,21 @@
         sum_ref[0, rows] = tn(v, raised.astype(LOW))[rows]
 
 
-def with_memory(
-    memory_rows, head_dim, place_ref, q_ref, qkv_ref, sum_ref, stat_ref, out_ref, log_ref
-):
-    q, km, vm = q_ref[...], qkv_ref[place_ref[1], 1], qkv_ref[place_ref[1], 2]
-    log_ref[...] = jnp.zeros_like(log_ref)
-    mixed = []
+def with_memory(memory_rows, head_dim, q, km, vm, sums, stats):
+    mixed, logs = [], []
     for head in range(q.shape[1] // head_dim):
         scores = memory_scores(memory_rows, km, columns_of(head, head_dim, q, SCALE))
-        top_before = stat_ref[0, 2 * head : 2 * head + 1]
+        top_before = stats[2 * head : 2 * head + 1]
         top = jnp.maximum(jnp.max(scores, 0, keepdims=True), top_before)
         raised = jnp.exp(scores - top)
         shrink = jnp.exp(top_before - top)
-        total = stat_ref[0, 2 * head + 1 : 2 * head + 2] * shrink
+        total = stats[2 * head + 1 : 2 * head + 2] * shrink
         total = total + 2.0 * jnp.sum(raised, 0, keepdims=True)
         rows = slice(head * head_dim, (head + 1) * head_dim)
-        both = sum_ref[0, rows] * shrink + 2.0 * tn(vm, raised.astype(LOW))[rows]
+        both = sums[rows] * shrink + 2.0 * tn(vm, raised.astype(LOW))[rows]
         mixed.append(both * (1.0 / total))
-        log_ref[0, head : head + 1] = top + jnp.log(total)
-    out_ref[...] = jnp.concatenate(mixed, 0).T.astype(LOW)
+        logs.append(top + jnp.log(total))
+    return jnp.concatenate(mixed, 0).T.astype(LOW), logs
 
 
 def token_attention_back(
@@ -1390,19 +1470,11 @@
     halves = [gather(half, head_stages[-1:]) for half in halves]
     biases = gather(biases, bias_groups[2])
     chunk = jnp.stack([chunk[position(j, head_order)] for j in range(1, groups)])
+    sides = (slice(0, share // 2), slice(share // 2, share))
     parts = []
-
-    def joined(part, have, bit):
-        at = sum(1 for b in have if b > bit)
-        mine = (dp // bit) % 2
-        other = swap(part, "dp", bit)
-        return jnp.where(mine == 1, jnp.stack([other, part], at), jnp.stack([part, other], at))
-
-    for rows, order in ((slice(0, share // 2), order_a), (slice(share // 2, share), order_b)):
-        part = chunk[:, rows]
-        for i, bit in enumerate(order[:-1]):
-            part = joined(part, order[:i], bit)
-        parts.append(part)
+    for rows, order in zip(sides, (order_a, order_b)):
+        part = gather(chunk[None, :, rows], [("dp", bit) for bit in order[:-2]])
+        parts += [part, swap(part, "dp", order[-2])]
     doc = lax.dynamic_index_in_dim(doc_ids, head, 0, False)
     doc_row, doc_column = doc[None, :], doc[:, None]
     init = jnp.pad(mem_init.astype(FULL), ((0, PAD - memory_rows), (0, 0)))
@@ -1413,27 +1485,41 @@
             (halves, parts, biases, cotangent, doc_row, doc_column, init, vectors)
         )
     )
-    parts = [
-        joined(part, order[:-1], order[-1]).reshape(dps, groups - 1, share // 2, width)
-        for part, order in zip(parts, (order_a, order_b))
-    ]
-    others = jnp.concatenate(parts, 2).transpose(1, 0, 2, 3).reshape(groups - 1, 4, here, width)
     cotangent = lax.all_to_all(cotangent, "head", 0, 0, tiled=True).reshape(seg_len, width)
-    w_attn = jnp.concatenate([shard.reshape(4, 1, here, width), others.transpose(1, 0, 2, 3)], 1)
-    w_attn = w_attn.reshape(4, groups * here, width)
+    crossed = [swap(part, "dp", bits[0]) for part in parts]
+    parts = [*parts[:2], *crossed[:2], *parts[2:], *crossed[2:]]
+    if layout.whole:
+        chunks = []
+        for i, order in ((0, order_a), (4, order_b)):
+            part = jnp.concatenate(parts[i : i + 4], 0)
+            native = [position(dp ^ c, order) for c in range(dps)]
+            chunks.append(jnp.stack([lax.dynamic_index_in_dim(part, n, 0, False) for n in native]))
+        others = jnp.concatenate(chunks, 2).transpose(1, 0, 2, 3).reshape(groups - 1, 4, here, width)
+        own = shard.reshape(4, 1, here, width)
+        attn_pieces = [
+            jnp.concatenate([own, others.transpose(1, 0, 2, 3)], 1).reshape(4, width, width)
+        ]
+    else:
+        attn_pieces = [shard.reshape(4, here, width), *parts]
     halves = [
         gather(half, stages[len(head_stages) : -2])
         for half, stages in zip(halves, (stages_a, stages_b))
     ]
-    keys, values, x, q, k, v, vectors, bias_in = whole_call(
+    keys, values, x, q, k, v, vectors, bias_in, w_attn = whole_call(
         functools.partial(project, layout, bias_stages, order_a, order_b, head_order),
         (place,),
-        (tokens, w_attn, biases, vectors),
-        (),
+        (tokens, biases, vectors),
+        attn_pieces,
         (shape(tokens.shape, LOW),) * 2
         + (shape((seg_len, width), LOW),) * 4
         + (shape((len(VECTORS), width), FULL), shape((layout.chunks, 1, layout.size), FULL)),
         6_000_000_000,
+        (
+            pltpu.VMEM((4, width, width), LOW),
+            pltpu.SemaphoreType.DMA((4 + 2 * dps * groups,)),
+            pltpu.SemaphoreType.DMA(()),
+        ),
+        (shape((4, width, width), LOW),),
     )
 
     pair = 2 * head_dim
@@ -1492,27 +1578,29 @@
         tokens_scratch(writes) + landing,
     )
 
-    attended, log_total = head_pairs(
-        functools.partial(with_memory, memory_rows, head_dim),
-        place,
-        (),
-        (q, qkv, *partial),
-        (shape((seg_len, width), LOW), shape((width // pair, 8, seg_len), FULL)),
-        pair,
-        8_000_000_000,
-        width // pair,
-    )
     if layout.whole:
         grad_shapes = (shape((layout.chunks, 2, layout.size, width), LOW),)
     else:
         grad_shapes = (shape((layout.blocks // 2, 2, half_units, width), LOW),) * 4
     sides = 2 * max(layout.size // (layout.size if layout.whole else half_units), 1)
-    result, grad_attn, grad_mixed, grad_attended, bias_sum, layer_sums, *ffn_grads = whole_call(
-        functools.partial(token_layer, layout),
-        (),
-        (x, attended, cotangent, bias_in, vectors),
+    (
+        attended,
+        log_total,
+        result,
+        grad_attn,
+        grad_mixed,
+        grad_attended,
+        bias_sum,
+        layer_sums,
+        *ffn_grads,
+    ) = whole_call(
+        functools.partial(token_layer, layout, memory_rows, head_dim),
+        (place,),
+        (x, q, qkv, *partial, cotangent, bias_in, vectors),
         (w_attn, *pieces),
         (
+            shape((seg_len, width), LOW),
+            shape((width // pair, 8, seg_len), FULL),
             shape((seg_len, width), LOW),
             shape((seg_len, width), FULL),
             shape((seg_len, width), LOW),
@@ -1568,13 +1656,11 @@
         for keep, send, back in zip(ffn_grads[::2], ffn_grads[1::2], (back_a, back_b))
     ]
     back_low = attention_back(0, blocks)
-    back_low, moving, grad_attended, result = lax.optimization_barrier(
-        (back_low, moving, grad_attended, result)
-    )
+    back_low, moving, grad_attended = lax.optimization_barrier((back_low, moving, grad_attended))
+    output = lax.all_to_all(result.reshape(groups, quarter, width), "head", 0, 0, tiled=True)
     sends = parcels(moving)
-    sends, grad_attended, result = lax.optimization_barrier((sends, grad_attended, result))
+    sends, grad_attended = lax.optimization_barrier((sends, grad_attended))
     moving = posted(moving, sends, stages_of(1))
-    output = lax.all_to_all(result.reshape(groups, quarter, width), "head", 0, 0, tiled=True)
     back_high = attention_back(1, blocks)
     token_part = jnp.concatenate([back_low[3], back_high[3]], 1)
     token_part, back_high = lax.optimization_barrier((token_part, back_high))
@@ -1595,8 +1681,8 @@
         (pltpu.VMEM((width, width), LOW), pltpu.SemaphoreType.DMA(())),
     )
     down_a, down_b = ([("dp", bit) for bit in order[::-1]] for order in (order_a, order_b))
-    grad_x, send_b, moving, output, token_parts = lax.optimization_barrier(
-        (grad_x, send_b, moving, output, token_parts)
+    grad_x, send_b, moving, token_parts, output = lax.optimization_barrier(
+        (grad_x, send_b, moving, token_parts, output)
     )
     token_parts = gather(token_parts, head_stages[1:])
     other_b = swap(send_b, *down_b[0])
@@ -1697,7 +1783,7 @@
     attn_moving = posted(attn_moving, sends[1:], (down_a[2], down_b[2]))
     for level in range(3, levels):
         attn_moving = advance_both(attn_moving, level)
-    factors = gather(factors[None], [("dp", order_a[0])])
+    factors = gather(factors[None], [("dp", order_b[0])])
     keep_own, send_own = whole_call(
         functools.partial(
             own_grads, layout, order_a, order_b, head_order, heads, heads_here, memory_rows
@@ -1738,7 +1824,16 @@
     attn_send, own_send, score_w = lax.optimization_barrier((attn_send, own_send, score_w))
     attn_moving = attn_moving + [swap(attn_send, "head", head_order[-1])]
     own = own + [swap(own_send, *down_a[1])]
-    factors = gather(factors, [("dp", order_a[1])])
+    factors = gather(factors, [("dp", order_b[1])])
+    for level in range(2, levels - 1):
+        own = reduce_step(own, down_a[level])
+    attn_send = summed(attn_moving, LOW, attn_moving[-1].shape[0] // 2)
+    own_send = summed(own, LOW, own[-1].shape[0] // 2)
+    attn_send, own_send, score_w = lax.optimization_barrier((attn_send, own_send, score_w))
+    attn_moving = attn_moving + [swap(attn_send, "head", head_order[0])]
+    own = own + [swap(own_send, *down_a[levels - 1])]
+    factors = gather(factors, stages_b[len(head_stages) + 2 : -1])
+    factors = [factors, swap(factors, *stages_b[-1])]
     (grad_tokens,) = whole_call(
         functools.partial(write_rows, heads, quarter),
         (place,),
@@ -1751,12 +1846,6 @@
     grad_tokens, own, factors, attn_moving = lax.optimization_barrier(
         (grad_tokens, own, factors, attn_moving)
     )
-    for bit in head_order[:-1][::-1]:
-        attn_moving = reduce_step(attn_moving, ("head", bit))
-    factors = gather(factors, stages_a[len(head_stages) + 2 : -1])
-    factors = [factors, swap(factors, *stages_a[-1])]
-    for level in range(2, levels):
-        own = reduce_step(own, down_a[level])
     own, factors, attn_moving, moving = lax.optimization_barrier(
         (own, factors, attn_moving, moving)
     )
@@ -1781,8 +1870,8 @@
     outs = pl.pallas_call(
         functools.partial(
             finish,
-            order_in(order_a, order_a),
-            order_in(order_b, order_a),
+            order_in(order_a, order_b),
+            order_in(order_b, order_b),
             memory_rows,
             [len(group) for group in groups_in],
         ),

time: 363 us -> 347 us (0.956)
  waiting for transfers between devices: 69.8 us -> 56.6 us
  starting transfers between devices: 55.2 us -> 67.4 us
  other arithmetic: 20.6 us -> 11.9 us
  Pallas kernels: 191 us -> 186 us
    ppermute x49 -> x51, waiting for transfers between devices: 69.8 us -> 56.6 us  [swap(): lax.ppermute(array, axis, [(i, i ^ bit) for i in range(lax.axis_size(axis...]
    ppermute x49 -> x51, starting transfers between devices: 43.2 us -> 52 us  [swap(): lax.ppermute(array, axis, [(i, i ^ bit) for i in range(lax.axis_size(axis...]
    select_n x8 -> x0, other arithmetic: 6.94 us -> none  [joined(): jnp.where(mine == 1, jnp.stack([other, part], at), jnp.stack([part, other...]
    pallas_call x4 -> x3, Pallas kernels: 34.6 us -> 28.1 us  [head_pairs(): pl.pallas_call(body, grid=(steps,), out_shape=shapes, in_specs=[pl.BlockS...]
    unnamed x92 -> x99, local copies, waits for them, and re-layouts: 11.8 us -> 12.5 us
  transfers between devices with their start and end apart: 52 -> 54, of which waited for: 21 -> 23; matrix products, arithmetic and copies ran while one was open for 8% -> 5% of each run, Pallas kernels for 32% -> 35%
where the time goes in v1:
time: 347 us; the launch traced here: 342 us
  Pallas kernels  186 us (54%)
  starting transfers between devices  67.4 us (19%)
  waiting for transfers between devices  56.6 us (16%)
  local copies, waits for them, and re-layouts  18.5 us (5%)
  other arithmetic  11.9 us (3%)
    pallas_call x8, Pallas kernels, whole_call(): pl.pallas_call(body, out_shape=(*shapes, *outside_shapes), in_specs=[in_s...  138 us
    ppermute x51, waiting for transfers between devices, swap(): lax.ppermute(array, axis, [(i, i ^ bit) for i in range(lax.axis_size(axis...  56.6 us
    ppermute x51, starting transfers between devices, swap(): lax.ppermute(array, axis, [(i, i ^ bit) for i in range(lax.axis_size(axis...  52 us
    pallas_call x3, Pallas kernels, head_pairs(): pl.pallas_call(body, grid=(steps,), out_shape=shapes, in_specs=[pl.BlockS...  28.1 us
    pallas_call x5, Pallas kernels, parcels(): pl.pallas_call(functools.partial(add_up, [len(terms) for terms in groups]...  16.6 us
    unnamed x99, local copies, waits for them, and re-layouts  12.5 us
  transfers between devices with their start and end apart: 54, of which 23 were waited for; matrix products, arithmetic and copies ran while one was open for 5% of the time, Pallas kernels for 35%

profile of v1, /device:TPU:0, one launch (start us, length us, event | category | flops | bytes accessed | tf_op | source)
XLA Modules:
  0.0 342.3 jit_solution(14188331217184928131)
XLA Ops:
  0.7 1.4 pad_maximum_fusion
  3.1 4.1 %collective-permute-start = (bf16[1,96,768]{2,1,0:T(8,128)(2,1)S(1)}, bf16[1,96,768]{2,1,0:T(8,128)(2,1)S(1)}, u32[]{:S(2)}, u32[]{:S(2)}) collective-permute-start(bf16[1,96,768]{2,1,0:T(8,128)(2,1)S(1)} %dynamic-slice_bitcast_fusion), channel_id=1, source_target_pairs={{0,2},{1,3},{2,0},{3,1},{4,6},{5,7},{6,4},{7,5},{8,10},{9,11},{10,... | collective-permute-start | bytes 442376 | tf_op jit(solution)/shard_map/ppermute | solution.py:54
  7.6 6.7 %collective-permute-done.1 = bf16[1,480]{1,0:T(2,128)(2,1)S(1)} collective-permute-done((bf16[1,480]{1,0:T(2,128)(2,1)S(1)}, bf16[1,480]{1,0:T(2,128)(2,1)S(1)}, u32[]{:S(2)}, u32[]{:S(2)}) %collective-permute-start.1) | collective-permute-done | bytes 992 | tf_op jit(solution)/shard_map/ppermute | solution.py:54
  14.4 1.6 collective-permute-start.3
  16.0 2.0 collective-permute-done.3
  18.0 1.6 collective-permute-start.4
  19.7 2.0 collective-permute-start.2
  21.6 2.1 collective-permute-start.6
  23.7 1.9 collective-permute-done.5
  25.6 4.8 %collective-permute-done.6 = bf16[1,2,48,768]{3,2,1,0:T(8,128)(2,1)S(1)} collective-permute-done((bf16[1,2,48,768]{3,2,1,0:T(8,128)(2,1)S(1)}, bf16[1,2,48,768]{3,2,1,0:T(8,128)(2,1)S(1)}, u32[]{:S(2)}, u32[]{:S(2)}) %collective-permute-start.6) | collective-permute-done | bytes 147488 | tf_op jit(solution)/shard_map/ppermute | solution.py:54
  30.4 2.2 collective-permute-done.2
  36.1 1.0 collective-permute-start.8
  37.2 1.2 collective-permute-start.11
  39.6 4.9 %collective-permute-done.11 = bf16[1,3,48,768]{3,2,1,0:T(8,128)(2,1)S(1)} collective-permute-done((bf16[1,3,48,768]{3,2,1,0:T(8,128)(2,1)S(1)}, bf16[1,3,48,768]{3,2,1,0:T(8,128)(2,1)S(1)}, u32[]{:S(2)}, u32[]{:S(2)}) %collective-permute-start.11) | collective-permute-done | bytes 221216 | tf_op jit(solution)/shard_map/ppermute | solution.py:54
  46.3 1.3 dynamic-slice_bitcast_fusion.1
  50.2 2.5 collective-permute-done.10.refs_2_
  52.7 1.3 collective-permute-done.12.refs_6_
  54.9 3.7 %collective-permute-start.20 = (bf16[4,2,48,768]{3,2,1,0:T(8,128)(2,1)S(1)}, bf16[4,2,48,768]{3,2,1,0:T(8,128)(2,1)S(1)}, u32[]{:S(2)}, u32[]{:S(2)}) collective-permute-start(bf16[4,2,48,768]{3,2,1,0:T(8,128)(2,1)S(1)} %pad_maximum_fusion.6), channel_id=1, source_target_pairs={{0,16},{4,20},{8,24},{12,28},{16,0},{20,4},{24,8},{28,12},{1,17},{... | collective-permute-start | bytes 1769480 | tf_op jit(solution)/shard_map/ppermute | solution.py:54
  58.6 4.6 %all-to-all-start = ((bf16[4,128,768]{2,1,0:T(8,128)(2,1)}), bf16[4,128,768]{2,1,0:T(8,128)(2,1)}, u32[]{:S(2)}, u32[]{:S(2)}) async-start(bf16[4,128,768]{2,1,0:T(8,128)(2,1)} %bitcast.16), calls=%async_computation | async-start | bytes 1572864 | tf_op jit(solution)/shard_map/all_to_all | solution.py:1488
  63.2 3.4 %collective-permute-done.19 = bf16[4,2,48,768]{3,2,1,0:T(8,128)(2,1)S(1)} collective-permute-done((bf16[4,2,48,768]{3,2,1,0:T(8,128)(2,1)S(1)}, bf16[4,2,48,768]{3,2,1,0:T(8,128)(2,1)S(1)}, u32[]{:S(2)}, u32[]{:S(2)}) %collective-permute-start.19) | collective-permute-done | bytes 589856 | tf_op jit(solution)/shard_map/ppermute | solution.py:54
  66.8 2.8 collective-permute-done.20
  71.0 1.2 collective-permute-done.15.refs_3_
  75.1 14.2 %shard_map.339 = (bf16[4,512,768]{2,1,0:T(8,128)(2,1)}, bf16[4,512,768]{2,1,0:T(8,128)(2,1)}, bf16[512,768]{1,0:T(8,128)(2,1)}, bf16[512,768]{1,0:T(8,128)(2,1)}...) custom-call(s32[2]{0:T(128)} %pad_add_fusion.place_ref, ...), custom_call_target="tpu_custom_call" | custom-call | flops 6000000 | bytes 17378 | tf_op jit(solution)/shard_map/pallas_call | solution.py:609
  89.4 9.5 %shard_map.340 = (f32[6,128,512]{2,1,0:T(8,128)}, f32[6,8,512]{2,1,0:T(8,128)}) custom-call(s32[2]{0:T(128)} %pad_add_fusion.place_ref, s32[1,512]{1,0:T(1,128)} %get-tuple-element.288.row_ref, s32[512,1]{1,0:T(8,128)} %copy.40.column_ref, bf16[512,768]{1,0:T(8,128)(2,1)} %get-tuple-element.279.q_ref, bf16[512,768]{1,0:T(8,128)(2,1)} %get-tuple-element.290.k_ref, ...), custom_call_target="tpu_custom_call" | custom-call | flops 8000000 | bytes 512 | tf_op jit(solution)/shard_map/pallas_call | solution.py:1392
  100.0 1.9 collective-permute-done.23.refs_2_.refs_6_
  101.9 5.1 %collective-permute-done.25.refs_6_.refs_10_ = bf16[8,2,48,768]{3,2,1,0:T(8,128)(2,1)} collective-permute-done((bf16[8,2,48,768]{3,2,1,0:T(8,128)(2,1)S(1)}, bf16[8,2,48,768]{3,2,1,0:T(8,128)(2,1)}, u32[]{:S(2)}, u32[]{:S(2)}) %collective-permute-start.25) | collective-permute-done | bytes 1179680 | tf_op jit(solution)/shard_map/ppermute | solution.py:54
  108.0 1.0 copy-done.7
  109.0 26.6 %shard_map.341 = (f32[4,16,768]{2,1,0:T(8,128)}, bf16[4,3,16,768]{3,2,1,0:T(8,128)(2,1)}, f32[3,192,512]{2,1,0:T(8,128)}, f32[3,192,16]{2,1,0:T(8,128)}, bf16[3,...) custom-call(s32[1,4]{1,0:T(1,128)} %reset_ref.3, ...), custom_call_target="tpu_custom_call" | custom-call | flops 20000000 | bytes 23273 | tf_op jit(solution)/shard_map/pallas_call | solution.py:609
  135.6 34.2 %shard_map.342 = (bf16[512,768]{1,0:T(8,128)(2,1)}, f32[6,8,512]{2,1,0:T(8,128)}, bf16[512,768]{1,0:T(8,128)(2,1)}, f32[512,768]{1,0:T(8,128)}, bf16[512,768]{1,...) custom-call(s32[2]{0:T(128)} %pad_add_fusion.place_ref, ...), custom_call_target="tpu_custom_call" | custom-call | flops 25000000 | bytes 23371 | tf_op jit(solution)/shard_map/pallas_call | solution.py:609
  170.4 5.8 %all-to-all-start.1 = ((bf16[4,128,768]{2,1,0:T(8,128)(2,1)}), bf16[4,128,768]{2,1,0:T(8,128)(2,1)S(1)}, u32[]{:S(2)}, u32[]{:S(2)}) async-start(bf16[4,128,768]{2,1,0:T(8,128)(2,1)} %bitcast.76), calls=%async_computation.1 | async-start | bytes 1572864 | tf_op jit(solution)/shard_map/all_to_all | solution.py:1660
  176.3 9.3 %shard_map.343 = (bf16[512,384]{1,0:T(8,128)(2,1)}, bf16[512,384]{1,0:T(8,128)(2,1)}, bf16[512,384]{1,0:T(8,128)(2,1)}, f32[32,384]{1,0:T(8,128)}) custom-call(s32[2]{0:T(128)} %pad_add_fusion.place_ref, s32[1,512]{1,0:T(1,128)} %get-tuple-element.288.row_ref, s32[512,1]{1,0:T(8,128)} %copy.40.column_ref, bf16[512,768]{1,0:T(8,128)(2,1)} %get-tuple-element.279.q_ref, ...), custom_call_target="tpu_custom_call" | custom-call | flops 10000000 | bytes 512 | tf_op jit(solution)/shard_map/pallas_call | solution.py:1392
  185.6 1.4 copy-done
  187.0 4.4 %shard_map.344 = (bf16[8,2,48,768]{3,2,1,0:T(8,128)(2,1)}, bf16[8,2,48,768]{3,2,1,0:T(8,128)(2,1)}) custom-call(bf16[16,2,48,768]{3,2,1,0:T(8,128)(2,1)} %get-tuple-element.474.refs_0_.refs_2_, bf16[16,2,48,768]{3,2,1,0:T(8,128)(2,1)} %copy-done, bf16[16,2,48,768]{3,2,1,0:T(8,128)(2,1)} %get-tuple-element.480.refs_2_.refs_3_.refs_4_.refs_5_.refs_8_, ...), custom_call_target="tpu_custom_call" | custom-call | flops 1000 | bytes 1000 | tf_op jit(solution)/shard_map/pallas_call | solution.py:113
  192.0 1.7 collective-permute-start.30
  193.8 9.3 %shard_map.345 = (bf16[512,384]{1,0:T(8,128)(2,1)}, bf16[512,384]{1,0:T(8,128)(2,1)}, bf16[512,384]{1,0:T(8,128)(2,1)}, f32[32,384]{1,0:T(8,128)}) custom-call(s32[2]{0:T(128)} %pad_add_fusion.place_ref, s32[1,512]{1,0:T(1,128)} %get-tuple-element.288.row_ref, s32[512,1]{1,0:T(8,128)} %copy.40.column_ref, bf16[512,768]{1,0:T(8,128)(2,1)} %get-tuple-element.279.q_ref, ...), custom_call_target="tpu_custom_call" | custom-call | flops 10000000 | bytes 512 | tf_op jit(solution)/shard_map/pallas_call | solution.py:1392
  203.9 3.0 collective-permute-start.31
  206.8 7.6 %shard_map.346 = (bf16[4,192,768]{2,1,0:T(8,128)(2,1)}, bf16[4,192,768]{2,1,0:T(8,128)(2,1)}, f32[512,768]{1,0:T(8,128)}, f32[1,768]{1,0:T(1,128)}) custom-call(s32[2]{0:T(128)} %pad_add_fusion.place_ref, bf16[512,768]{1,0:T(8,128)(2,1)} %get-tuple-element.278.x_ref, bf16[512,768]{1,0:T(8,128)(2,1)} %get-tuple-element.304.mixed_ref, ...), custom_call_target="tpu_custom_call" | custom-call | flops 5000000 | bytes 13372 | tf_op jit(solution)/shard_map/pallas_call | solution.py:609
  215.1 4.2 %collective-permute-done.29.refs_2_.refs_4_ = bf16[8,2,48,768]{3,2,1,0:T(8,128)(2,1)S(1)} collective-permute-done((bf16[8,2,48,768]{3,2,1,0:T(8,128)(2,1)}, bf16[8,2,48,768]{3,2,1,0:T(8,128)(2,1)S(1)}, u32[]{:S(2)}, u32[]{:S(2)}) %collective-permute-start.29) | collective-permute-done | bytes 1179680 | tf_op jit(solution)/shard_map/ppermute | solution.py:54
  220.9 4.0 %shard_map.347 = (bf16[4,2,48,768]{3,2,1,0:T(8,128)(2,1)}, bf16[4,2,48,768]{3,2,1,0:T(8,128)(2,1)}) custom-call(bf16[16,2,48,768]{3,2,1,0:T(8,128)(2,1)} %get-tuple-element.474.refs_0_.refs_2_, bf16[16,2,48,768]{3,2,1,0:T(8,128)(2,1)} %copy-done, bf16[8,2,48,768]{3,2,1,0:T(8,128)(2,1)} %copy-done.1, ...), custom_call_target="tpu_custom_call" | custom-call | flops 1000 | bytes 1000 | tf_op jit(solution)/shard_map/pallas_call | solution.py:113
  224.9 1.6 collective-permute-start.34
  226.6 1.2 collective-permute-start.35
  227.8 1.7 collective-permute-start.32
  229.5 10.4 %shard_map.348 = (bf16[4,224,768]{2,1,0:T(8,128)(2,1)}, bf16[4,224,768]{2,1,0:T(8,128)(2,1)}, bf16[512,768]{1,0:T(8,128)(2,1)}) custom-call(s32[2]{0:T(128)} %pad_add_fusion.place_ref, bf16[512,768]{1,0:T(8,128)(2,1)} %get-tuple-element.278.x_ref, bf16[512,384]{1,0:T(8,128)(2,1)} %get-tuple-element.347.dq0_ref, bf16[512,384]{1,0:T(8,128)(2,1)} %get-tuple-element.348.dq1_ref, ...), custom_call_target="tpu_custom_call" | custom-call | flops 10000000 | bytes 12229 | tf_op jit(solution)/shard_map/pallas_call | solution.py:609
  242.0 2.6 shard_map.349
  245.3 1.1 copy-done.8
  246.4 2.5 shard_map.350
  248.9 5.0 %all-to-all-start.2 = ((bf16[4,128,768]{2,1,0:T(8,128)(2,1)}), bf16[4,128,768]{2,1,0:T(8,128)(2,1)S(1)}, u32[]{:S(2)}, u32[]{:S(2)}) async-start(bf16[4,128,768]{2,1,0:T(8,128)(2,1)} %bitcast.24), calls=%async_computation.2 | async-start | bytes 1572864 | tf_op jit(solution)/shard_map/all_to_all | solution.py:1733
  253.9 1.3 collective-permute-start.38
  256.0 2.0 collective-permute-start.37
  258.5 29.3 %shard_map.351 = (bf16[3,192,512]{2,1,0:T(8,128)(2,1)}, bf16[3,16,768]{2,1,0:T(8,128)(2,1)}, bf16[3,16,768]{2,1,0:T(8,128)(2,1)}, bf16[4,3,16,768]{3,2,1,0:T(8,1...) custom-call(s32[1,4]{1,0:T(1,128)} %reset_ref.3, ...), custom_call_target="tpu_custom_call" | custom-call | flops 20000000 | bytes 24859 | tf_op jit(solution)/shard_map/pallas_call | solution.py:609
  289.5 3.2 shard_map.352
  292.7 2.4 collective-permute-start.43
  295.1 1.6 collective-permute-start.40
  296.7 1.3 collective-permute-start.41
  298.0 9.1 %shard_map.353 = (bf16[4,128,768]{2,1,0:T(8,128)(2,1)}, bf16[4,128,768]{2,1,0:T(8,128)(2,1)}) custom-call(s32[2]{0:T(128)} %pad_add_fusion.place_ref, bf16[3,192,512]{2,1,0:T(8,128)(2,1)} %get-tuple-element.445.score_ref, f32[3,192,512]{2,1,0:T(8,128)} %get-tuple-element.341.soft_ref, bf16[4,3,16,768]{3,2,1,0:T(8,128)(2,1)} %get-tuple-element.300.qkv_ref, ...), custom_call_target="tpu_custom_call" | custom-call | flops 5000000 | bytes 7581 | tf_op jit(solution)/shard_map/pallas_call | solution.py:609
  308.1 1.6 collective-permute-start.48
  309.8 1.3 fusion
  311.1 1.2 fusion.1
  313.7 1.3 collective-permute-start.46
  315.1 4.6 %collective-permute-done.48 = bf16[2,4,32,768]{3,2,1,0:T(8,128)(2,1)S(1)} collective-permute-done((bf16[2,4,32,768]{3,2,1,0:T(8,128)(2,1)S(1)}, bf16[2,4,32,768]{3,2,1,0:T(8,128)(2,1)S(1)}, u32[]{:S(2)}, u32[]{:S(2)}) %collective-permute-start.48) | collective-permute-done | bytes 393248 | tf_op jit(solution)/shard_map/ppermute | solution.py:54
  319.9 3.9 %collective-permute-done.45.refs_15_ = bf16[2,224,384]{2,1,0:T(8,128)(2,1)S(1)} collective-permute-done((bf16[2,224,384]{2,1,0:T(8,128)(2,1)S(1)}, bf16[2,224,384]{2,1,0:T(8,128)(2,1)S(1)}, u32[]{:S(2)}, u32[]{:S(2)}) %collective-permute-start.45) | collective-permute-done | bytes 344096 | tf_op jit(solution)/shard_map/ppermute | solution.py:54
  325.7 2.8 collective-permute-start.50
  329.6 6.3 %shard_map.354 = f32[4,128,768]{2,1,0:T(8,128)} custom-call(s32[2]{0:T(128)} %pad_add_fusion.place_ref, bf16[3,192,512]{2,1,0:T(8,128)(2,1)} %get-tuple-element.445.score_ref, f32[3,192,512]{2,1,0:T(8,128)} %get-tuple-element.341.soft_ref, bf16[4,3,16,768]{3,2,1,0:T(8,128)(2,1)} %get-tuple-element.300.qkv_ref, ...), custom_call_target="tpu_custom_call" | custom-call | flops 5000000 | bytes 9216 | tf_op jit(solution)/shard_map/pallas_call | solution.py:609
  337.3 3.8 %shard_map.355 = (f32[96,192]{1,0:T(8,128)}, f32[96,192]{1,0:T(8,128)}, f32[96,192]{1,0:T(8,128)}, f32[3,8]{1,0:T(4,128)}, f32[3,8]{1,0:T(4,128)}, /*index=5*/f3...) custom-call(bf16[4,4,32,768]{3,2,1,0:T(8,128)(2,1)} %copy-done.19, ...), custom_call_target="tpu_custom_call" | custom-call | flops 1000 | bytes 1000 | tf_op jit(solution)/shard_map/pallas_call | solution.py:1870
  (215 shorter events, 35.9 us)
Async XLA Ops:
  3.1 11.2 %collective-permute-start = (bf16[1,96,768]{2,1,0:T(8,128)(2,1)S(1)}, bf16[1,96,768]{2,1,0:T(8,128)(2,1)S(1)}, u32[]{:S(2)}, u32[]{:S(2)}) collective-permute-start(bf16[1,96,768]{2,1,0:T(8,128)(2,1)S(1)} %dynamic-slice_bitcast_fusion), channel_id=1, source_target_pairs={{0,2},{1,3},{2,0},{3,1},{4,6},{5,7},{6,4},{7,5},{8,10},{9,11},{10,... | collective-permute-start | bytes 442376 | tf_op jit(solution)/shard_map/ppermute | solution.py:54
  7.5 6.8 %collective-permute-start.1 = (bf16[1,480]{1,0:T(2,128)(2,1)S(1)}, bf16[1,480]{1,0:T(2,128)(2,1)S(1)}, u32[]{:S(2)}, u32[]{:S(2)}) collective-permute-start(bf16[1,480]{1,0:T(2,128)(2,1)S(1)} %broadcast_in_dim.35), channel_id=1, source_target_pairs={{0,2},{1,3},{2,0},{3,1},{4,6},{5,7},{6,4},{7,5},{8,10},{9,11},{10,... | collective-permute-start | bytes 2888 | tf_op jit(solution)/shard_map/ppermute | solution.py:54
  14.4 3.7 %collective-permute-start.3 = (bf16[2,480]{1,0:T(2,128)(2,1)S(1)}, bf16[2,480]{1,0:T(2,128)(2,1)S(1)}, u32[]{:S(2)}, u32[]{:S(2)}) collective-permute-start(bf16[2,480]{1,0:T(2,128)(2,1)S(1)} %pad_maximum_fusion.22), channel_id=1, source_target_pairs={{0,8},{4,12},{8,0},{12,4},{16,24},{20,28},{24,16},{28,20},{1,9},{5... | collective-permute-start | bytes 5768 | tf_op jit(solution)/shard_map/ppermute | solution.py:54
  16.0 9.6 %collective-permute-start.5 = (bf16[1,2,48,768]{3,2,1,0:T(8,128)(2,1)S(1)}, bf16[1,2,48,768]{3,2,1,0:T(8,128)(2,1)S(1)}, u32[]{:S(2)}, u32[]{:S(2)}) collective-permute-start(bf16[1,2,48,768]{3,2,1,0:T(8,128)(2,1)S(1)} %get-tuple-element.266), channel_id=1, source_target_pairs={{0,2},{1,3},{2,0},{3,1},{4,6},{5,7},{6,4},{7,5},{8,10},{9,11},{10,... | collective-permute-start | bytes 442376 | tf_op jit(solution)/shard_map/ppermute | solution.py:54
  18.0 5.7 %collective-permute-start.4 = (bf16[4,480]{1,0:T(4,128)(2,1)S(1)}, bf16[4,480]{1,0:T(4,128)(2,1)S(1)}, u32[]{:S(2)}, u32[]{:S(2)}) collective-permute-start(bf16[4,480]{1,0:T(4,128)(2,1)S(1)} %pad_maximum_fusion.21), channel_id=1, source_target_pairs={{0,16},{4,20},{8,24},{12,28},{16,0},{20,4},{24,8},{28,12},{1,17},{... | collective-permute-start | bytes 11528 | tf_op jit(solution)/shard_map/ppermute | solution.py:54
  19.7 12.9 %collective-permute-start.2 = (bf16[2,96,768]{2,1,0:T(8,128)(2,1)S(1)}, bf16[2,96,768]{2,1,0:T(8,128)(2,1)S(1)}, u32[]{:S(2)}, u32[]{:S(2)}) collective-permute-start(bf16[2,96,768]{2,1,0:T(8,128)(2,1)S(1)} %pad_maximum_fusion.13), channel_id=1, source_target_pairs={{0,1},{1,0},{2,3},{3,2},{4,5},{5,4},{6,7},{7,6},{8,9},{9,8},{10,11... | collective-permute-start | bytes 884744 | tf_op jit(solution)/shard_map/ppermute | solution.py:54
  21.6 8.8 %collective-permute-start.6 = (bf16[1,2,48,768]{3,2,1,0:T(8,128)(2,1)S(1)}, bf16[1,2,48,768]{3,2,1,0:T(8,128)(2,1)S(1)}, u32[]{:S(2)}, u32[]{:S(2)}) collective-permute-start(bf16[1,2,48,768]{3,2,1,0:T(8,128)(2,1)S(1)} %get-tuple-element.267), channel_id=1, source_target_pairs={{0,2},{1,3},{2,0},{3,1},{4,6},{5,7},{6,4},{7,5},{8,10},{9,11},{10,... | collective-permute-start | bytes 442376 | tf_op jit(solution)/shard_map/ppermute | solution.py:54
  32.8 14.8 %copy-start.37 = (bf16[768]{0:T(1024)(128)(2,1)S(1)}, bf16[768]{0:T(1024)(128)(2,1)}, u32[]{:S(2)}) copy-start(bf16[768]{0:T(1024)(128)(2,1)} %param.30) | copy-start | bytes 4612
  32.8 14.9 %copy-start.38 = (bf16[768]{0:T(1024)(128)(2,1)S(1)}, bf16[768]{0:T(1024)(128)(2,1)}, u32[]{:S(2)}) copy-start(bf16[768]{0:T(1024)(128)(2,1)} %param.31) | copy-start | bytes 4612
  32.8 15.1 %copy-start.39 = (bf16[768]{0:T(1024)(128)(2,1)S(1)}, bf16[768]{0:T(1024)(128)(2,1)}, u32[]{:S(2)}) copy-start(bf16[768]{0:T(1024)(128)(2,1)} %param.32) | copy-start | bytes 4612
  32.9 15.3 %copy-start.40 = (bf16[768]{0:T(1024)(128)(2,1)S(1)}, bf16[768]{0:T(1024)(128)(2,1)}, u32[]{:S(2)}) copy-start(bf16[768]{0:T(1024)(128)(2,1)} %param.36) | copy-start | bytes 4612
  32.9 15.5 %copy-start.41 = (bf16[768]{0:T(1024)(128)(2,1)S(1)}, bf16[768]{0:T(1024)(128)(2,1)}, u32[]{:S(2)}) copy-start(bf16[768]{0:T(1024)(128)(2,1)} %param.37) | copy-start | bytes 4612
  32.9 15.7 %copy-start.42 = (bf16[768]{0:T(1024)(128)(2,1)S(1)}, bf16[768]{0:T(1024)(128)(2,1)}, u32[]{:S(2)}) copy-start(bf16[768]{0:T(1024)(128)(2,1)} %param.38) | copy-start | bytes 4612
  32.9 6.1 %collective-permute-start.9 = (bf16[1,3,48,768]{3,2,1,0:T(8,128)(2,1)S(1)}, bf16[1,3,48,768]{3,2,1,0:T(8,128)(2,1)S(1)}, u32[]{:S(2)}, u32[]{:S(2)}) collective-permute-start(bf16[1,3,48,768]{3,2,1,0:T(8,128)(2,1)S(1)} %get-tuple-element.515), channel_id=1, source_target_pairs={{0,8},{4,12},{8,0},{12,4},{16,24},{20,28},{24,16},{28,20},{1,9},{5... | collective-permute-start | bytes 663560 | tf_op jit(solution)/shard_map/ppermute | solution.py:54
  33.5 4.9 %collective-permute-start.13 = (bf16[8,480]{1,0:T(8,128)(2,1)S(1)}, bf16[8,480]{1,0:T(8,128)(2,1)S(1)}, u32[]{:S(2)}, u32[]{:S(2)}) collective-permute-start(bf16[8,480]{1,0:T(8,128)(2,1)S(1)} %pad_maximum_fusion.20), channel_id=1, source_target_pairs={{0,1},{1,0},{2,3},{3,2},{4,5},{5,4},{6,7},{7,6},{8,9},{9,8},{10,11... | collective-permute-start | bytes 23048 | tf_op jit(solution)/shard_map/ppermute | solution.py:54
  35.1 14.9 %collective-permute-start.7 = (bf16[2,2,48,768]{3,2,1,0:T(8,128)(2,1)S(1)}, bf16[2,2,48,768]{3,2,1,0:T(8,128)(2,1)S(1)}, u32[]{:S(2)}, u32[]{:S(2)}) collective-permute-start(bf16[2,2,48,768]{3,2,1,0:T(8,128)(2,1)S(1)} %pad_maximum_fusion.14), channel_id=1, source_target_pairs={{0,1},{1,0},{2,3},{3,2},{4,5},{5,4},{6,7},{7,6},{8,9},{9,8},{10,11... | collective-permute-start | bytes 884744 | tf_op jit(solution)/shard_map/ppermute | solution.py:54
  36.1 14.0 %collective-permute-start.8 = (bf16[2,2,48,768]{3,2,1,0:T(8,128)(2,1)S(1)}, bf16[2,2,48,768]{3,2,1,0:T(8,128)(2,1)S(1)}, u32[]{:S(2)}, u32[]{:S(2)}) collective-permute-start(bf16[2,2,48,768]{3,2,1,0:T(8,128)(2,1)S(1)} %pad_maximum_fusion.15), channel_id=1, source_target_pairs={{0,1},{1,0},{2,3},{3,2},{4,5},{5,4},{6,7},{7,6},{8,9},{9,8},{10,11... | collective-permute-start | bytes 884744 | tf_op jit(solution)/shard_map/ppermute | solution.py:54
  37.2 7.3 %collective-permute-start.11 = (bf16[1,3,48,768]{3,2,1,0:T(8,128)(2,1)S(1)}, bf16[1,3,48,768]{3,2,1,0:T(8,128)(2,1)S(1)}, u32[]{:S(2)}, u32[]{:S(2)}) collective-permute-start(bf16[1,3,48,768]{3,2,1,0:T(8,128)(2,1)S(1)} %get-tuple-element.514), channel_id=1, source_target_pairs={{0,16},{4,20},{8,24},{12,28},{16,0},{20,4},{24,8},{28,12},{1,17},{... | collective-permute-start | bytes 663560 | tf_op jit(solution)/shard_map/ppermute | solution.py:54
  38.4 11.0 %collective-permute-start.14 = (bf16[16,480]{1,0:T(8,128)(2,1)S(1)}, bf16[16,480]{1,0:T(8,128)(2,1)S(1)}, u32[]{:S(2)}, u32[]{:S(2)}) collective-permute-start(bf16[16,480]{1,0:T(8,128)(2,1)S(1)} %pad_maximum_fusion.19), channel_id=1, source_target_pairs={{0,4},{4,0},{8,12},{12,8},{16,20},{20,16},{24,28},{28,24},{1,5},{5... | collective-permute-start | bytes 46088 | tf_op jit(solution)/shard_map/ppermute | solution.py:54
  39.0 13.6 %collective-permute-start.10 = (bf16[2,3,48,768]{3,2,1,0:T(8,128)(2,1)S(1)}, bf16[2,3,48,768]{3,2,1,0:T(8,128)(2,1)}, u32[]{:S(2)}, u32[]{:S(2)}) collective-permute-start(bf16[2,3,48,768]{3,2,1,0:T(8,128)(2,1)S(1)} %pad_maximum_fusion.8.refs_1_), channel_id=1, source_target_pairs={{0,16},{4,20},{8,24},{12,28},{16,0},{20,4},{24,8},{28,12},{1,17},{... | collective-permute-start | bytes 1327112 | tf_op jit(solution)/shard_map/ppermute | solution.py:54
  45.3 8.6 %collective-permute-start.12 = (bf16[2,3,48,768]{3,2,1,0:T(8,128)(2,1)}, bf16[2,3,48,768]{3,2,1,0:T(8,128)(2,1)}, u32[]{:S(2)}, u32[]{:S(2)}) collective-permute-start(bf16[2,3,48,768]{3,2,1,0:T(8,128)(2,1)} %pad_maximum_fusion.9.refs_5_), channel_id=1, source_target_pairs={{0,8},{4,12},{8,0},{12,4},{16,24},{20,28},{24,16},{28,20},{1,9},{5... | collective-permute-start | bytes 1327112 | tf_op jit(solution)/shard_map/ppermute | solution.py:54
  54.0 12.7 %collective-permute-start.19 = (bf16[4,2,48,768]{3,2,1,0:T(8,128)(2,1)S(1)}, bf16[4,2,48,768]{3,2,1,0:T(8,128)(2,1)S(1)}, u32[]{:S(2)}, u32[]{:S(2)}) collective-permute-start(bf16[4,2,48,768]{3,2,1,0:T(8,128)(2,1)S(1)} %pad_maximum_fusion.5), channel_id=1, source_target_pairs={{0,8},{4,12},{8,0},{12,4},{16,24},{20,28},{24,16},{28,20},{1,9},{5... | collective-permute-start | bytes 1769480 | tf_op jit(solution)/shard_map/ppermute | solution.py:54
  54.9 14.7 %collective-permute-start.20 = (bf16[4,2,48,768]{3,2,1,0:T(8,128)(2,1)S(1)}, bf16[4,2,48,768]{3,2,1,0:T(8,128)(2,1)S(1)}, u32[]{:S(2)}, u32[]{:S(2)}) collective-permute-start(bf16[4,2,48,768]{3,2,1,0:T(8,128)(2,1)S(1)} %pad_maximum_fusion.6), channel_id=1, source_target_pairs={{0,16},{4,20},{8,24},{12,28},{16,0},{20,4},{24,8},{28,12},{1,17},{... | collective-permute-start | bytes 1769480 | tf_op jit(solution)/shard_map/ppermute | solution.py:54
  58.6 40.9 %all-to-all-start = ((bf16[4,128,768]{2,1,0:T(8,128)(2,1)}), bf16[4,128,768]{2,1,0:T(8,128)(2,1)}, u32[]{:S(2)}, u32[]{:S(2)}) async-start(bf16[4,128,768]{2,1,0:T(8,128)(2,1)} %bitcast.16), calls=%async_computation | async-start | bytes 1572864 | tf_op jit(solution)/shard_map/all_to_all | solution.py:1488
  66.8 32.1 %copy-start.3 = (bf16[8,2,48,768]{3,2,1,0:T(8,128)(2,1)}, bf16[8,2,48,768]{3,2,1,0:T(8,128)(2,1)S(1)}, u32[]{:S(2)}) copy-start(bf16[8,2,48,768]{3,2,1,0:T(8,128)(2,1)S(1)} %pad_maximum_fusion.1.refs_0_.refs_4_) | copy-start | bytes 3538948
  69.7 29.4 %copy-start.4 = (bf16[8,2,48,768]{3,2,1,0:T(8,128)(2,1)}, bf16[8,2,48,768]{3,2,1,0:T(8,128)(2,1)S(1)}, u32[]{:S(2)}) copy-start(bf16[8,2,48,768]{3,2,1,0:T(8,128)(2,1)S(1)} %pad_maximum_fusion.2.refs_4_.refs_8_) | copy-start | bytes 3538948
  69.7 29.7 %collective-permute-start.21 = (bf16[8,2,48,768]{3,2,1,0:T(8,128)(2,1)S(1)}, bf16[8,2,48,768]{3,2,1,0:T(8,128)(2,1)S(1)}, u32[]{:S(2)}, u32[]{:S(2)}) collective-permute-start(bf16[8,2,48,768]{3,2,1,0:T(8,128)(2,1)S(1)} %pad_maximum_fusion.1.refs_0_.refs_4_), channel_id=1, source_target_pairs={{0,16},{4,20},{8,24},{12,28},{16,0},{20,4},{24,8},{28,12},{1,17},{... | collective-permute-start | bytes 3538952 | tf_op jit(solution)/shard_map/ppermute | solution.py:54
  70.4 29.0 %collective-permute-start.22 = (bf16[8,2,48,768]{3,2,1,0:T(8,128)(2,1)S(1)}, bf16[8,2,48,768]{3,2,1,0:T(8,128)(2,1)}, u32[]{:S(2)}, u32[]{:S(2)}) collective-permute-start(bf16[8,2,48,768]{3,2,1,0:T(8,128)(2,1)S(1)} %pad_maximum_fusion.2.refs_4_.refs_8_), channel_id=1, source_target_pairs={{0,8},{4,12},{8,0},{12,4},{16,24},{20,28},{24,16},{28,20},{1,9},{5... | collective-permute-start | bytes 3538952 | tf_op jit(solution)/shard_map/ppermute | solution.py:54
  70.5 1.8 collective-permute-start.15
  70.5 4.1 %collective-permute-start.16 = (bf16[2,3,48,768]{3,2,1,0:T(8,128)(2,1)}, bf16[2,3,48,768]{3,2,1,0:T(8,128)(2,1)}, u32[]{:S(2)}, u32[]{:S(2)}) collective-permute-start(bf16[2,3,48,768]{3,2,1,0:T(8,128)(2,1)} %collective-permute-done.10.refs_2_), channel_id=1, source_target_pairs={{0,4},{4,0},{8,12},{12,8},{16,20},{20,16},{24,28},{28,24},{1,5},{5... | collective-permute-start | bytes 1327112 | tf_op jit(solution)/shard_map/ppermute | solution.py:54
  71.0 3.6 %collective-permute-start.17 = (bf16[2,3,48,768]{3,2,1,0:T(8,128)(2,1)}, bf16[2,3,48,768]{3,2,1,0:T(8,128)(2,1)}, u32[]{:S(2)}, u32[]{:S(2)}) collective-permute-start(bf16[2,3,48,768]{3,2,1,0:T(8,128)(2,1)} %pad_maximum_fusion.9.refs_5_), channel_id=1, source_target_pairs={{0,4},{4,0},{8,12},{12,8},{16,20},{20,16},{24,28},{28,24},{1,5},{5... | collective-permute-start | bytes 1327112 | tf_op jit(solution)/shard_map/ppermute | solution.py:54
  73.0 2.1 collective-permute-start.18
  98.9 3.0 collective-permute-start.23
  99.1 7.9 %collective-permute-start.25 = (bf16[8,2,48,768]{3,2,1,0:T(8,128)(2,1)S(1)}, bf16[8,2,48,768]{3,2,1,0:T(8,128)(2,1)}, u32[]{:S(2)}, u32[]{:S(2)}) collective-permute-start(bf16[8,2,48,768]{3,2,1,0:T(8,128)(2,1)S(1)} %pad_maximum_fusion.2.refs_4_.refs_8_), channel_id=1, source_target_pairs={{0,4},{4,0},{8,12},{12,8},{16,20},{20,16},{24,28},{28,24},{1,5},{5... | collective-permute-start | bytes 3538952 | tf_op jit(solution)/shard_map/ppermute | solution.py:54
  99.5 7.5 %collective-permute-start.24 = (bf16[8,2,48,768]{3,2,1,0:T(8,128)(2,1)S(1)}, bf16[8,2,48,768]{3,2,1,0:T(8,128)(2,1)S(1)}, u32[]{:S(2)}, u32[]{:S(2)}) collective-permute-start(bf16[8,2,48,768]{3,2,1,0:T(8,128)(2,1)S(1)} %collective-permute-done.21.refs_1_.refs_5_), channel_id=1, source_target_pairs={{0,4},{4,0},{8,12},{12,8},{16,20},{20,16},{24,28},{28,24},{1,5},{5... | collective-permute-start | bytes 3538952 | tf_op jit(solution)/shard_map/ppermute | solution.py:54
  99.7 8.3 %collective-permute-start.26 = (bf16[8,2,48,768]{3,2,1,0:T(8,128)(2,1)}, bf16[8,2,48,768]{3,2,1,0:T(8,128)(2,1)S(1)}, u32[]{:S(2)}, u32[]{:S(2)}) collective-permute-start(bf16[8,2,48,768]{3,2,1,0:T(8,128)(2,1)} %collective-permute-done.22.refs_5_.refs_9_), channel_id=1, source_target_pairs={{0,4},{4,0},{8,12},{12,8},{16,20},{20,16},{24,28},{28,24},{1,5},{5... | collective-permute-start | bytes 3538952 | tf_op jit(solution)/shard_map/ppermute | solution.py:54
  169.8 15.7 %collective-permute-start.27 = (bf16[16,2,48,768]{3,2,1,0:T(8,128)(2,1)}, bf16[16,2,48,768]{3,2,1,0:T(8,128)(2,1)S(1)}, u32[]{:S(2)}, u32[]{:S(2)}) collective-permute-start(bf16[16,2,48,768]{3,2,1,0:T(8,128)(2,1)} %get-tuple-element.313), channel_id=1, source_target_pairs={{0,4},{4,0},{8,12},{12,8},{16,20},{20,16},{24,28},{28,24},{1,5},{5... | collective-permute-start | bytes 7077896 | tf_op jit(solution)/shard_map/ppermute | solution.py:54
  170.0 15.5 %collective-permute-start.28 = (bf16[16,2,48,768]{3,2,1,0:T(8,128)(2,1)}, bf16[16,2,48,768]{3,2,1,0:T(8,128)(2,1)}, u32[]{:S(2)}, u32[]{:S(2)}) collective-permute-start(bf16[16,2,48,768]{3,2,1,0:T(8,128)(2,1)} %get-tuple-element.315), channel_id=1, source_target_pairs={{0,4},{4,0},{8,12},{12,8},{16,20},{20,16},{24,28},{28,24},{1,5},{5... | collective-permute-start | bytes 7077896 | tf_op jit(solution)/shard_map/ppermute | solution.py:54
  170.4 44.7 %all-to-all-start.1 = ((bf16[4,128,768]{2,1,0:T(8,128)(2,1)}), bf16[4,128,768]{2,1,0:T(8,128)(2,1)S(1)}, u32[]{:S(2)}, u32[]{:S(2)}) async-start(bf16[4,128,768]{2,1,0:T(8,128)(2,1)} %bitcast.76), calls=%async_computation.1 | async-start | bytes 1572864 | tf_op jit(solution)/shard_map/all_to_all | solution.py:1660
  191.4 11.7 %copy-start.35 = (f32[32,384]{1,0:T(8,128)S(1)}, f32[32,384]{1,0:T(8,128)}, u32[]{:S(2)}) copy-start(f32[32,384]{1,0:T(8,128)} %get-tuple-element.317) | copy-start | bytes 147460
  191.4 27.9 %collective-permute-start.29 = (bf16[8,2,48,768]{3,2,1,0:T(8,128)(2,1)}, bf16[8,2,48,768]{3,2,1,0:T(8,128)(2,1)S(1)}, u32[]{:S(2)}, u32[]{:S(2)}) collective-permute-start(bf16[8,2,48,768]{3,2,1,0:T(8,128)(2,1)} %get-tuple-element.334), channel_id=1, source_target_pairs={{0,16},{4,20},{8,24},{12,28},{16,0},{20,4},{24,8},{28,12},{1,17},{... | collective-permute-start | bytes 3538952 | tf_op jit(solution)/shard_map/ppermute | solution.py:54
  192.0 27.7 %collective-permute-start.30 = (bf16[8,2,48,768]{3,2,1,0:T(8,128)(2,1)}, bf16[8,2,48,768]{3,2,1,0:T(8,128)(2,1)S(1)}, u32[]{:S(2)}, u32[]{:S(2)}) collective-permute-start(bf16[8,2,48,768]{3,2,1,0:T(8,128)(2,1)} %get-tuple-element.335), channel_id=1, source_target_pairs={{0,8},{4,12},{8,0},{12,4},{16,24},{20,28},{24,16},{28,20},{1,9},{5... | collective-permute-start | bytes 3538952 | tf_op jit(solution)/shard_map/ppermute | solution.py:54
  203.9 10.5 %collective-permute-start.31 = (f32[1,32,768]{2,1,0:T(8,128)S(1)}, f32[1,32,768]{2,1,0:T(8,128)S(1)}, u32[]{:S(2)}, u32[]{:S(2)}) collective-permute-start(f32[1,32,768]{2,1,0:T(8,128)S(1)} %bitcast.77), channel_id=1, source_target_pairs={{0,2},{1,3},{2,0},{3,1},{4,6},{5,7},{6,4},{7,5},{8,10},{9,11},{10,... | collective-permute-start | bytes 294920 | tf_op jit(solution)/shard_map/ppermute | solution.py:54
  219.7 21.4 %collective-permute-start.33 = (bf16[4,192,768]{2,1,0:T(8,128)(2,1)}, bf16[4,192,768]{2,1,0:T(8,128)(2,1)S(1)}, u32[]{:S(2)}, u32[]{:S(2)}) collective-permute-start(bf16[4,192,768]{2,1,0:T(8,128)(2,1)} %get-tuple-element.367), channel_id=1, source_target_pairs={{0,4},{4,0},{8,12},{12,8},{16,20},{20,16},{24,28},{28,24},{1,5},{5... | collective-permute-start | bytes 3538952 | tf_op jit(solution)/shard_map/ppermute | solution.py:54
  224.9 15.8 %collective-permute-start.34 = (bf16[4,2,48,768]{3,2,1,0:T(8,128)(2,1)}, bf16[4,2,48,768]{3,2,1,0:T(8,128)(2,1)S(1)}, u32[]{:S(2)}, u32[]{:S(2)}) collective-permute-start(bf16[4,2,48,768]{3,2,1,0:T(8,128)(2,1)} %get-tuple-element.369), channel_id=1, source_target_pairs={{0,8},{4,12},{8,0},{12,4},{16,24},{20,28},{24,16},{28,20},{1,9},{5... | collective-permute-start | bytes 1769480 | tf_op jit(solution)/shard_map/ppermute | solution.py:54
  226.6 14.6 %collective-permute-start.35 = (bf16[4,2,48,768]{3,2,1,0:T(8,128)(2,1)}, bf16[4,2,48,768]{3,2,1,0:T(8,128)(2,1)S(1)}, u32[]{:S(2)}, u32[]{:S(2)}) collective-permute-start(bf16[4,2,48,768]{3,2,1,0:T(8,128)(2,1)} %get-tuple-element.370), channel_id=1, source_target_pairs={{0,16},{4,20},{8,24},{12,28},{16,0},{20,4},{24,8},{28,12},{1,17},{... | collective-permute-start | bytes 1769480 | tf_op jit(solution)/shard_map/ppermute | solution.py:54
  227.8 12.1 %collective-permute-start.32 = (f32[2,32,768]{2,1,0:T(8,128)}, f32[2,32,768]{2,1,0:T(8,128)S(1)}, u32[]{:S(2)}, u32[]{:S(2)}) collective-permute-start(f32[2,32,768]{2,1,0:T(8,128)} %pad_maximum_fusion.16), channel_id=1, source_target_pairs={{0,1},{1,0},{2,3},{3,2},{4,5},{5,4},{6,7},{7,6},{8,9},{9,8},{10,11... | collective-permute-start | bytes 589832 | tf_op jit(solution)/shard_map/ppermute | solution.py:54
  242.0 3.3 collective-permute-start.36
  248.9 38.9 %all-to-all-start.2 = ((bf16[4,128,768]{2,1,0:T(8,128)(2,1)}), bf16[4,128,768]{2,1,0:T(8,128)(2,1)S(1)}, u32[]{:S(2)}, u32[]{:S(2)}) async-start(bf16[4,128,768]{2,1,0:T(8,128)(2,1)} %bitcast.24), calls=%async_computation.2 | async-start | bytes 1572864 | tf_op jit(solution)/shard_map/all_to_all | solution.py:1733
  253.9 33.9 %collective-permute-start.38 = (bf16[2,224,768]{2,1,0:T(8,128)(2,1)}, bf16[2,224,768]{2,1,0:T(8,128)(2,1)S(1)}, u32[]{:S(2)}, u32[]{:S(2)}) collective-permute-start(bf16[2,224,768]{2,1,0:T(8,128)(2,1)} %get-tuple-element.395), channel_id=1, source_target_pairs={{0,16},{4,20},{8,24},{12,28},{16,0},{20,4},{24,8},{28,12},{1,17},{... | collective-permute-start | bytes 2064392 | tf_op jit(solution)/shard_map/ppermute | solution.py:54
  256.0 31.8 %collective-permute-start.37 = (bf16[2,2,2,48,768]{4,3,2,0,1:T(8,128)(2,1)}, bf16[2,2,2,48,768]{4,3,2,0,1:T(8,128)(2,1)S(1)}, u32[]{:S(2)}, u32[]{:S(2)}) collective-permute-start(bf16[2,2,2,48,768]{4,3,2,0,1:T(8,128)(2,1)} %copy.43), channel_id=1, source_target_pairs={{0,1},{1,0},{2,3},{3,2},{4,5},{5,4},{6,7},{7,6},{8,9},{9,8},{10,11... | collective-permute-start | bytes 1769480 | tf_op jit(solution)/shard_map/ppermute | solution.py:54
  258.1 29.7 %collective-permute-start.39 = (bf16[2,192,768]{2,1,0:T(8,128)(2,1)}, bf16[2,192,768]{2,1,0:T(8,128)(2,1)S(1)}, u32[]{:S(2)}, u32[]{:S(2)}) collective-permute-start(bf16[2,192,768]{2,1,0:T(8,128)(2,1)} %get-tuple-element.396), channel_id=1, source_target_pairs={{0,8},{4,12},{8,0},{12,4},{16,24},{20,28},{24,16},{28,20},{1,9},{5... | collective-permute-start | bytes 1769480 | tf_op jit(solution)/shard_map/ppermute | solution.py:54
  287.9 19.2 %collective-permute-start.42 = (bf16[1,4,32,768]{3,2,1,0:T(8,128)(2,1)}, bf16[1,4,32,768]{3,2,1,0:T(8,128)(2,1)S(1)}, u32[]{:S(2)}, u32[]{:S(2)}) collective-permute-start(bf16[1,4,32,768]{3,2,1,0:T(8,128)(2,1)} %bitcast.82), channel_id=1, source_target_pairs={{0,16},{4,20},{8,24},{12,28},{16,0},{20,4},{24,8},{28,12},{1,17},{... | collective-permute-start | bytes 589832 | tf_op jit(solution)/shard_map/ppermute | solution.py:54
  292.7 14.7 %collective-permute-start.43 = (bf16[1,2,2,48,768]{4,3,2,1,0:T(8,128)(2,1)}, bf16[1,2,2,48,768]{4,3,2,1,0:T(8,128)(2,1)S(1)}, u32[]{:S(2)}, u32[]{:S(2)}) collective-permute-start(bf16[1,2,2,48,768]{4,3,2,1,0:T(8,128)(2,1)} %get-tuple-element.430), channel_id=1, source_target_pairs={{0,2},{1,3},{2,0},{3,1},{4,6},{5,7},{6,4},{7,5},{8,10},{9,11},{10,... | collective-permute-start | bytes 884744 | tf_op jit(solution)/shard_map/ppermute | solution.py:54
  295.1 13.0 %collective-permute-start.40 = (bf16[1,224,768]{2,1,0:T(8,128)(2,1)}, bf16[1,224,768]{2,1,0:T(8,128)(2,1)S(1)}, u32[]{:S(2)}, u32[]{:S(2)}) collective-permute-start(bf16[1,224,768]{2,1,0:T(8,128)(2,1)} %get-tuple-element.427), channel_id=1, source_target_pairs={{0,8},{4,12},{8,0},{12,4},{16,24},{20,28},{24,16},{28,20},{1,9},{5... | collective-permute-start | bytes 1032200 | tf_op jit(solution)/shard_map/ppermute | solution.py:54
  296.7 11.4 %collective-permute-start.41 = (bf16[1,192,768]{2,1,0:T(8,128)(2,1)}, bf16[1,192,768]{2,1,0:T(8,128)(2,1)S(1)}, u32[]{:S(2)}, u32[]{:S(2)}) collective-permute-start(bf16[1,192,768]{2,1,0:T(8,128)(2,1)} %get-tuple-element.428), channel_id=1, source_target_pairs={{0,16},{4,20},{8,24},{12,28},{16,0},{20,4},{24,8},{28,12},{1,17},{... | collective-permute-start | bytes 884744 | tf_op jit(solution)/shard_map/ppermute | solution.py:54
  308.1 4.7 %collective-permute-start.44 = (bf16[4,128,768]{2,1,0:T(8,128)(2,1)}, bf16[4,128,768]{2,1,0:T(8,128)(2,1)S(1)}, u32[]{:S(2)}, u32[]{:S(2)}) collective-permute-start(bf16[4,128,768]{2,1,0:T(8,128)(2,1)} %get-tuple-element.440), channel_id=1, source_target_pairs={{0,4},{4,0},{8,12},{12,8},{16,20},{20,16},{24,28},{28,24},{1,5},{5... | collective-permute-start | bytes 2359304 | tf_op jit(solution)/shard_map/ppermute | solution.py:54
  308.1 11.5 %collective-permute-start.48 = (bf16[2,4,32,768]{3,2,1,0:T(8,128)(2,1)S(1)}, bf16[2,4,32,768]{3,2,1,0:T(8,128)(2,1)S(1)}, u32[]{:S(2)}, u32[]{:S(2)}) collective-permute-start(bf16[2,4,32,768]{3,2,1,0:T(8,128)(2,1)S(1)} %pad_maximum_fusion.11), channel_id=1, source_target_pairs={{0,8},{4,12},{8,0},{12,4},{16,24},{20,28},{24,16},{28,20},{1,9},{5... | collective-permute-start | bytes 1179656 | tf_op jit(solution)/shard_map/ppermute | solution.py:54
  313.5 11.5 %copy-start.17 = (bf16[4,128,768]{2,1,0:T(8,128)(2,1)}, bf16[4,128,768]{2,1,0:T(8,128)(2,1)S(1)}, u32[]{:S(2)}) copy-start(bf16[4,128,768]{2,1,0:T(8,128)(2,1)S(1)} %collective-permute-done.44.refs_18_) | copy-start | bytes 2359300
  313.6 10.2 %collective-permute-start.45 = (bf16[2,224,384]{2,1,0:T(8,128)(2,1)S(1)}, bf16[2,224,384]{2,1,0:T(8,128)(2,1)S(1)}, u32[]{:S(2)}, u32[]{:S(2)}) collective-permute-start(bf16[2,224,384]{2,1,0:T(8,128)(2,1)S(1)} %pad_maximum_fusion.12), channel_id=1, source_target_pairs={{0,1},{1,0},{2,3},{3,2},{4,5},{5,4},{6,7},{7,6},{8,9},{9,8},{10,11... | collective-permute-start | bytes 1032200 | tf_op jit(solution)/shard_map/ppermute | solution.py:54
  313.7 11.3 %collective-permute-start.46 = (bf16[2,128,768]{2,1,0:T(8,128)(2,1)S(1)}, bf16[2,128,768]{2,1,0:T(8,128)(2,1)S(1)}, u32[]{:S(2)}, u32[]{:S(2)}) collective-permute-start(bf16[2,128,768]{2,1,0:T(8,128)(2,1)S(1)} %add_convert_fusion), channel_id=1, source_target_pairs={{0,16},{4,20},{8,24},{12,28},{16,0},{20,4},{24,8},{28,12},{1,17},{... | collective-permute-start | bytes 1179656 | tf_op jit(solution)/shard_map/ppermute | solution.py:54
  319.7 16.3 %collective-permute-start.49 = (bf16[4,4,32,768]{3,2,1,0:T(8,128)(2,1)S(1)}, bf16[4,4,32,768]{3,2,1,0:T(8,128)(2,1)}, u32[]{:S(2)}, u32[]{:S(2)}) collective-permute-start(bf16[4,4,32,768]{3,2,1,0:T(8,128)(2,1)S(1)} %constant_dynamic-update-slice_fusion.refs_0_), channel_id=1, source_target_pairs={{0,4},{4,0},{8,12},{12,8},{16,20},{20,16},{24,28},{28,24},{1,5},{5... | collective-permute-start | bytes 2359304 | tf_op jit(solution)/shard_map/ppermute | solution.py:54
  325.1 10.9 %collective-permute-start.47 = (bf16[1,128,768]{2,1,0:T(8,128)(2,1)S(1)}, bf16[1,128,768]{2,1,0:T(8,128)(2,1)S(1)}, u32[]{:S(2)}, u32[]{:S(2)}) collective-permute-start(bf16[1,128,768]{2,1,0:T(8,128)(2,1)S(1)} %add_convert_fusion.3), channel_id=1, source_target_pairs={{0,8},{4,12},{8,0},{12,4},{16,24},{20,28},{24,16},{28,20},{1,9},{5... | collective-permute-start | bytes 589832 | tf_op jit(solution)/shard_map/ppermute | solution.py:54
  325.7 10.3 %collective-permute-start.50 = (bf16[1,224,384]{2,1,0:T(8,128)(2,1)}, bf16[1,224,384]{2,1,0:T(8,128)(2,1)S(1)}, u32[]{:S(2)}, u32[]{:S(2)}) collective-permute-start(bf16[1,224,384]{2,1,0:T(8,128)(2,1)} %add_convert_fusion.4), channel_id=1, source_target_pairs={{0,2},{1,3},{2,0},{3,1},{4,6},{5,7},{6,4},{7,5},{8,10},{9,11},{10,... | collective-permute-start | bytes 516104 | tf_op jit(solution)/shard_map/ppermute | solution.py:54
  (36 other events, 147.0 us)
